TPU v7x, 512 devices: a whole 4x4x16 slice. The times are simulated.
512 devices in a mesh: space: 32 (over y, x, core), dp: 16 (over z).
Axes of the slice: x: 4, y: 4, z: 16, core: 2. Of those that a mesh axis runs over, the one named last changes fastest.
Arguments:
- features: bfloat16 [2, 128, 32, 128, 128], P(None, 'space', None, 'dp'), may hold values from -6 to 6
- cotangent: bfloat16 [2, 128, 32, 128, 128], P(None, 'space', None, 'dp'), may hold values from -6 to 6
- spectral_weight: bfloat16 [256, 2, 16, 1024], P('space', None, 'dp'), may hold values from -0.75 to 0.75
- mix_weight: bfloat16 [32, 32], replicated, may hold values from -1 to 1
- bias_term: float32 [32], replicated, may hold values from -3 to 3
Outputs:
- activated: bfloat16 [2, 128, 32, 128, 128], P(None, 'space', None, 'dp')
- grad_input: bfloat16 [2, 128, 32, 128, 128], P(None, 'space', None, 'dp')
- grad_spectral: float32 [256, 2, 16, 1024], P('space', None, 'dp')
- grad_mix: float32 [32, 32], replicated
- grad_bias: float32 [32], replicated
All inputs are finite; a program needn't handle non-finite values.
Results may differ from a plain program's by a relative error of at most 0.008.
Values sent between devices are 32-bit elements; how exact they have to be, the bound alone decides.
No kernel may reach another device: no remote copies, remote signals or barrier semaphores. Data moves between devices by JAX's collectives and lax.ppermute only.
A program may use at most 64 MiB of HBM per device.

v0:
```python
import math

import jax
import jax.numpy as jnp
from jax import lax
from jax.sharding import PartitionSpec as P

KX = 16
KY = 16
KZ = 16


HIGHEST = lax.Precision.HIGHEST
ROOT_HALF = 0.7071067811865476
INV_ROOT_TAU = 0.3989422804014327


def signed_modes(indices, extent):
    return jnp.where(indices < extent // 2, indices, indices - extent)


def phase_table(modes, places, length):
    phases = modes[:, None] * places[None, :] % length
    angles = phases.astype(jnp.float32) * (2.0 * math.pi / length)
    return (jnp.cos(angles), jnp.sin(angles))


def blend(pattern, operand_a, operand_b):
    return jnp.einsum(pattern, operand_a, operand_b, precision=HIGHEST)


def plane_tables(mode_count, places_x, total_x, places_y, total_y):
    mode_ids = jnp.arange(mode_count, dtype=jnp.int32)
    modes_x = signed_modes(mode_ids // KY, KX)
    modes_y = signed_modes(mode_ids % KY, KY)
    phase_x = modes_x[:, None] * places_x[None, :] % total_x
    phase_y = modes_y[:, None] * places_y[None, :] % total_y
    rotations = (
        phase_x[:, :, None].astype(jnp.float32) / total_x
        + phase_y[:, None, :].astype(jnp.float32) / total_y
    )
    angles = rotations * (2.0 * math.pi)
    return (jnp.cos(angles), jnp.sin(angles))


def on_device(features, cotangent, spectral_weight, mix_weight, bias_term):
    samples, planes, channels, rows_y, rows_z = features.shape
    spaces = lax.axis_size("space")
    groups = lax.axis_size("dp")
    total_x = planes * spaces
    total_y = rows_y * groups
    pairs = KX * KY
    owned = pairs // spaces
    depth = KZ // groups
    width = samples * channels
    places_x = lax.axis_index("space") * planes + jnp.arange(planes, dtype=jnp.int32)
    places_y = lax.axis_index("dp") * rows_y + jnp.arange(rows_y, dtype=jnp.int32)
    cell_count = total_x * total_y * rows_z
    scale_cells = 1.0 / math.sqrt(cell_count)
    scale_modes = 1.0 / math.sqrt(KX * KY * KZ)
    scale_all = 1.0 / math.sqrt(cell_count * samples)
    cosine_z, sine_z = phase_table(
        jnp.arange(KZ, dtype=jnp.int32), jnp.arange(rows_z, dtype=jnp.int32), rows_z
    )
    table_wide = jnp.concatenate([cosine_z, -sine_z], 0)
    table_narrow = table_wide.astype(jnp.bfloat16)

    def analyse(field):
        depth_part = jnp.einsum(
            "tz,spcyz->pytsc", table_narrow, field, preferred_element_type=jnp.float32
        )
        depth_part = depth_part.reshape(planes, rows_y, 2, KZ, width)
        depth_real = depth_part[:, :, 0]
        depth_imag = depth_part[:, :, 1]
        cosines, sines = plane_tables(
            lax.axis_size("space") * owned, places_x, total_x, places_y, total_y
        )
        part_real = blend("jpy,pykm->jkm", cosines, depth_real) + blend(
            "jpy,pykm->jkm", sines, depth_imag
        )
        part_imag = blend("jpy,pykm->jkm", cosines, depth_imag) - blend(
            "jpy,pykm->jkm", sines, depth_real
        )
        summed = lax.psum_scatter(
            (jnp.stack([part_real, part_imag], 1) * scale_cells).reshape(
                lax.axis_size("space") * owned, 2 * KZ * width
            ),
            "space",
            scatter_dimension=0,
            tiled=True,
        ).reshape(owned, 2, KZ, width)
        return lax.psum_scatter(summed, "dp", scatter_dimension=2, tiled=True)

    def synthesize(mixed):
        full_depth = lax.all_gather(mixed, "dp", axis=2, tiled=True)
        piece = lax.all_gather(full_depth, "space", axis=0, tiled=True)
        cosines, sines = plane_tables(piece.shape[0], places_x, total_x, places_y, total_y)
        row_real = blend("jpy,jkm->pykm", cosines, piece[:, 0]) - blend(
            "jpy,jkm->pykm", sines, piece[:, 1]
        )
        row_imag = blend("jpy,jkm->pykm", cosines, piece[:, 1]) + blend(
            "jpy,jkm->pykm", sines, piece[:, 0]
        )
        rows = jnp.stack([row_real, row_imag], 2)
        merged = rows.reshape(planes, rows_y, 2 * KZ, samples, channels)
        return jnp.einsum("pytsc,tz->spcyz", merged, table_wide, precision=HIGHEST)

    weights = spectral_weight.astype(jnp.float32).reshape(owned, 2, depth, channels, channels)
    weight_real = weights[:, 0]
    weight_imag = weights[:, 1]
    coeffs = analyse(features).reshape(owned, 2, depth, samples, channels)
    coeff_real = coeffs[:, 0]
    coeff_imag = coeffs[:, 1]
    mixed_real = blend("jksc,jkco->jkso", coeff_real, weight_real) - blend(
        "jksc,jkco->jkso", coeff_imag, weight_imag
    )
    mixed_imag = blend("jksc,jkco->jkso", coeff_real, weight_imag) + blend(
        "jksc,jkco->jkso", coeff_imag, weight_real
    )
    mixed = jnp.stack([mixed_real, mixed_imag], 1).reshape(owned, 2, depth, width)
    spectral_part = synthesize(mixed)
    preact = spectral_part * scale_modes + jnp.einsum(
        "spcyz,co->spoyz", features, mix_weight, preferred_element_type=jnp.float32
    )
    preact = preact + bias_term[None, None, :, None, None]
    normal_cdf = 0.5 * (1.0 + lax.erf(preact * ROOT_HALF))
    activated = (preact * normal_cdf).astype(jnp.bfloat16)
    gelu_slope = normal_cdf + preact * jnp.exp(-0.5 * preact * preact) * INV_ROOT_TAU
    grad_pre = (cotangent.astype(jnp.float32) * gelu_slope).astype(jnp.bfloat16)
    cot_coeffs = analyse(grad_pre).reshape(owned, 2, depth, samples, channels)
    cot_real = cot_coeffs[:, 0]
    cot_imag = cot_coeffs[:, 1]
    back_real = blend("jkso,jkco->jksc", cot_real, weight_real) + blend(
        "jkso,jkco->jksc", cot_imag, weight_imag
    )
    back_imag = blend("jkso,jkco->jksc", cot_imag, weight_real) - blend(
        "jkso,jkco->jksc", cot_real, weight_imag
    )
    outer_real = blend("jksc,jkso->jkco", coeff_real, cot_real) + blend(
        "jksc,jkso->jkco", coeff_imag, cot_imag
    )
    outer_imag = blend("jksc,jkso->jkco", coeff_real, cot_imag) - blend(
        "jksc,jkso->jkco", coeff_imag, cot_real
    )
    grad_spectral = jnp.stack([outer_real, outer_imag], 1).reshape(
        owned, 2, depth, channels * channels
    )
    grad_spectral = grad_spectral / math.sqrt(samples)
    back = jnp.stack([back_real, back_imag], 1).reshape(owned, 2, depth, width)
    spectral_back = synthesize(back)
    grad_input = jnp.einsum(
        "spoyz,co->spcyz", grad_pre, mix_weight, preferred_element_type=jnp.float32
    )
    grad_input = (grad_input + spectral_back * scale_modes).astype(jnp.bfloat16)
    moments = jnp.einsum("spcyz,spoyz->co", features, grad_pre, preferred_element_type=jnp.float32)
    totals = jnp.sum(grad_pre.astype(jnp.float32), axis=(0, 1, 3, 4))
    grad_mix, grad_bias = lax.psum((moments, totals), ("space", "dp"))
    return (activated, grad_input, grad_spectral, grad_mix * scale_all, grad_bias * scale_all)


def solution(mesh):
    placed = (
        P(None, "space", None, "dp", None),
        P(None, "space", None, "dp", None),
        P("space", None, "dp", None),
        P(),
        P(),
    )
    return jax.shard_map(
        on_device,
        mesh=mesh,
        in_specs=placed,
        out_specs=(
            P(None, "space", None, "dp", None),
            P(None, "space", None, "dp", None),
            P("space", None, "dp", None),
            P(),
            P(),
        ),
        check_vma=False,
    )
```

profile of v0, /device:TPU:1, one launch (start us, length us, event | category | flops | bytes accessed | tf_op | source)
XLA Modules:
  0.0 657.0 jit_solution(15472303105896129946)
XLA Ops:
  7.3 0.9 copy-done
  8.2 0.9 convolution_bitcast_fusion.3
  9.1 0.8 copy.149
  9.9 0.6 reshape.332
  10.7 1.1 convolution_bitcast_fusion.10
  11.8 1.1 convolution_bitcast_fusion.8
  12.9 1.1 fusion.6
  14.1 1.1 fusion.8
  15.4 1.8 copy.145
  17.3 105.7 %reduce-scatter.13.cloned.1.call-done = f32[8,2048]{1,0:T(8,128)} async-done(((f32[256,2048]{1,0:T(8,128)}), f32[8,2048]{1,0:T(8,128)}) %reduce-scatter.13.cloned.1.call-update) | async-done | bytes 65552
  123.0 1.2 copy.146
  124.2 1.0 copy.99
  125.4 59.2 %reduce-scatter.9.cloned.1.call-done = f32[8,2,1,64]{3,0,1,2:T(8,128)} async-done(((f32[8,2,16,64]{3,0,1,2:T(8,128)}), f32[8,2,1,64]{3,0,1,2:T(8,128)}) %reduce-scatter.9.cloned.1.call-update) | async-done | bytes 4112 | tf_op jit(solution)/shard_map/reduce_scatter | solution.py:92
  184.7 0.8 reshape.296
  186.3 20.9 %all_gather.12 = f32[8,2,16,64]{3,0,1,2:T(8,128)S(1)} all-gather(f32[8,2,1,64]{3,0,1,2:T(8,128)S(1)} %maximum_bitcast_fusion), channel_id=1, replica_groups=mesh['space'=32,'dp'=16] {'dp'}, dimensions={2}, use_global_device_ids=true | all-gather | bytes 69632 | tf_op jit(solution)/shard_map/all_gather | solution.py:95
  207.2 0.7 copy.102
  208.0 0.5 reduce-scatter.15.cloned.1.call-start
  208.5 1.4 convolution_bitcast_fusion.2
  209.9 77.6 %all-gather.3.cloned.1.call-done = f32[256,2,16,64]{3,2,1,0:T(8,128)} async-done(((f32[8,2,16,64]{3,2,1,0:T(8,128)}), f32[256,2,16,64]{3,2,1,0:T(8,128)}) %all-gather.3.cloned.1.call-update) | async-done | bytes 2097168 | tf_op jit(solution)/shard_map/all_gather | solution.py:96
  287.4 4.5 fusion.176
  291.9 2.5 copy.153
  294.4 1.6 fusion.34
  296.1 2.5 copy.154
  298.6 1.6 fusion.30
  300.2 1.6 fusion.17
  301.8 1.6 fusion.16
  303.7 1.6 reshape.302
  305.3 4.5 convert_reduce_fusion
  309.8 0.8 copy-done.2
  310.9 1.7 copy.151
  312.7 0.6 reshape.333
  313.3 1.1 convolution_bitcast_fusion.6
  314.4 1.1 convolution_bitcast_fusion.4
  315.5 1.1 fusion.10
  316.7 1.1 fusion.12
  318.0 1.8 copy.147
  319.9 99.4 %reduce-scatter.15.cloned.1.call-done = f32[8,2048]{1,0:T(8,128)} async-done(((f32[256,2048]{1,0:T(8,128)}), f32[8,2048]{1,0:T(8,128)}) %reduce-scatter.15.cloned.1.call-update) | async-done | bytes 65552
  419.3 1.2 copy.148
  420.5 1.0 copy.114
  421.6 58.8 %reduce-scatter.11.cloned.1.call-done = f32[8,2,1,64]{3,0,1,2:T(8,128)} async-done(((f32[8,2,16,64]{3,0,1,2:T(8,128)}), f32[8,2,1,64]{3,0,1,2:T(8,128)}) %reduce-scatter.11.cloned.1.call-update) | async-done | bytes 4112 | tf_op jit(solution)/shard_map/reduce_scatter | solution.py:92
  480.4 0.8 reshape.305
  482.2 20.8 %all_gather.14 = f32[8,2,16,64]{3,0,1,2:T(8,128)S(1)} all-gather(f32[8,2,1,64]{3,0,1,2:T(8,128)S(1)} %maximum_bitcast_fusion.1), channel_id=1, replica_groups=mesh['space'=32,'dp'=16] {'dp'}, dimensions={2}, use_global_device_ids=true | all-gather | bytes 69632 | tf_op jit(solution)/shard_map/all_gather | solution.py:95
  503.0 0.7 copy.116
  504.0 119.4 %all-reduce = (f32[32,32]{0,1:T(8,128)S(1)}, f32[32]{0:T(128)S(1)}) all-reduce(f32[32,32]{0,1:T(8,128)S(1)} %convolution_bitcast_fusion.12, f32[32]{0:T(128)S(1)} %get-tuple-element.27), channel_id=1, replica_groups=mesh['space'=32,'dp'=16] {'space','dp'}, use_global_device_ids=true, to_apply=%region_4.5 | all-reduce | flops 1056 | bytes 8448 | tf_op jit(solution)/shard_map/psum | solution.py:157
  623.4 0.7 copy.127
  624.1 1.1 copy.125
  625.2 0.5 broadcast_multiply_fusion.1
  625.8 1.3 convolution_bitcast_fusion
  627.1 0.4 fusion.149
  627.5 0.4 convolution_add_fusion.2
  628.0 0.4 fusion.148
  628.5 0.4 convolution_subtract_fusion.2
  629.0 0.7 maximum_multiply_fusion.2
  629.7 4.5 fusion.175
  634.2 2.5 copy.155
  636.7 1.6 fusion.28
  638.4 2.5 copy.156
  640.9 1.6 fusion.24
  642.5 1.6 fusion.15
  644.1 1.6 fusion.14
  645.9 0.6 reshape.308
  646.5 0.5 copy-done.1
  647.0 1.8 fusion.13
  648.8 1.1 copy.126
  (63 shorter events, 4.2 us)
Async XLA Ops:
  7.2 1.0 copy-start
  7.2 115.8 %reduce-scatter.13.cloned.1.call-start = ((), (), s32[]{:S(2)}) async-start(), calls=%async_computation.8 | async-start | bytes 2162688
  17.2 108.0 %copy-start.7 = (bf16[8,2,1,1024]{3,1,2,0:T(2,128)(2,1)S(1)}, bf16[8,2,1,1024]{3,1,2,0:T(2,128)(2,1)}, u32[]{:S(2)}) copy-start(bf16[8,2,1,1024]{3,1,2,0:T(2,128)(2,1)} %param.7) | copy-start | bytes 98308
  17.3 191.2 %copy-start.6 = (bf16[32,32]{1,0:T(8,128)(2,1)S(1)}, bf16[32,32]{1,0:T(8,128)(2,1)}, u32[]{:S(2)}) copy-start(bf16[32,32]{1,0:T(8,128)(2,1)} %param.8) | copy-start | bytes 6148
  17.3 167.4 %reduce-scatter.9.cloned.1.call-start = ((), (), s32[]{:S(2)}) async-start(), calls=%async_computation.4 | async-start | bytes 139264 | tf_op jit(solution)/shard_map/reduce_scatter | solution.py:92
  125.2 162.2 %all-gather.3.cloned.1.call-start = ((), (), s32[]{:S(2)}) async-start(), calls=%async_computation.5 | async-start | bytes 4325376 | tf_op jit(solution)/shard_map/all_gather | solution.py:96
  208.0 211.4 %reduce-scatter.15.cloned.1.call-start = ((), (), s32[]{:S(2)}) async-start(), calls=%async_computation.9 | async-start | bytes 2162688
  303.5 1.8 copy-start.4
  303.5 1.8 copy-start.9
  303.6 1.7 copy-start.8
  309.7 0.8 copy-start.2
  319.8 183.9 %copy-start.3 = (bf16[2,4,32,8,128]{4,2,0,3,1:T(8,128)(2,1)S(1)}, bf16[2,4,32,8,128]{4,2,0,3,1:T(8,128)(2,1)}, u32[]{:S(2)}) copy-start(bf16[2,4,32,8,128]{4,2,0,3,1:T(8,128)(2,1)} %copy-done.2) | copy-start | bytes 1572868
  319.9 160.6 %reduce-scatter.11.cloned.1.call-start = ((), (), s32[]{:S(2)}) async-start(), calls=%async_computation.6 | async-start | bytes 139264 | tf_op jit(solution)/shard_map/reduce_scatter | solution.py:92
  420.5 203.6 %copy-start.5 = (bf16[2,4,32,8,128]{4,2,0,3,1:T(8,128)(2,1)S(1)}, bf16[2,4,32,8,128]{4,2,0,3,1:T(8,128)(2,1)}, u32[]{:S(2)}) copy-start(bf16[2,4,32,8,128]{4,2,0,3,1:T(8,128)(2,1)} %get-tuple-element.33) | copy-start | bytes 1572868
  421.5 208.2 %all-gather.5.cloned.1.call-start = ((), (), s32[]{:S(2)}) async-start(), calls=%async_computation.7 | async-start | bytes 4325376 | tf_op jit(solution)/shard_map/all_gather | solution.py:96
  645.8 1.2 copy-start.1
Sparse Core Ops, SparseCore 0:
  17.4 105.5 reduce-scatter.12
  126.4 58.2 reduce-scatter.8
  208.1 79.2 all-gather.2
  320.0 99.3 reduce-scatter.14
  422.2 58.1 reduce-scatter.10
  503.8 79.3 all-gather.4
where the time goes:
time: 664 us; the launch traced here: 657 us
  waiting for transfers between devices  401 us (60%)
  blocking collectives  161 us (24%)
  local copies, waits for them, and re-layouts  41.9 us (6%)
  matrix products  35.7 us (5%)
  between operations  14.8 us (2%)
    unnamed x8, waiting for transfers between devices  205 us
    psum x1, blocking collectives, on_device(): grad_mix, grad_bias = lax.psum((moments, totals), ('space', 'dp'))  119 us
    reduce_scatter x2, waiting for transfers between devices, analyse(): return lax.psum_scatter(summed, 'dp', scatter_dimension=2, tiled=True)  118 us
    all_gather x2, waiting for transfers between devices, synthesize(): piece = lax.all_gather(full_depth, 'space', axis=0, tiled=True)  77.6 us
    all_gather x2, blocking collectives, synthesize(): full_depth = lax.all_gather(mixed, 'dp', axis=2, tiled=True)  41.7 us
    dot_general x28, matrix products, blend(): return jnp.einsum(pattern, operand_a, operand_b, precision=HIGHEST)  25.1 us
    unnamed x32, local copies, waits for them, and re-layouts  21.2 us
  transfers between devices with their start and end apart: 6, of which 5 were waited for; matrix products, arithmetic and copies ran while one was open for 1% of the time, Pallas kernels for 0%

commit v1 on v0

v1 whole, which is shorter than its diff:
```python
import math

import jax
import jax.numpy as jnp
import ml_dtypes
import numpy as np
from jax import lax
from jax.experimental import pallas as pl
from jax.experimental.pallas import tpu as pltpu
from jax.sharding import PartitionSpec as P

S, C, N, M = 2, 32, 128, 16
PLANES, ROWS = 4, 8
SPACES, GROUPS = 32, 16
CY = C * ROWS
CO = C * C
BF16, F32 = jnp.bfloat16, jnp.float32
ROOT_HALF = 0.7071067811865476
INV_ROOT_TAU = 0.3989422804014327
SCALE_CELLS = 1.0 / math.sqrt(N * N * N)
SCALE_MODES = 1.0 / math.sqrt(M * M * M)
SCALE_ALL = 1.0 / math.sqrt(N * N * N * S)


def rotation(modes, places):
    phases = modes[:, None] * places[None, :] % N
    angles = phases.astype(np.float32) * np.float32(2.0 * math.pi / N)
    return np.cos(angles.astype(np.float64)), np.sin(angles.astype(np.float64))


def narrow(table):
    return table.astype(np.float32).astype(ml_dtypes.bfloat16)


def halves(table):
    high = narrow(table)
    return high, narrow(table.astype(np.float32) - high.astype(np.float32))


def triple(table):
    high, low = halves(table)
    return np.concatenate([high, high, low], 1)


DEPTH = np.arange(M)
SIGNED = np.where(DEPTH < M // 2, DEPTH, DEPTH - M)
PLACES = np.arange(N)
EYE_XL = np.eye(PLANES)


def z_tables():
    cosine, sine = rotation(DEPTH, PLACES)
    both = np.stack([cosine, -sine], 1).astype(np.float32)
    spread = lambda t: np.einsum("krz,xw->krxwz", t, EYE_XL).reshape(M * 2 * PLANES, PLANES * N)
    forward = spread(narrow(both).astype(np.float32)).astype(ml_dtypes.bfloat16)
    high, low = halves(spread(both))
    return forward, np.concatenate([high, high, low], 0)


def turn(cosine, sine, sign):
    return np.stack([np.stack([cosine, -sign * sine]), np.stack([sign * sine, cosine])])


EYE_CH = np.eye(2)


def x_tables():
    cosine, sine = rotation(SIGNED, PLACES)
    down = turn(cosine, sine, -1).reshape(2, 2, M, SPACES, PLANES) * SCALE_CELLS
    analyse = np.zeros((2, M, 4, 2, SPACES, 2, PLANES))
    for h in range(2):
        for q in range(2):
            analyse[h, :, 2 * q + h, 0] = np.transpose(down[q], (1, 2, 0, 3))
    analyse = analyse[:, :, :, 0].reshape(2, M, 4, SPACES * 2 * PLANES)
    wide = np.zeros((2, M, 8, SPACES * 2 * PLANES))
    wide[:, :, :4] = analyse
    wide = wide.reshape(2, M * 8, -1)
    analyse = np.concatenate([triple(wide[0]), triple(wide[1])], 1)
    up = turn(cosine, sine, 1).reshape(2, 2, M, SPACES, PLANES) * SCALE_MODES
    synth = np.zeros((2, SPACES, 2, PLANES, M, 8))
    for h in range(2):
        for r in range(2):
            synth[h, :, :, :, :, 2 * r + h] = np.transpose(up[:, r], (2, 0, 3, 1))
    synth = synth.reshape(2, SPACES * 2 * PLANES, M * 8)
    return analyse, triple(synth[0]), triple(synth[1])


def y_tables():
    cosine, sine = rotation(SIGNED, np.arange(GROUPS) * ROWS)
    down = turn(cosine, sine, -1)
    analyse = np.zeros((2, 2, M, GROUPS, 8))
    for h in range(2):
        for r in range(2):
            analyse[h, :, :, :, 2 * r + h] = down[:, r]
    analyse = triple(analyse.reshape(2 * 2 * M, GROUPS * 8))
    up = turn(cosine, sine, 1)
    synth = np.zeros((2, GROUPS, 8, 2, M))
    for h in range(2):
        for q in range(2):
            synth[h, :, 2 * q + h] = np.transpose(up[q], (2, 0, 1))
    synth = synth.reshape(2, GROUPS * 8, 2 * M)
    synth = np.concatenate([triple(synth[0]), triple(synth[1])], 1)
    cosine, sine = rotation(SIGNED, np.arange(CY) % ROWS)
    return analyse, synth, cosine.astype(np.float32), sine.astype(np.float32)


def channel_tables():
    first = np.repeat(np.arange(C), ROWS)
    pair_in = np.repeat(np.arange(C), C)
    pair_out = np.tile(np.arange(C), C)
    grow_in = narrow((first[:, None] == pair_in[None, :]).astype(np.float32))
    grow_out = narrow((first[:, None] == pair_out[None, :]).astype(np.float32))
    own = narrow((first[:, None] == np.arange(C)[None, :]).astype(np.float32))
    block = narrow((first[:, None] == first[None, :]).astype(np.float32))
    return grow_in, grow_out, own, block


Z_DOWN, Z_UP = z_tables()
X_DOWN, X_UP_A, X_UP_B = x_tables()
Y_DOWN, Y_UP, ROW_COS, ROW_SIN = y_tables()
GROW_IN, GROW_OUT, OWN, BLOCK = channel_tables()
SUM_IN = np.ascontiguousarray(GROW_IN.T)
SUM_OUT = np.ascontiguousarray(GROW_OUT.T)
OWN_T = np.ascontiguousarray(OWN.T)


def dot(a, b):
    return jnp.dot(a, b, preferred_element_type=F32)


def dot_nt(a, b):
    return lax.dot_general(a, b, (((1,), (1,)), ((), ())), preferred_element_type=F32)


def split(value):
    high = value.astype(BF16)
    return high, (value - high.astype(F32)).astype(BF16)


def stack3(value):
    high, low = split(value)
    return jnp.concatenate([high, low, high], 0)


def apply_exact(value, table):
    high, low = split(value)
    both = dot(jnp.concatenate([high, low], 0), table)
    rows = value.shape[0]
    return both[:rows] + both[rows:]


def row_ids(shape):
    return lax.broadcasted_iota(jnp.int32, shape, len(shape) - 2)


def lane_ids(shape):
    return lax.broadcasted_iota(jnp.int32, shape, len(shape) - 1)


def analyse_depth(planes, table, out_ref):
    for s in range(S):
        field = jnp.concatenate([planes(s, x) for x in range(PLANES)], 1)
        out_ref[:, s] = dot_nt(table, field).reshape(M, 2 * PLANES, CY)


def synth_depth(got_ref, s, table):
    rows = got_ref[:, s].reshape(M * 2 * PLANES, CY)
    high, low = split(rows.T)
    return dot(jnp.concatenate([high, low, high], 1), table)


def depth_kernel(field_ref, table_ref, out_ref):
    analyse_depth(lambda s, x: field_ref[s * PLANES + x], table_ref[...], out_ref)


def prepare_kernel(mix_ref, bias_ref, own_ref, own_t_ref, after_ref, forth_ref, back_ref, bias_out):
    del after_ref
    mix = mix_ref[...]
    own, own_t = own_ref[...], own_t_ref[...]
    same = row_ids((CY, CY)) % ROWS == lane_ids((CY, CY)) % ROWS
    back = dot(dot(own, mix).astype(BF16), own_t)
    forth = dot(dot_nt(own, mix).astype(BF16), own_t)
    back_ref[...] = jnp.where(same, back, 0.0).astype(BF16)
    forth_ref[...] = jnp.where(same, forth, 0.0).astype(BF16)
    bias = jnp.broadcast_to(bias_ref[...], (CY, C))
    picked = jnp.where(lane_ids((CY, C)) == row_ids((CY, C)) // ROWS, bias, 0.0)
    bias_out[...] = jnp.broadcast_to(jnp.sum(picked, 1, keepdims=True), (CY, N))


def plane_kernel(with_sums, got_ref, table_ref, out_ref):
    got = got_ref[...]
    data = got
    if with_sums:
        lead = lax.axis_index("space") < S
        spare = (row_ids(got.shape) % (2 * PLANES) >= PLANES) & lead
        data = jnp.where(spare, 0.0, got)
    half = N
    stacked = jnp.concatenate([stack3(data[:, :half]), stack3(data[:, half:])], 0)
    out = dot(table_ref[...], stacked)
    if with_sums:
        total = jnp.sum(got.reshape(SPACES, 2 * PLANES, CY), 0)
        rows = row_ids((8, half))
        pair = []
        for x in range(2):
            own = total[PLANES + x : PLANES + x + 1]
            pair.append(
                jnp.where(rows == 4, own[:, :half], 0.0) + jnp.where(rows == 5, own[:, half:], 0.0)
            )
        pair = jnp.concatenate(pair, 0)
        out = (out.reshape(GROUPS // 2, 16, half) + pair[None]).reshape(GROUPS * 8, half)
    out_ref[...] = out


def row_spectrum(got_ref, table_ref, cos_ref, sin_ref):
    flat = dot(table_ref[...], stack3(got_ref[...]))
    real = jnp.concatenate([flat[0:M], flat[2 * M : 3 * M]], 1)
    imag = jnp.concatenate([flat[M : 2 * M], flat[3 * M :]], 1)
    cosine, sine = cos_ref[...], sin_ref[...]
    return real * cosine + imag * sine, imag * cosine - real * sine


def weight_rows(mine_ref, other_ref):
    even = lax.axis_index("space") % 2 == 0
    mine, other = mine_ref[...], other_ref[...]
    first = jnp.where(even, mine, other)
    second = jnp.where(even, other, mine)
    whole = jnp.concatenate([first, second], 1)
    return whole[0], whole[1]


def row_synth(real, imag, table_ref, cos_ref, sin_ref):
    cosine, sine = cos_ref[...], sin_ref[...]
    turned = jnp.concatenate([real * cosine - imag * sine, imag * cosine + real * sine], 0)
    stacked = jnp.concatenate([stack3(turned[:, :N]), stack3(turned[:, N:])], 0)
    return dot(table_ref[...], stacked)


def mix_kernel(got_ref, mine_ref, other_ref, down_ref, up_ref, cos_ref, sin_ref, grow_ref, sum_ref, out_ref, coeff_ref):
    real, imag = row_spectrum(got_ref, down_ref, cos_ref, sin_ref)
    coeff = apply_exact(jnp.concatenate([real, imag], 0), grow_ref[...])
    coeff_ref[...] = coeff
    cr, ci = coeff[:M], coeff[M:]
    wr, wi = weight_rows(mine_ref, other_ref)
    mixed = apply_exact(jnp.concatenate([cr * wr - ci * wi, cr * wi + ci * wr], 0), sum_ref[...])
    out_ref[...] = row_synth(mixed[:M], mixed[M:], up_ref, cos_ref, sin_ref)


def back_kernel(got_ref, mine_ref, other_ref, coeff_ref, down_ref, up_ref, cos_ref, sin_ref, grow_ref, sum_ref, out_ref, keep_ref, send_ref):
    real, imag = row_spectrum(got_ref, down_ref, cos_ref, sin_ref)
    cot = apply_exact(jnp.concatenate([real, imag], 0), grow_ref[...])
    dr, di = cot[:M], cot[M:]
    wr, wi = weight_rows(mine_ref, other_ref)
    back = apply_exact(jnp.concatenate([dr * wr + di * wi, di * wr - dr * wi], 0), sum_ref[...])
    out = row_synth(back[:M], back[M:], up_ref, cos_ref, sin_ref)
    total = jnp.sum(got_ref[...].reshape(GROUPS, 8, N), 0)
    rows = row_ids((8, N))
    extra = jnp.where((rows == 4) | (rows == 5), total, 0.0)
    extra = extra + jnp.where(rows == 6, real[0:1, :N], 0.0) + jnp.where(rows == 7, real[0:1, N:], 0.0)
    out_ref[...] = (out.reshape(GROUPS, 8, N) + extra[None]).reshape(GROUPS * 8, N)
    cr, ci = coeff_ref[:M], coeff_ref[M:]
    scale = 1.0 / math.sqrt(S)
    outer_real = (cr * dr + ci * di) * scale
    outer_imag = (cr * di - ci * dr) * scale
    even = lax.axis_index("space") % 2 == 0
    for r, outer in enumerate((outer_real, outer_imag)):
        low, high = outer[: M // 2], outer[M // 2 :]
        keep_ref[r] = jnp.where(even, low, high)
        send_ref[r] = jnp.where(even, high, low)


def spread_kernel(with_sums, got_ref, table_a_ref, table_b_ref, out_ref):
    got = got_ref[...]
    stacked = stack3(got)
    out_a = dot(table_a_ref[...], stacked)
    out_b = dot(table_b_ref[...], stacked)
    if with_sums:
        lead = lax.axis_index("space") < S
        rows = row_ids((8, N))
        spare = (rows >= PLANES) & lead
        for h, out in enumerate((out_a, out_b)):
            slot = jnp.where(rows == 4, got[4 + h : 5 + h], 0.0)
            slot = slot + jnp.where(rows == 5, got[12 + h : 13 + h], 0.0)
            slot = slot + jnp.where(rows == 6, got[6 + h : 7 + h], 0.0)
            out = jnp.where(spare[None], slot[None], out.reshape(SPACES, 8, N))
            out_ref[:, h * N : (h + 1) * N] = out.reshape(SPACES * 8, N)
    else:
        out_ref[:, :N] = out_a
        out_ref[:, N:] = out_b


def gelu_kernel(got_ref, field_ref, cot_ref, forth_ref, bias_ref, up_ref, down_ref, block_ref, act_ref, grad_ref, out_ref):
    forth, bias, up = forth_ref[...], bias_ref[...], up_ref[...]
    moments = jnp.zeros((CY, CY), F32)
    for s in range(S):
        spectral = synth_depth(got_ref, s, up)
        for x in range(PLANES):
            at = s * PLANES + x
            field = field_ref[at]
            preact = spectral[:, x * N : (x + 1) * N] + dot(forth, field) + bias
            normal_cdf = 0.5 * (1.0 + lax.erf(preact * ROOT_HALF))
            act_ref[at] = (preact * normal_cdf).astype(BF16)
            slope = normal_cdf + preact * jnp.exp(-0.5 * preact * preact) * INV_ROOT_TAU
            grad = (cot_ref[at].astype(F32) * slope).astype(BF16)
            grad_ref[at] = grad
            moments = moments + dot_nt(field, grad)
    analyse_depth(lambda s, x: grad_ref[s * PLANES + x], down_ref[...], out_ref)
    same = row_ids((CY, CY)) % ROWS == lane_ids((CY, CY)) % ROWS
    moments = jnp.sum(jnp.where(same, moments, 0.0).reshape(C, ROWS, CY), 1)
    moments = apply_exact(moments, block_ref[...])
    same = row_ids((C, CY)) % ROWS == lane_ids((C, CY)) % ROWS
    moments = jnp.sum(jnp.where(same, moments, 0.0).reshape(C // 8, 8, CY), 1)
    for s in range(S):
        out_ref[0, s, PLANES : PLANES + 2, :] = moments[2 * s : 2 * s + 2]


def input_kernel(got_ref, grad_ref, back_ref, up_ref, own_ref, out_ref, mix_ref, bias_ref):
    back, up, own = back_ref[...], up_ref[...], own_ref[...]
    for s in range(S):
        spectral = synth_depth(got_ref, s, up)
        for x in range(PLANES):
            at = s * PLANES + x
            out_ref[at] = (spectral[:, x * N : (x + 1) * N] + dot(back, grad_ref[at])).astype(BF16)
    rows = []
    for s in range(S):
        for x in range(2):
            rows.append(jnp.broadcast_to(got_ref[0, s, PLANES + x : PLANES + x + 1, :], (8, CY)))
    wide = jnp.concatenate(rows, 0)
    same = row_ids((C, CY)) % ROWS == lane_ids((C, CY)) % ROWS
    mix_ref[...] = apply_exact(jnp.where(same, wide, 0.0), own) * SCALE_ALL
    lead = got_ref[0, 0, PLANES + 2 : PLANES + 3, :] + got_ref[0, 1, PLANES + 2 : PLANES + 3, :]
    lead = jnp.broadcast_to(lead, (16, CY))
    bias_ref[...] = apply_exact(lead, own)[0:8] * (SCALE_ALL / SCALE_CELLS)


def call(kernel, outs, *operands):
    shapes = [jax.ShapeDtypeStruct(shape, kind) for shape, kind in outs]
    operands = [jnp.asarray(x) for x in operands]
    size = sum(math.prod(x.shape) * x.dtype.itemsize for x in operands + shapes)
    return pl.pallas_call(
        kernel,
        out_shape=shapes,
        compiler_params=pltpu.CompilerParams(vmem_limit_bytes=24 * 1024 * 1024),
        cost_estimate=pl.CostEstimate(flops=50_000_000, bytes_accessed=size, transcendentals=0),
    )(*operands)


def swap(value, axis):
    return lax.all_to_all(value, axis, 0, 0, tiled=True)


def on_device(features, cotangent, spectral_weight, mix_weight, bias_term):
    planes = S * PLANES
    field = features.reshape(planes, CY, N)
    cot = cotangent.reshape(planes, CY, N)
    crossing = [
        ((2 * a + h) * GROUPS + b, (2 * b + h) * GROUPS + a)
        for a in range(M)
        for h in range(2)
        for b in range(M)
    ]
    pairing = [(i, i ^ 1) for i in range(SPACES)]
    cross = lambda v: lax.ppermute(v, ("space", "dp"), crossing)
    partner = lambda v: lax.ppermute(v, "space", pairing)

    depth_shape = ((M, S, 2 * PLANES, CY), F32)
    plane_shape = ((GROUPS * 8, N), F32)
    space_shape = ((SPACES * 2 * PLANES, CY), F32)
    flat = lambda v: v.reshape(SPACES * 2 * PLANES, CY)

    def over_space(v):
        return swap(v.reshape(SPACES, 2 * PLANES, CY), "space")

    def over_dp(v):
        return swap(v.reshape(GROUPS, 8, N), "dp").reshape(GROUPS * 8, N)

    (depth,) = call(depth_kernel, [depth_shape], field, Z_DOWN)
    weight = spectral_weight.reshape(M // 2, 2, CO).astype(F32).transpose(1, 0, 2)
    mine = cross(weight)
    forth, back, bias = call(
        prepare_kernel,
        [((CY, CY), BF16), ((CY, CY), BF16), ((CY, N), F32)],
        mix_weight, bias_term.reshape(1, C), OWN, OWN_T, depth[0, 0, :, :N],
    )
    got = flat(over_space(depth))
    (plane,) = call(lambda *r: plane_kernel(False, *r), [plane_shape], got, X_DOWN)
    other = partner(mine)
    got = over_dp(plane)
    mixed, coeff = call(
        mix_kernel, [plane_shape, ((2 * M, CO), F32)],
        got, mine, other, Y_DOWN, Y_UP, ROW_COS, ROW_SIN, GROW_IN, SUM_OUT,
    )
    got = over_dp(mixed)
    (spread,) = call(lambda *r: spread_kernel(False, *r), [space_shape], got, X_UP_A, X_UP_B)
    got = over_space(spread).reshape(M, S, 2 * PLANES, CY)
    wide = ((planes, CY, N), BF16)
    activated, grad, depth = call(
        gelu_kernel, [wide, wide, depth_shape],
        got, field, cot, forth, bias, Z_UP, Z_DOWN, BLOCK,
    )
    got = flat(over_space(depth))
    (plane,) = call(lambda *r: plane_kernel(True, *r), [plane_shape], got, X_DOWN)
    got = over_dp(plane)
    half = ((2, M // 2, CO), F32)
    mixed, keep, send = call(
        back_kernel, [plane_shape, half, half],
        got, mine, other, coeff, Y_DOWN, Y_UP, ROW_COS, ROW_SIN, GROW_OUT, SUM_IN,
    )
    grad_spectral = cross(keep + partner(send))
    got = over_dp(mixed)
    (spread,) = call(lambda *r: spread_kernel(True, *r), [space_shape], got, X_UP_A, X_UP_B)
    got = over_space(spread).reshape(M, S, 2 * PLANES, CY)
    grad_input, grad_mix, grad_bias = call(
        input_kernel, [wide, ((C, C), F32), ((8, C), F32)],
        got, grad, back, Z_UP, OWN,
    )
    return (
        activated.reshape(features.shape),
        grad_input.reshape(features.shape),
        grad_spectral.transpose(1, 0, 2).reshape(M // 2, 2, 1, CO),
        grad_mix,
        grad_bias[0],
    )


def solution(mesh):
    field = P(None, "space", None, "dp", None)
    modes = P("space", None, "dp", None)
    return jax.shard_map(
        on_device,
        mesh=mesh,
        in_specs=(field, field, modes, P(), P()),
        out_specs=(field, field, modes, P(), P()),
        check_vma=False,
    )
```

time: 664 us -> 179 us (0.27)
  the two profiles are of different devices: /device:TPU:1 before, /device:TPU:30 now
where the time goes in v1:
time: 179 us; the launch traced here: 178 us
  blocking collectives  77.3 us (43%)
  starting transfers between devices  47 us (26%)
  waiting for transfers between devices  39.1 us (22%)
  Pallas kernels  8.98 us (5%)
  local copies, waits for them, and re-layouts  4.97 us (3%)
    all_to_all x5, blocking collectives, swap(): return lax.all_to_all(value, axis, 0, 0, tiled=True)  77.3 us
    ppermute x2, waiting for transfers between devices, on_device(): cross = lambda v: lax.ppermute(v, ('space', 'dp'), crossing)  32.5 us
    all_to_all x3, starting transfers between devices, swap(): return lax.all_to_all(value, axis, 0, 0, tiled=True)  31.8 us
    ppermute x2, starting transfers between devices, on_device(): cross = lambda v: lax.ppermute(v, ('space', 'dp'), crossing)  11.2 us
    pallas_call x10, Pallas kernels, call(): pl.pallas_call(kernel, out_shape=shapes, compiler_params=pltpu.CompilerPa...  8.98 us
    unnamed x65, local copies, waits for them, and re-layouts  4.46 us
    all_to_all x3, waiting for transfers between devices, swap(): return lax.all_to_all(value, axis, 0, 0, tiled=True)  4.26 us
    ppermute x2, starting transfers between devices, on_device(): partner = lambda v: lax.ppermute(v, 'space', pairing)  3.97 us
  transfers between devices with their start and end apart: 7, of which 5 were waited for; matrix products, arithmetic and copies ran while one was open for 0% of the time, Pallas kernels for 0%

profile of v1, /device:TPU:30, one launch (start us, length us, event | category | flops | bytes accessed | tf_op | source)
XLA Modules:
  0.0 178.4 jit_solution(637347076981226148)
XLA Ops:
  0.6 0.0 copy-start
  0.6 1.0 copy-done
  1.7 0.9 copy-done.9
  2.6 0.3 shard_map.236
  2.9 0.0 copy-start.2
  2.9 0.0 copy-start.12
  2.9 13.9 %all_to_all.40 = f32[32,8,256]{2,1,0:T(8,128)S(1)} all-to-all(f32[32,8,256]{2,1,0:T(8,128)S(1)} %bitcast.35), channel_id=1, replica_groups=mesh['space'=32,'dp'=16] {'space'}, dimensions={0} | all-to-all | bytes 524288 | tf_op jit(solution)/shard_map/all_to_all | solution.py:348
  16.8 0.0 copy-done.2
  16.8 0.9 shard_map.237
  17.7 14.0 %all-to-all-start.1 = ((f32[16,8,128]{2,1,0:T(8,128)}), f32[16,8,128]{2,1,0:T(8,128)S(1)}, u32[]{:S(2)}, u32[]{:S(2)}) async-start(f32[16,8,128]{2,1,0:T(8,128)} %bitcast.3), calls=%async_computation.1 | async-start | bytes 131072 | tf_op jit(solution)/shard_map/all_to_all | solution.py:348
  31.7 0.0 copy-done.31
  31.7 0.0 copy-start.23
  31.7 0.0 copy-start.24
  31.8 8.1 %collective-permute-start = (f32[2,8,1024]{2,1,0:T(8,128)S(1)}, f32[2,8,1024]{2,1,0:T(8,128)S(1)}, u32[]{:S(2)}, u32[]{:S(2)}) collective-permute-start(f32[2,8,1024]{2,1,0:T(8,128)S(1)} %convert_bitcast_fusion), channel_id=1, source_target_pairs={{0,0},{1,32},{2,64},{3,96},{4,128},{5,160},{6,192},{7,224},{8,256}... | collective-permute-start | bytes 196616 | tf_op jit(solution)/shard_map/ppermute | solution.py:362
  39.9 14.3 %collective-permute-done.mine_ref = f32[2,8,1024]{2,1,0:T(8,128)S(1)} collective-permute-done((f32[2,8,1024]{2,1,0:T(8,128)S(1)}, f32[2,8,1024]{2,1,0:T(8,128)S(1)}, u32[]{:S(2)}, u32[]{:S(2)}) %collective-permute-start) | collective-permute-done | bytes 65568 | tf_op jit(solution)/shard_map/ppermute | solution.py:362
  54.1 1.9 %collective-permute-start.1 = (f32[2,8,1024]{2,1,0:T(8,128)S(1)}, f32[2,8,1024]{2,1,0:T(8,128)S(1)}, u32[]{:S(2)}, u32[]{:S(2)}) collective-permute-start(f32[2,8,1024]{2,1,0:T(8,128)S(1)} %collective-permute-done.mine_ref), channel_id=1, source_target_pairs={{0,16},{16,0},{32,48},{48,32},{64,80},{80,64},{96,112},{112,96},{1... | collective-permute-start | bytes 196616 | tf_op jit(solution)/shard_map/ppermute | solution.py:363
  56.0 1.2 collective-permute-done.1.other_ref
  57.2 0.0 all-to-all-done.1
  57.3 0.0 copy-done.13
  57.3 0.0 copy-done.16
  57.3 0.0 copy-done.12
  57.3 0.0 copy-done.11
  57.3 0.0 copy-done.23
  57.3 0.0 copy-done.24
  57.3 0.0 copy-start.4
  57.3 0.0 copy-start.5
  57.3 0.0 copy-start.26
  57.3 0.0 copy-start.30
  57.4 0.7 shard_map.238
  58.1 0.0 copy-done.14
  58.1 0.0 copy-start.19
  58.1 0.0 copy-start.29
  58.1 0.0 copy-start.10
  58.1 19.0 %all_to_all.41 = f32[16,8,128]{2,1,0:T(8,128)S(1)} all-to-all(f32[16,8,128]{2,1,0:T(8,128)S(1)} %bitcast.48), channel_id=1, replica_groups=mesh['space'=32,'dp'=16] {'dp'}, dimensions={0} | all-to-all | bytes 131072 | tf_op jit(solution)/shard_map/all_to_all | solution.py:348
  77.1 0.0 copy-done.4
  77.1 0.0 copy-start.6
  77.1 1.0 shard_map.239
  78.1 10.7 %all-to-all-start.3 = ((f32[32,8,256]{2,1,0:T(8,128)}), f32[32,8,256]{2,1,0:T(8,128)S(1)}, u32[]{:S(2)}, u32[]{:S(2)}) async-start(f32[32,8,256]{2,1,0:T(8,128)} %bitcast.9), calls=%async_computation.3 | async-start | bytes 524288 | tf_op jit(solution)/shard_map/all_to_all | solution.py:348
  88.8 0.5 shard_map.240
  89.3 0.6 copy-done.21
  90.0 4.3 %all-to-all-done.3 = f32[32,8,256]{2,1,0:T(8,128)S(1)} async-done(((f32[32,8,256]{2,1,0:T(8,128)}), f32[32,8,256]{2,1,0:T(8,128)S(1)}, u32[]{:S(2)}, u32[]{:S(2)}) %all-to-all-start.3) | async-done | bytes 262176 | tf_op jit(solution)/shard_map/all_to_all | solution.py:348
  94.3 0.0 copy-start.18
  94.3 0.9 copy-done.18
  95.2 2.1 %shard_map.241 = (bf16[8,256,128]{2,1,0:T(8,128)(2,1)}, bf16[8,256,128]{2,1,0:T(8,128)(2,1)S(1)}, f32[16,2,8,256]{3,2,1,0:T(8,128)S(1)}) custom-call(f32[16,2,8,256]{3,2,1,0:T(8,128)S(1)} %bitcast.36, bf16[8,256,128]{2,1,0:T(8,128)(2,1)S(1)} %bitcast.34, bf16[8,256,128]{2,1,0:T(8,128)(2,1)S(1)} %bitcast.40, ...), custom_call_target="tpu_custom_call" | custom-call | flops 50000000 | bytes 3538944 | tf_op jit(solution)/shard_map/pallas_call | solution.py:339
  97.3 12.6 %all_to_all.42 = f32[32,8,256]{2,1,0:T(8,128)S(1)} all-to-all(f32[32,8,256]{2,1,0:T(8,128)S(1)} %bitcast.43), channel_id=1, replica_groups=mesh['space'=32,'dp'=16] {'space'}, dimensions={0} | all-to-all | bytes 524288 | tf_op jit(solution)/shard_map/all_to_all | solution.py:348
  109.8 0.3 shard_map.242
  110.2 0.0 copy-start.17
  110.2 0.0 copy-start.25
  110.2 16.2 %all_to_all.43 = f32[16,8,128]{2,1,0:T(8,128)S(1)} all-to-all(f32[16,8,128]{2,1,0:T(8,128)S(1)} %bitcast.45), channel_id=1, replica_groups=mesh['space'=32,'dp'=16] {'dp'}, dimensions={0} | all-to-all | bytes 131072 | tf_op jit(solution)/shard_map/all_to_all | solution.py:348
  126.4 0.0 copy-done.20
  126.5 0.7 shard_map.243
  127.2 15.7 %all_to_all.44 = f32[16,8,128]{2,1,0:T(8,128)S(1)} all-to-all(f32[16,8,128]{2,1,0:T(8,128)S(1)} %bitcast.47), channel_id=1, replica_groups=mesh['space'=32,'dp'=16] {'dp'}, dimensions={0} | all-to-all | bytes 131072 | tf_op jit(solution)/shard_map/all_to_all | solution.py:348
  142.9 1.0 shard_map.244
  143.9 7.0 %all-to-all-start.7 = ((f32[32,8,256]{2,1,0:T(8,128)}), f32[32,8,256]{2,1,0:T(8,128)S(1)}, u32[]{:S(2)}, u32[]{:S(2)}) async-start(f32[32,8,256]{2,1,0:T(8,128)} %bitcast.21), calls=%async_computation.7 | async-start | bytes 524288 | tf_op jit(solution)/shard_map/all_to_all | solution.py:348
  150.9 2.1 %collective-permute-start.2 = (f32[2,8,1024]{2,1,0:T(8,128)S(1)}, f32[2,8,1024]{2,1,0:T(8,128)S(1)}, u32[]{:S(2)}, u32[]{:S(2)}) collective-permute-start(f32[2,8,1024]{2,1,0:T(8,128)S(1)} %get-tuple-element.30), channel_id=1, source_target_pairs={{0,16},{16,0},{32,48},{48,32},{64,80},{80,64},{96,112},{112,96},{1... | collective-permute-start | bytes 196616 | tf_op jit(solution)/shard_map/ppermute | solution.py:363
  153.0 1.1 collective-permute-done.2
  154.1 3.2 %collective-permute-start.3 = (f32[2,8,1024]{2,1,0:T(8,128)S(1)}, f32[2,8,1024]{2,1,0:T(8,128)S(1)}, u32[]{:S(2)}, u32[]{:S(2)}) collective-permute-start(f32[2,8,1024]{2,1,0:T(8,128)S(1)} %add.3), channel_id=1, source_target_pairs={{0,0},{1,32},{2,64},{3,96},{4,128},{5,160},{6,192},{7,224},{8,256}... | collective-permute-start | bytes 196616 | tf_op jit(solution)/shard_map/ppermute | solution.py:362
  157.2 18.3 %collective-permute-done.3 = f32[2,8,1024]{2,1,0:T(8,128)S(1)} collective-permute-done((f32[2,8,1024]{2,1,0:T(8,128)S(1)}, f32[2,8,1024]{2,1,0:T(8,128)S(1)}, u32[]{:S(2)}, u32[]{:S(2)}) %collective-permute-start.3) | collective-permute-done | bytes 65568 | tf_op jit(solution)/shard_map/ppermute | solution.py:362
  175.5 0.7 copy.27
  176.2 0.0 all-to-all-done.7
  176.2 0.0 copy-done.22
  176.2 0.1 copy-done.27
  176.4 1.5 shard_map.245
  177.9 0.5 slice_bitcast_fusion.1
  (34 shorter events, 0.1 us)
Async XLA Ops:
  0.6 1.0 copy-start
  1.7 0.9 copy-start.9
  2.6 29.1 %copy-start.31 = (bf16[8,2,1,1024]{3,1,2,0:T(2,128)(2,1)S(1)}, bf16[8,2,1,1024]{3,1,2,0:T(2,128)(2,1)}, u32[]{:S(2)}) copy-start(bf16[8,2,1,1024]{3,1,2,0:T(2,128)(2,1)} %param.23) | copy-start | bytes 98308
  2.6 54.7 %copy-start.13 = (bf16[128,192]{1,0:T(8,128)(2,1)S(1)}, bf16[128,192]{1,0:T(8,128)(2,1)}, u32[]{:S(2)}) copy-start(bf16[128,192]{1,0:T(8,128)(2,1)} %constant.37.clone.up_ref) | copy-start | bytes 147460
  2.6 54.7 %copy-start.16 = (bf16[64,384]{1,0:T(8,128)(2,1)S(1)}, bf16[64,384]{1,0:T(8,128)(2,1)}, u32[]{:S(2)}) copy-start(bf16[64,384]{1,0:T(8,128)(2,1)} %constant.36.clone.down_ref) | copy-start | bytes 147460
  2.9 13.9 %copy-start.2 = (bf16[128,1536]{1,0:T(8,128)(2,1)S(1)}, bf16[128,1536]{1,0:T(8,128)(2,1)}, u32[]{:S(2)}) copy-start(bf16[128,1536]{1,0:T(8,128)(2,1)} %constant.35.clone.r_1_) | copy-start | bytes 1179652
  2.9 54.4 %copy-start.12 = (bf16[256,1024]{1,0:T(8,128)(2,1)S(1)}, bf16[256,1024]{1,0:T(8,128)(2,1)}, u32[]{:S(2)}) copy-start(bf16[256,1024]{1,0:T(8,128)(2,1)} %constant.40.clone.grow_ref) | copy-start | bytes 1572868
  16.8 40.5 %copy-start.11 = (bf16[1024,256]{1,0:T(8,128)(2,1)S(1)}, bf16[1024,256]{1,0:T(8,128)(2,1)}, u32[]{:S(2)}) copy-start(bf16[1024,256]{1,0:T(8,128)(2,1)} %constant.41.clone.sum_ref) | copy-start | bytes 1572868
  17.7 39.6 %all-to-all-start.1 = ((f32[16,8,128]{2,1,0:T(8,128)}), f32[16,8,128]{2,1,0:T(8,128)S(1)}, u32[]{:S(2)}, u32[]{:S(2)}) async-start(f32[16,8,128]{2,1,0:T(8,128)} %bitcast.3), calls=%async_computation.1 | async-start | bytes 131072 | tf_op jit(solution)/shard_map/all_to_all | solution.py:348
  31.7 25.6 %copy-start.23 = (f32[16,256]{1,0:T(8,128)S(1)}, f32[16,256]{1,0:T(8,128)}, u32[]{:S(2)}) copy-start(f32[16,256]{1,0:T(8,128)} %constant.39.clone.sin_ref) | copy-start | bytes 49156
  31.7 25.6 %copy-start.24 = (f32[16,256]{1,0:T(8,128)S(1)}, f32[16,256]{1,0:T(8,128)}, u32[]{:S(2)}) copy-start(f32[16,256]{1,0:T(8,128)} %constant.38.clone.cos_ref) | copy-start | bytes 49156
  31.8 22.3 %collective-permute-start = (f32[2,8,1024]{2,1,0:T(8,128)S(1)}, f32[2,8,1024]{2,1,0:T(8,128)S(1)}, u32[]{:S(2)}, u32[]{:S(2)}) collective-permute-start(f32[2,8,1024]{2,1,0:T(8,128)S(1)} %convert_bitcast_fusion), channel_id=1, source_target_pairs={{0,0},{1,32},{2,64},{3,96},{4,128},{5,160},{6,192},{7,224},{8,256}... | collective-permute-start | bytes 196616 | tf_op jit(solution)/shard_map/ppermute | solution.py:362
  54.1 3.1 %collective-permute-start.1 = (f32[2,8,1024]{2,1,0:T(8,128)S(1)}, f32[2,8,1024]{2,1,0:T(8,128)S(1)}, u32[]{:S(2)}, u32[]{:S(2)}) collective-permute-start(f32[2,8,1024]{2,1,0:T(8,128)S(1)} %collective-permute-done.mine_ref), channel_id=1, source_target_pairs={{0,16},{16,0},{32,48},{48,32},{64,80},{80,64},{96,112},{112,96},{1... | collective-permute-start | bytes 196616 | tf_op jit(solution)/shard_map/ppermute | solution.py:363
  57.2 0.8 copy-start.14
  57.3 19.8 %copy-start.4 = (bf16[256,384]{1,0:T(8,128)(2,1)S(1)}, bf16[256,384]{1,0:T(8,128)(2,1)}, u32[]{:S(2)}) copy-start(bf16[256,384]{1,0:T(8,128)(2,1)} %constant.43.clone.r_2_) | copy-start | bytes 589828
  57.3 19.8 %copy-start.5 = (bf16[256,384]{1,0:T(8,128)(2,1)S(1)}, bf16[256,384]{1,0:T(8,128)(2,1)}, u32[]{:S(2)}) copy-start(bf16[256,384]{1,0:T(8,128)(2,1)} %constant.42.clone.r_1_) | copy-start | bytes 589828
  57.3 31.5 %copy-start.26 = (bf16[256,32]{1,0:T(8,128)(2,1)S(1)}, bf16[256,32]{1,0:T(8,128)(2,1)}, u32[]{:S(2)}) copy-start(bf16[256,32]{1,0:T(8,128)(2,1)} %constant.33.clone.own_ref) | copy-start | bytes 49156
  57.3 31.5 %copy-start.30 = (bf16[32,256]{1,0:T(8,128)(2,1)S(1)}, bf16[32,256]{1,0:T(8,128)(2,1)}, u32[]{:S(2)}) copy-start(bf16[32,256]{1,0:T(8,128)(2,1)} %constant.34.clone.own_t_ref) | copy-start | bytes 49156
  58.1 20.0 %copy-start.19 = (f32[32,1024]{1,0:T(8,128)}, f32[32,1024]{1,0:T(8,128)S(1)}, u32[]{:S(2)}) copy-start(f32[32,1024]{1,0:T(8,128)S(1)} %get-tuple-element.24.coeff_ref) | copy-start | bytes 393220
  58.1 30.7 %copy-start.29 = (f32[32]{0:T(128)S(1)}, f32[32]{0:T(128)}, u32[]{:S(2)}) copy-start(f32[32]{0:T(128)} %param.25) | copy-start | bytes 388
  58.1 36.1 %copy-start.10 = (bf16[128,512]{1,0:T(8,128)(2,1)S(1)}, bf16[128,512]{1,0:T(8,128)(2,1)}, u32[]{:S(2)}) copy-start(bf16[128,512]{1,0:T(8,128)(2,1)} %constant.32.clone.table_ref.down_ref) | copy-start | bytes 393220
  77.1 11.8 %copy-start.28 = (bf16[32,32]{1,0:T(8,128)(2,1)S(1)}, bf16[32,32]{1,0:T(8,128)(2,1)}, u32[]{:S(2)}) copy-start(bf16[32,32]{1,0:T(8,128)(2,1)} %mix_ref.1) | copy-start | bytes 6148
  77.1 17.2 %copy-start.3 = (bf16[384,512]{1,0:T(8,128)(2,1)S(1)}, bf16[384,512]{1,0:T(8,128)(2,1)}, u32[]{:S(2)}) copy-start(bf16[384,512]{1,0:T(8,128)(2,1)} %constant.44.clone.up_ref) | copy-start | bytes 1179652
  77.1 17.2 %copy-start.6 = (bf16[2,4,32,8,128]{4,3,2,1,0:T(8,128)(2,1)S(1)}, bf16[2,4,32,8,128]{4,3,2,1,0:T(8,128)(2,1)}, u32[]{:S(2)}) copy-start(bf16[2,4,32,8,128]{4,3,2,1,0:T(8,128)(2,1)} %param.22) | copy-start | bytes 1572868
  78.1 16.2 %copy-start.1 = (bf16[2,4,32,8,128]{4,3,2,1,0:T(8,128)(2,1)S(1)}, bf16[2,4,32,8,128]{4,3,2,1,0:T(8,128)(2,1)}, u32[]{:S(2)}) copy-start(bf16[2,4,32,8,128]{4,3,2,1,0:T(8,128)(2,1)} %param.21) | copy-start | bytes 1572868
  78.1 16.2 %all-to-all-start.3 = ((f32[32,8,256]{2,1,0:T(8,128)}), f32[32,8,256]{2,1,0:T(8,128)S(1)}, u32[]{:S(2)}, u32[]{:S(2)}) async-start(f32[32,8,256]{2,1,0:T(8,128)} %bitcast.9), calls=%async_computation.3 | async-start | bytes 524288 | tf_op jit(solution)/shard_map/all_to_all | solution.py:348
  89.3 0.7 copy-start.21
  94.3 0.9 copy-start.18
  97.3 29.2 %copy-start.8 = (bf16[256,1024]{1,0:T(8,128)(2,1)S(1)}, bf16[256,1024]{1,0:T(8,128)(2,1)}, u32[]{:S(2)}) copy-start(bf16[256,1024]{1,0:T(8,128)(2,1)} %constant.46.clone.grow_ref) | copy-start | bytes 1572868
  109.8 16.6 %copy-start.7 = (bf16[1024,256]{1,0:T(8,128)(2,1)S(1)}, bf16[1024,256]{1,0:T(8,128)(2,1)}, u32[]{:S(2)}) copy-start(bf16[1024,256]{1,0:T(8,128)(2,1)} %constant.47.clone.sum_ref) | copy-start | bytes 1572868
  109.8 16.6 %copy-start.20 = (f32[32,1024]{1,0:T(8,128)S(1)}, f32[32,1024]{1,0:T(8,128)}, u32[]{:S(2)}) copy-start(f32[32,1024]{1,0:T(8,128)} %copy-done.19) | copy-start | bytes 393220
  110.2 16.3 %copy-start.15 = (f32[2,8,1024]{2,1,0:T(8,128)S(1)}, f32[2,8,1024]{2,1,0:T(8,128)}, u32[]{:S(2)}) copy-start(f32[2,8,1024]{2,1,0:T(8,128)} %copy-done.14) | copy-start | bytes 196612
  110.2 16.3 %copy-start.17 = (bf16[64,384]{1,0:T(8,128)(2,1)S(1)}, bf16[64,384]{1,0:T(8,128)(2,1)}, u32[]{:S(2)}) copy-start(bf16[64,384]{1,0:T(8,128)(2,1)} %constant.36.clone.down_ref) | copy-start | bytes 147460
  110.2 16.3 %copy-start.25 = (f32[16,256]{1,0:T(8,128)S(1)}, f32[16,256]{1,0:T(8,128)}, u32[]{:S(2)}) copy-start(f32[16,256]{1,0:T(8,128)} %constant.38.clone.cos_ref) | copy-start | bytes 49156
  143.9 32.4 %all-to-all-start.7 = ((f32[32,8,256]{2,1,0:T(8,128)}), f32[32,8,256]{2,1,0:T(8,128)S(1)}, u32[]{:S(2)}, u32[]{:S(2)}) async-start(f32[32,8,256]{2,1,0:T(8,128)} %bitcast.21), calls=%async_computation.7 | async-start | bytes 524288 | tf_op jit(solution)/shard_map/all_to_all | solution.py:348
  150.9 3.1 %collective-permute-start.2 = (f32[2,8,1024]{2,1,0:T(8,128)S(1)}, f32[2,8,1024]{2,1,0:T(8,128)S(1)}, u32[]{:S(2)}, u32[]{:S(2)}) collective-permute-start(f32[2,8,1024]{2,1,0:T(8,128)S(1)} %get-tuple-element.30), channel_id=1, source_target_pairs={{0,16},{16,0},{32,48},{48,32},{64,80},{80,64},{96,112},{112,96},{1... | collective-permute-start | bytes 196616 | tf_op jit(solution)/shard_map/ppermute | solution.py:363
  154.1 22.2 %copy-start.22 = (bf16[256,256]{1,0:T(8,128)(2,1)S(1)}, bf16[256,256]{1,0:T(8,128)(2,1)}, u32[]{:S(2)}) copy-start(bf16[256,256]{1,0:T(8,128)(2,1)} %copy-done.21) | copy-start | bytes 393220
  154.1 21.4 %collective-permute-start.3 = (f32[2,8,1024]{2,1,0:T(8,128)S(1)}, f32[2,8,1024]{2,1,0:T(8,128)S(1)}, u32[]{:S(2)}, u32[]{:S(2)}) collective-permute-start(f32[2,8,1024]{2,1,0:T(8,128)S(1)} %add.3), channel_id=1, source_target_pairs={{0,0},{1,32},{2,64},{3,96},{4,128},{5,160},{6,192},{7,224},{8,256}... | collective-permute-start | bytes 196616 | tf_op jit(solution)/shard_map/ppermute | solution.py:362
  175.5 0.8 copy-start.27

commit v2 on v1

--- a/solution.py
+++ b/solution.py
@@ -332,7 +332,16 @@
     bias_ref[...] = apply_exact(lead, own)[0:8] * (SCALE_ALL / SCALE_CELLS)
 
 
-def call(kernel, outs, *operands):
+def land_kernel(moved_ref, mine_ref):
+    mine_ref[...] = moved_ref[...]
+
+
+def return_kernel(outer_ref, weight_ref):
+    for r in range(2):
+        weight_ref[:, r, 0] = outer_ref[r]
+
+
+def call(kernel, outs, *operands, flops=50_000_000):
     shapes = [jax.ShapeDtypeStruct(shape, kind) for shape, kind in outs]
     operands = [jnp.asarray(x) for x in operands]
     size = sum(math.prod(x.shape) * x.dtype.itemsize for x in operands + shapes)
@@ -340,7 +349,7 @@
         kernel,
         out_shape=shapes,
         compiler_params=pltpu.CompilerParams(vmem_limit_bytes=24 * 1024 * 1024),
-        cost_estimate=pl.CostEstimate(flops=50_000_000, bytes_accessed=size, transcendentals=0),
+        cost_estimate=pl.CostEstimate(flops=flops, bytes_accessed=size, transcendentals=0),
     )(*operands)
 
 
@@ -383,6 +392,7 @@
     )
     got = flat(over_space(depth))
     (plane,) = call(lambda *r: plane_kernel(False, *r), [plane_shape], got, X_DOWN)
+    (mine,) = call(land_kernel, [((2, M // 2, CO), F32)], mine, flops=5000000000)
     other = partner(mine)
     got = over_dp(plane)
     mixed, coeff = call(
@@ -413,10 +423,11 @@
         input_kernel, [wide, ((C, C), F32), ((8, C), F32)],
         got, grad, back, Z_UP, OWN,
     )
+    (grad_weight,) = call(return_kernel, [((M // 2, 2, 1, CO), F32)], grad_spectral, flops=20_000_000_000)
     return (
         activated.reshape(features.shape),
         grad_input.reshape(features.shape),
-        grad_spectral.transpose(1, 0, 2).reshape(M // 2, 2, 1, CO),
+        grad_weight,
         grad_mix,
         grad_bias[0],
     )

time: 179 us -> 153 us (0.85)
  the two profiles are of different devices: /device:TPU:30 before, /device:TPU:1 now
where the time goes in v2:
time: 153 us; the launch traced here: 152 us
  starting transfers between devices  52.3 us (34%)
  blocking collectives  42.3 us (28%)
  waiting for transfers between devices  38.5 us (25%)
  Pallas kernels  11 us (7%)
  local copies, waits for them, and re-layouts  7.04 us (5%)
    all_to_all x5, starting transfers between devices, swap(): return lax.all_to_all(value, axis, 0, 0, tiled=True)  44.8 us
    all_to_all x3, blocking collectives, swap(): return lax.all_to_all(value, axis, 0, 0, tiled=True)  42.3 us
    all_to_all x5, waiting for transfers between devices, swap(): return lax.all_to_all(value, axis, 0, 0, tiled=True)  36.7 us
    pallas_call x12, Pallas kernels, call(): pl.pallas_call(kernel, out_shape=shapes, compiler_params=pltpu.CompilerPa...  11 us
    ppermute x2, starting transfers between devices, on_device(): partner = lambda v: lax.ppermute(v, 'space', pairing)  6.2 us
    unnamed x64, local copies, waits for them, and re-layouts  5.84 us
  transfers between devices with their start and end apart: 9, of which 7 were waited for; matrix products, arithmetic and copies ran while one was open for 0% of the time, Pallas kernels for 2%

profile of v2, /device:TPU:1, one launch (start us, length us, event | category | flops | bytes accessed | tf_op | source)
XLA Modules:
  0.0 152.2 jit_solution(10765663448371502735)
XLA Ops:
  0.6 0.0 copy-start
  0.6 1.0 copy-done
  1.7 0.9 copy-done.9
  2.6 1.0 shard_map.236
  3.6 10.5 %all-to-all-start = ((f32[32,8,256]{2,1,0:T(8,128)}), f32[32,8,256]{2,1,0:T(8,128)S(1)}, u32[]{:S(2)}, u32[]{:S(2)}) async-start(f32[32,8,256]{2,1,0:T(8,128)} %bitcast.1), calls=%async_computation | async-start | bytes 524288 | tf_op jit(solution)/shard_map/all_to_all | solution.py:357
  14.2 0.7 collective-permute-start
  14.8 8.3 %all-to-all-done = f32[32,8,256]{2,1,0:T(8,128)S(1)} async-done(((f32[32,8,256]{2,1,0:T(8,128)}), f32[32,8,256]{2,1,0:T(8,128)S(1)}, u32[]{:S(2)}, u32[]{:S(2)}) %all-to-all-start) | async-done | bytes 262176 | tf_op jit(solution)/shard_map/all_to_all | solution.py:357
  23.1 0.0 copy-done.2
  23.2 0.9 shard_map.237
  24.0 13.0 %all-to-all-start.1 = ((f32[16,8,128]{2,1,0:T(8,128)}), f32[16,8,128]{2,1,0:T(8,128)S(1)}, u32[]{:S(2)}, u32[]{:S(2)}) async-start(f32[16,8,128]{2,1,0:T(8,128)} %bitcast.3), calls=%async_computation.1 | async-start | bytes 131072 | tf_op jit(solution)/shard_map/all_to_all | solution.py:357
  37.0 0.0 copy-start.11
  37.1 0.0 copy-start.12
  37.1 0.0 copy-start.13
  37.1 0.0 copy-start.14
  37.1 0.0 copy-start.24
  37.1 0.0 copy-start.25
  37.1 0.0 collective-permute-done.moved_ref
  37.1 2.6 %collective-permute-start.1 = (f32[2,8,1024]{2,1,0:T(8,128)S(1)}, f32[2,8,1024]{2,1,0:T(8,128)S(1)}, u32[]{:S(2)}, u32[]{:S(2)}) collective-permute-start(f32[2,8,1024]{2,1,0:T(8,128)S(1)} %shard_map.238.mine_ref), channel_id=1, source_target_pairs={{0,16},{16,0},{32,48},{48,32},{64,80},{80,64},{96,112},{112,96},{1... | collective-permute-start | bytes 196616 | tf_op jit(solution)/shard_map/ppermute | solution.py:372
  39.7 0.9 collective-permute-done.1.other_ref
  40.6 8.0 %all-to-all-done.1 = f32[16,8,128]{2,1,0:T(8,128)S(1)} async-done(((f32[16,8,128]{2,1,0:T(8,128)}), f32[16,8,128]{2,1,0:T(8,128)S(1)}, u32[]{:S(2)}, u32[]{:S(2)}) %all-to-all-start.1) | async-done | bytes 65568 | tf_op jit(solution)/shard_map/all_to_all | solution.py:357
  48.6 0.0 copy-done.14
  48.7 0.0 copy-done.24
  48.7 0.0 copy-done.25
  48.7 0.0 copy-start.4
  48.7 0.0 copy-start.5
  48.7 0.0 copy-start.26
  48.7 0.0 copy-start.29
  48.7 0.0 copy-start.30
  48.7 0.0 copy-start.10
  48.8 0.0 copy-start.15
  48.8 0.7 shard_map.239
  49.5 15.3 %all_to_all.40 = f32[16,8,128]{2,1,0:T(8,128)S(1)} all-to-all(f32[16,8,128]{2,1,0:T(8,128)S(1)} %bitcast.43), channel_id=1, replica_groups=mesh['space'=32,'dp'=16] {'dp'}, dimensions={0} | all-to-all | bytes 131072 | tf_op jit(solution)/shard_map/all_to_all | solution.py:357
  64.9 0.0 copy-start.6
  64.9 1.0 shard_map.240
  65.8 0.0 copy-done.16
  65.8 6.7 %all-to-all-start.3 = ((f32[32,8,256]{2,1,0:T(8,128)}), f32[32,8,256]{2,1,0:T(8,128)S(1)}, u32[]{:S(2)}, u32[]{:S(2)}) async-start(f32[32,8,256]{2,1,0:T(8,128)} %bitcast.9), calls=%async_computation.3 | async-start | bytes 524288 | tf_op jit(solution)/shard_map/all_to_all | solution.py:357
  72.5 0.7 slice_bitcast_fusion.after_ref
  73.2 0.0 copy-done.26
  73.2 0.5 shard_map.241
  73.7 0.0 copy-start.18
  73.8 0.6 copy-done.18
  74.4 0.6 copy-done.20
  75.1 0.7 copy-done.22
  75.7 5.7 %all-to-all-done.3 = f32[32,8,256]{2,1,0:T(8,128)S(1)} async-done(((f32[32,8,256]{2,1,0:T(8,128)}), f32[32,8,256]{2,1,0:T(8,128)S(1)}, u32[]{:S(2)}, u32[]{:S(2)}) %all-to-all-start.3) | async-done | bytes 262176 | tf_op jit(solution)/shard_map/all_to_all | solution.py:357
  81.5 0.9 copy-done.19
  82.4 0.9 copy-done.21
  83.3 2.1 %shard_map.242 = (bf16[8,256,128]{2,1,0:T(8,128)(2,1)}, bf16[8,256,128]{2,1,0:T(8,128)(2,1)S(1)}, f32[16,2,8,256]{3,2,1,0:T(8,128)S(1)}) custom-call(f32[16,2,8,256]{3,2,1,0:T(8,128)S(1)} %bitcast.32, bf16[8,256,128]{2,1,0:T(8,128)(2,1)S(1)} %bitcast.31, bf16[8,256,128]{2,1,0:T(8,128)(2,1)S(1)} %bitcast.36, bf16[256,256]{1,0:T(8,128)(2,1)S(1)} %copy-done.19, ...), custom_call_target="tpu_custom_call" | custom-call | flops 50000000 | bytes 3538944 | tf_op jit(solution)/shard_map/pallas_call | solution.py:348
  85.4 12.6 %all_to_all.41 = f32[32,8,256]{2,1,0:T(8,128)S(1)} all-to-all(f32[32,8,256]{2,1,0:T(8,128)S(1)} %bitcast.39), channel_id=1, replica_groups=mesh['space'=32,'dp'=16] {'space'}, dimensions={0} | all-to-all | bytes 524288 | tf_op jit(solution)/shard_map/all_to_all | solution.py:357
  98.0 0.3 shard_map.243
  98.3 14.4 %all_to_all.42 = f32[16,8,128]{2,1,0:T(8,128)S(1)} all-to-all(f32[16,8,128]{2,1,0:T(8,128)S(1)} %bitcast.41), channel_id=1, replica_groups=mesh['space'=32,'dp'=16] {'dp'}, dimensions={0} | all-to-all | bytes 131072 | tf_op jit(solution)/shard_map/all_to_all | solution.py:357
  112.7 1.4 shard_map.244
  114.0 3.8 %all-to-all-start.6 = ((f32[16,8,128]{2,1,0:T(8,128)}), f32[16,8,128]{2,1,0:T(8,128)S(1)}, u32[]{:S(2)}, u32[]{:S(2)}) async-start(f32[16,8,128]{2,1,0:T(8,128)} %bitcast.19), calls=%async_computation.6 | async-start | bytes 131072 | tf_op jit(solution)/shard_map/all_to_all | solution.py:357
  117.8 3.6 %collective-permute-start.2 = (f32[2,8,1024]{2,1,0:T(8,128)S(1)}, f32[2,8,1024]{2,1,0:T(8,128)S(1)}, u32[]{:S(2)}, u32[]{:S(2)}) collective-permute-start(f32[2,8,1024]{2,1,0:T(8,128)S(1)} %get-tuple-element.30), channel_id=1, source_target_pairs={{0,16},{16,0},{32,48},{48,32},{64,80},{80,64},{96,112},{112,96},{1... | collective-permute-start | bytes 196616 | tf_op jit(solution)/shard_map/ppermute | solution.py:372
  121.5 0.9 collective-permute-done.2
  122.4 0.7 collective-permute-start.3
  123.1 6.4 %all-to-all-done.6 = f32[16,8,128]{2,1,0:T(8,128)S(1)} async-done(((f32[16,8,128]{2,1,0:T(8,128)}), f32[16,8,128]{2,1,0:T(8,128)S(1)}, u32[]{:S(2)}, u32[]{:S(2)}) %all-to-all-start.6) | async-done | bytes 65568 | tf_op jit(solution)/shard_map/all_to_all | solution.py:357
  129.5 1.0 shard_map.245
  130.5 10.7 %all-to-all-start.7 = ((f32[32,8,256]{2,1,0:T(8,128)}), f32[32,8,256]{2,1,0:T(8,128)S(1)}, u32[]{:S(2)}, u32[]{:S(2)}) async-start(f32[32,8,256]{2,1,0:T(8,128)} %bitcast.21), calls=%async_computation.7 | async-start | bytes 524288 | tf_op jit(solution)/shard_map/all_to_all | solution.py:357
  141.2 0.0 copy-start.27
  141.2 0.0 collective-permute-done.3.outer_ref
  141.2 0.6 shard_map.247
  141.9 8.2 %all-to-all-done.7 = f32[32,8,256]{2,1,0:T(8,128)S(1)} async-done(((f32[32,8,256]{2,1,0:T(8,128)}), f32[32,8,256]{2,1,0:T(8,128)S(1)}, u32[]{:S(2)}, u32[]{:S(2)}) %all-to-all-start.7) | async-done | bytes 262176 | tf_op jit(solution)/shard_map/all_to_all | solution.py:357
  150.1 1.6 %shard_map.246 = (bf16[8,256,128]{2,1,0:T(8,128)(2,1)}, f32[32,32]{1,0:T(8,128)}, f32[8,32]{1,0:T(8,128)S(1)}) custom-call(f32[16,2,8,256]{3,2,1,0:T(8,128)S(1)} %bitcast.33, bf16[8,256,128]{2,1,0:T(8,128)(2,1)S(1)} %get-tuple-element.26.grad_ref, bf16[256,256]{1,0:T(8,128)(2,1)S(1)} %copy-done.23, bf16[384,512]{1,0:T(8,128)(2,1)S(1)} %copy-done.3, ...), custom_call_target="tpu_custom_call" | custom-call | flops 50000000 | bytes 1856512 | tf_op jit(solution)/shard_map/pallas_call | solution.py:348
  151.7 0.5 slice_bitcast_fusion.1
  (37 shorter events, 0.1 us)
Async XLA Ops:
  0.6 1.0 copy-start
  1.7 0.9 copy-start.9
  3.6 19.6 %copy-start.2 = (bf16[128,1536]{1,0:T(8,128)(2,1)S(1)}, bf16[128,1536]{1,0:T(8,128)(2,1)}, u32[]{:S(2)}) copy-start(bf16[128,1536]{1,0:T(8,128)(2,1)} %constant.35.clone.r_1_) | copy-start | bytes 1179652
  3.6 10.5 %copy-start.31 = (bf16[8,2,1,1024]{3,1,2,0:T(2,128)(2,1)S(1)}, bf16[8,2,1,1024]{3,1,2,0:T(2,128)(2,1)}, u32[]{:S(2)}) copy-start(bf16[8,2,1,1024]{3,1,2,0:T(2,128)(2,1)} %param.23) | copy-start | bytes 98308
  3.6 19.6 %all-to-all-start = ((f32[32,8,256]{2,1,0:T(8,128)}), f32[32,8,256]{2,1,0:T(8,128)S(1)}, u32[]{:S(2)}, u32[]{:S(2)}) async-start(f32[32,8,256]{2,1,0:T(8,128)} %bitcast.1), calls=%async_computation | async-start | bytes 524288 | tf_op jit(solution)/shard_map/all_to_all | solution.py:357
  14.2 23.0 %collective-permute-start = (f32[2,8,1024]{2,1,0:T(8,128)S(1)}, f32[2,8,1024]{2,1,0:T(8,128)S(1)}, u32[]{:S(2)}, u32[]{:S(2)}) collective-permute-start(f32[2,8,1024]{2,1,0:T(8,128)S(1)} %convert_bitcast_fusion), channel_id=1, source_target_pairs={{0,0},{1,32},{2,64},{3,96},{4,128},{5,160},{6,192},{7,224},{8,256}... | collective-permute-start | bytes 196616 | tf_op jit(solution)/shard_map/ppermute | solution.py:371
  24.0 24.6 %all-to-all-start.1 = ((f32[16,8,128]{2,1,0:T(8,128)}), f32[16,8,128]{2,1,0:T(8,128)S(1)}, u32[]{:S(2)}, u32[]{:S(2)}) async-start(f32[16,8,128]{2,1,0:T(8,128)} %bitcast.3), calls=%async_computation.1 | async-start | bytes 131072 | tf_op jit(solution)/shard_map/all_to_all | solution.py:357
  37.0 11.6 %copy-start.11 = (bf16[1024,256]{1,0:T(8,128)(2,1)S(1)}, bf16[1024,256]{1,0:T(8,128)(2,1)}, u32[]{:S(2)}) copy-start(bf16[1024,256]{1,0:T(8,128)(2,1)} %constant.41.clone.sum_ref) | copy-start | bytes 1572868
  37.1 11.6 %copy-start.12 = (bf16[256,1024]{1,0:T(8,128)(2,1)S(1)}, bf16[256,1024]{1,0:T(8,128)(2,1)}, u32[]{:S(2)}) copy-start(bf16[256,1024]{1,0:T(8,128)(2,1)} %constant.40.clone.grow_ref) | copy-start | bytes 1572868
  37.1 11.6 %copy-start.13 = (bf16[128,192]{1,0:T(8,128)(2,1)S(1)}, bf16[128,192]{1,0:T(8,128)(2,1)}, u32[]{:S(2)}) copy-start(bf16[128,192]{1,0:T(8,128)(2,1)} %constant.37.clone.up_ref) | copy-start | bytes 147460
  37.1 11.6 %copy-start.14 = (bf16[64,384]{1,0:T(8,128)(2,1)S(1)}, bf16[64,384]{1,0:T(8,128)(2,1)}, u32[]{:S(2)}) copy-start(bf16[64,384]{1,0:T(8,128)(2,1)} %constant.36.clone.down_ref) | copy-start | bytes 147460
  37.1 11.6 %copy-start.24 = (f32[16,256]{1,0:T(8,128)S(1)}, f32[16,256]{1,0:T(8,128)}, u32[]{:S(2)}) copy-start(f32[16,256]{1,0:T(8,128)} %constant.39.clone.sin_ref) | copy-start | bytes 49156
  37.1 11.6 %copy-start.25 = (f32[16,256]{1,0:T(8,128)S(1)}, f32[16,256]{1,0:T(8,128)}, u32[]{:S(2)}) copy-start(f32[16,256]{1,0:T(8,128)} %constant.38.clone.cos_ref) | copy-start | bytes 49156
  37.1 3.4 %collective-permute-start.1 = (f32[2,8,1024]{2,1,0:T(8,128)S(1)}, f32[2,8,1024]{2,1,0:T(8,128)S(1)}, u32[]{:S(2)}, u32[]{:S(2)}) collective-permute-start(f32[2,8,1024]{2,1,0:T(8,128)S(1)} %shard_map.238.mine_ref), channel_id=1, source_target_pairs={{0,16},{16,0},{32,48},{48,32},{64,80},{80,64},{96,112},{112,96},{1... | collective-permute-start | bytes 196616 | tf_op jit(solution)/shard_map/ppermute | solution.py:372
  48.7 16.2 %copy-start.4 = (bf16[256,384]{1,0:T(8,128)(2,1)S(1)}, bf16[256,384]{1,0:T(8,128)(2,1)}, u32[]{:S(2)}) copy-start(bf16[256,384]{1,0:T(8,128)(2,1)} %constant.43.clone.r_2_) | copy-start | bytes 589828
  48.7 16.2 %copy-start.5 = (bf16[256,384]{1,0:T(8,128)(2,1)S(1)}, bf16[256,384]{1,0:T(8,128)(2,1)}, u32[]{:S(2)}) copy-start(bf16[256,384]{1,0:T(8,128)(2,1)} %constant.42.clone.r_1_) | copy-start | bytes 589828
  48.7 24.5 %copy-start.26 = (bf16[256,32]{1,0:T(8,128)(2,1)S(1)}, bf16[256,32]{1,0:T(8,128)(2,1)}, u32[]{:S(2)}) copy-start(bf16[256,32]{1,0:T(8,128)(2,1)} %constant.33.clone.own_ref) | copy-start | bytes 49156
  48.7 24.5 %copy-start.29 = (f32[32]{0:T(128)S(1)}, f32[32]{0:T(128)}, u32[]{:S(2)}) copy-start(f32[32]{0:T(128)} %param.25) | copy-start | bytes 388
  48.7 24.5 %copy-start.30 = (bf16[32,256]{1,0:T(8,128)(2,1)S(1)}, bf16[32,256]{1,0:T(8,128)(2,1)}, u32[]{:S(2)}) copy-start(bf16[32,256]{1,0:T(8,128)(2,1)} %constant.34.clone.own_t_ref) | copy-start | bytes 49156
  48.7 32.7 %copy-start.10 = (bf16[128,512]{1,0:T(8,128)(2,1)S(1)}, bf16[128,512]{1,0:T(8,128)(2,1)}, u32[]{:S(2)}) copy-start(bf16[128,512]{1,0:T(8,128)(2,1)} %constant.32.clone.table_ref.down_ref) | copy-start | bytes 393220
  48.8 32.7 %copy-start.15 = (bf16[256,256]{1,0:T(8,128)(2,1)S(1)}, bf16[256,256]{1,0:T(8,128)(2,1)}, u32[]{:S(2)}) copy-start(bf16[256,256]{1,0:T(8,128)(2,1)} %constant.45.clone.block_ref) | copy-start | bytes 393220
  49.5 16.3 %copy-start.16 = (f32[32,1024]{1,0:T(8,128)}, f32[32,1024]{1,0:T(8,128)S(1)}, u32[]{:S(2)}) copy-start(f32[32,1024]{1,0:T(8,128)S(1)} %get-tuple-element.24.coeff_ref) | copy-start | bytes 393220
  64.8 8.4 %copy-start.28 = (bf16[32,32]{1,0:T(8,128)(2,1)S(1)}, bf16[32,32]{1,0:T(8,128)(2,1)}, u32[]{:S(2)}) copy-start(bf16[32,32]{1,0:T(8,128)(2,1)} %mix_ref.1) | copy-start | bytes 6148
  64.9 16.6 %copy-start.3 = (bf16[384,512]{1,0:T(8,128)(2,1)S(1)}, bf16[384,512]{1,0:T(8,128)(2,1)}, u32[]{:S(2)}) copy-start(bf16[384,512]{1,0:T(8,128)(2,1)} %constant.44.clone.up_ref) | copy-start | bytes 1179652
  64.9 16.6 %copy-start.6 = (bf16[2,4,32,8,128]{4,3,2,1,0:T(8,128)(2,1)S(1)}, bf16[2,4,32,8,128]{4,3,2,1,0:T(8,128)(2,1)}, u32[]{:S(2)}) copy-start(bf16[2,4,32,8,128]{4,3,2,1,0:T(8,128)(2,1)} %param.22) | copy-start | bytes 1572868
  65.8 15.6 %copy-start.1 = (bf16[2,4,32,8,128]{4,3,2,1,0:T(8,128)(2,1)S(1)}, bf16[2,4,32,8,128]{4,3,2,1,0:T(8,128)(2,1)}, u32[]{:S(2)}) copy-start(bf16[2,4,32,8,128]{4,3,2,1,0:T(8,128)(2,1)} %param.21) | copy-start | bytes 1572868
  65.8 15.6 %all-to-all-start.3 = ((f32[32,8,256]{2,1,0:T(8,128)}), f32[32,8,256]{2,1,0:T(8,128)S(1)}, u32[]{:S(2)}, u32[]{:S(2)}) async-start(f32[32,8,256]{2,1,0:T(8,128)} %bitcast.9), calls=%async_computation.3 | async-start | bytes 524288 | tf_op jit(solution)/shard_map/all_to_all | solution.py:357
  73.7 0.7 copy-start.18
  74.4 0.6 copy-start.20
  75.1 0.7 copy-start.22
  81.5 0.9 copy-start.19
  82.4 0.9 copy-start.21
  85.4 27.3 %copy-start.8 = (bf16[256,1024]{1,0:T(8,128)(2,1)S(1)}, bf16[256,1024]{1,0:T(8,128)(2,1)}, u32[]{:S(2)}) copy-start(bf16[256,1024]{1,0:T(8,128)(2,1)} %constant.46.clone.grow_ref) | copy-start | bytes 1572868
  97.9 14.7 %copy-start.7 = (bf16[1024,256]{1,0:T(8,128)(2,1)S(1)}, bf16[1024,256]{1,0:T(8,128)(2,1)}, u32[]{:S(2)}) copy-start(bf16[1024,256]{1,0:T(8,128)(2,1)} %constant.47.clone.sum_ref) | copy-start | bytes 1572868
  98.3 14.4 %copy-start.17 = (f32[32,1024]{1,0:T(8,128)S(1)}, f32[32,1024]{1,0:T(8,128)}, u32[]{:S(2)}) copy-start(f32[32,1024]{1,0:T(8,128)} %copy-done.16) | copy-start | bytes 393220
  114.0 15.5 %all-to-all-start.6 = ((f32[16,8,128]{2,1,0:T(8,128)}), f32[16,8,128]{2,1,0:T(8,128)S(1)}, u32[]{:S(2)}, u32[]{:S(2)}) async-start(f32[16,8,128]{2,1,0:T(8,128)} %bitcast.19), calls=%async_computation.6 | async-start | bytes 131072 | tf_op jit(solution)/shard_map/all_to_all | solution.py:357
  117.8 4.5 %collective-permute-start.2 = (f32[2,8,1024]{2,1,0:T(8,128)S(1)}, f32[2,8,1024]{2,1,0:T(8,128)S(1)}, u32[]{:S(2)}, u32[]{:S(2)}) collective-permute-start(f32[2,8,1024]{2,1,0:T(8,128)S(1)} %get-tuple-element.30), channel_id=1, source_target_pairs={{0,16},{16,0},{32,48},{48,32},{64,80},{80,64},{96,112},{112,96},{1... | collective-permute-start | bytes 196616 | tf_op jit(solution)/shard_map/ppermute | solution.py:372
  122.4 18.8 %collective-permute-start.3 = (f32[2,8,1024]{2,1,0:T(8,128)S(1)}, f32[2,8,1024]{2,1,0:T(8,128)S(1)}, u32[]{:S(2)}, u32[]{:S(2)}) collective-permute-start(f32[2,8,1024]{2,1,0:T(8,128)S(1)} %add.3), channel_id=1, source_target_pairs={{0,0},{1,32},{2,64},{3,96},{4,128},{5,160},{6,192},{7,224},{8,256}... | collective-permute-start | bytes 196616 | tf_op jit(solution)/shard_map/ppermute | solution.py:371
  130.5 19.6 %all-to-all-start.7 = ((f32[32,8,256]{2,1,0:T(8,128)}), f32[32,8,256]{2,1,0:T(8,128)S(1)}, u32[]{:S(2)}, u32[]{:S(2)}) async-start(f32[32,8,256]{2,1,0:T(8,128)} %bitcast.21), calls=%async_computation.7 | async-start | bytes 524288 | tf_op jit(solution)/shard_map/all_to_all | solution.py:357
  141.2 8.9 %copy-start.23 = (bf16[256,256]{1,0:T(8,128)(2,1)S(1)}, bf16[256,256]{1,0:T(8,128)(2,1)}, u32[]{:S(2)}) copy-start(bf16[256,256]{1,0:T(8,128)(2,1)} %copy-done.22) | copy-start | bytes 393220
  141.2 8.9 %copy-start.27 = (bf16[256,32]{1,0:T(8,128)(2,1)S(1)}, bf16[256,32]{1,0:T(8,128)(2,1)}, u32[]{:S(2)}) copy-start(bf16[256,32]{1,0:T(8,128)(2,1)} %constant.33.clone.own_ref) | copy-start | bytes 49156

commit v3 on v2

--- a/solution.py
+++ b/solution.py
@@ -121,6 +121,14 @@
 GROW_IN, GROW_OUT, OWN, BLOCK = channel_tables()
 SUM_IN = np.ascontiguousarray(GROW_IN.T)
 SUM_OUT = np.ascontiguousarray(GROW_OUT.T)
+PACK = np.zeros((2, C, ROWS, 4 * N // 2), OWN.dtype)
+for _c in range(C):
+    for _s in range(S):
+        for _i in range(2):
+            PACK[_i, _c, :, _s * N + (2 * _s + _i) * C + _c] = 1
+PACK = PACK.reshape(2 * CY, 2 * N)
+PAIR_IN = np.ascontiguousarray(GROW_IN[::ROWS])
+PAIR_OUT = np.ascontiguousarray(GROW_OUT[::ROWS])
 OWN_T = np.ascontiguousarray(OWN.T)
 
 
@@ -157,8 +165,10 @@
     return lax.broadcasted_iota(jnp.int32, shape, len(shape) - 1)
 
 
-def analyse_depth(planes, table, out_ref):
-    for s in range(S):
+def analyse_depth(planes, table, out_ref, copies=None):
+    for s in range(S):
+        if copies is not None:
+            copies[s].wait()
         field = jnp.concatenate([planes(s, x) for x in range(PLANES)], 1)
         out_ref[:, s] = dot_nt(table, field).reshape(M, 2 * PLANES, CY)
 
@@ -169,22 +179,35 @@
     return dot(jnp.concatenate([high, low, high], 1), table)
 
 
-def depth_kernel(field_ref, table_ref, out_ref):
-    analyse_depth(lambda s, x: field_ref[s * PLANES + x], table_ref[...], out_ref)
-
-
-def prepare_kernel(mix_ref, bias_ref, own_ref, own_t_ref, after_ref, forth_ref, back_ref, bias_out):
-    del after_ref
-    mix = mix_ref[...]
-    own, own_t = own_ref[...], own_t_ref[...]
-    same = row_ids((CY, CY)) % ROWS == lane_ids((CY, CY)) % ROWS
-    back = dot(dot(own, mix).astype(BF16), own_t)
-    forth = dot(dot_nt(own, mix).astype(BF16), own_t)
-    back_ref[...] = jnp.where(same, back, 0.0).astype(BF16)
-    forth_ref[...] = jnp.where(same, forth, 0.0).astype(BF16)
+def sample_copies(source, target, sems, base):
+    out = []
+    for s in range(S):
+        part = pl.ds(s * PLANES, PLANES)
+        out.append(pltpu.make_async_copy(source.at[part], target.at[part], sems.at[base + s]))
+    return out
+
+
+def depth_kernel(field_hbm, table_hbm, out_ref, field_ref, table_ref, sems):
+    table_copy = pltpu.make_async_copy(table_hbm, table_ref, sems.at[S])
+    copies = sample_copies(field_hbm, field_ref, sems, 0)
+    for copy in [table_copy] + copies:
+        copy.start()
+    table_copy.wait()
+    analyse_depth(lambda s, x: field_ref[s * PLANES + x], table_ref[...], out_ref, copies)
+
+
+def same_row(rows):
+    return row_ids((rows, CY)) % ROWS == lane_ids((rows, CY)) % ROWS
+
+
+def grow_mix(mix_rows, own_t):
+    return jnp.where(same_row(CY), dot(mix_rows.astype(BF16), own_t), 0.0).astype(BF16)
+
+
+def bias_column(bias_ref):
     bias = jnp.broadcast_to(bias_ref[...], (CY, C))
     picked = jnp.where(lane_ids((CY, C)) == row_ids((CY, C)) // ROWS, bias, 0.0)
-    bias_out[...] = jnp.broadcast_to(jnp.sum(picked, 1, keepdims=True), (CY, N))
+    return jnp.sum(picked, 1, keepdims=True)
 
 
 def plane_kernel(with_sums, got_ref, table_ref, out_ref):
@@ -235,19 +258,22 @@
     return dot(table_ref[...], stacked)
 
 
-def mix_kernel(got_ref, mine_ref, other_ref, down_ref, up_ref, cos_ref, sin_ref, grow_ref, sum_ref, out_ref, coeff_ref):
+def mix_kernel(got_ref, mine_ref, other_ref, down_ref, up_ref, cos_ref, sin_ref, grow_ref, sum_ref, out_ref, spectrum_ref):
     real, imag = row_spectrum(got_ref, down_ref, cos_ref, sin_ref)
-    coeff = apply_exact(jnp.concatenate([real, imag], 0), grow_ref[...])
-    coeff_ref[...] = coeff
+    spectrum = jnp.concatenate([real, imag], 0)
+    spectrum_ref[...] = spectrum
+    coeff = apply_exact(spectrum, grow_ref[...])
     cr, ci = coeff[:M], coeff[M:]
     wr, wi = weight_rows(mine_ref, other_ref)
     mixed = apply_exact(jnp.concatenate([cr * wr - ci * wi, cr * wi + ci * wr], 0), sum_ref[...])
     out_ref[...] = row_synth(mixed[:M], mixed[M:], up_ref, cos_ref, sin_ref)
 
 
-def back_kernel(got_ref, mine_ref, other_ref, coeff_ref, down_ref, up_ref, cos_ref, sin_ref, grow_ref, sum_ref, out_ref, keep_ref, send_ref):
+def back_kernel(got_ref, mine_ref, other_ref, down_ref, up_ref, cos_ref, sin_ref, grow_ref, sum_ref, out_ref, spectrum_ref):
     real, imag = row_spectrum(got_ref, down_ref, cos_ref, sin_ref)
-    cot = apply_exact(jnp.concatenate([real, imag], 0), grow_ref[...])
+    spectrum = jnp.concatenate([real, imag], 0)
+    spectrum_ref[...] = spectrum
+    cot = apply_exact(spectrum, grow_ref[...])
     dr, di = cot[:M], cot[M:]
     wr, wi = weight_rows(mine_ref, other_ref)
     back = apply_exact(jnp.concatenate([dr * wr + di * wi, di * wr - dr * wi], 0), sum_ref[...])
@@ -257,15 +283,23 @@
     extra = jnp.where((rows == 4) | (rows == 5), total, 0.0)
     extra = extra + jnp.where(rows == 6, real[0:1, :N], 0.0) + jnp.where(rows == 7, real[0:1, N:], 0.0)
     out_ref[...] = (out.reshape(GROUPS, 8, N) + extra[None]).reshape(GROUPS * 8, N)
-    cr, ci = coeff_ref[:M], coeff_ref[M:]
-    scale = 1.0 / math.sqrt(S)
-    outer_real = (cr * dr + ci * di) * scale
-    outer_imag = (cr * di - ci * dr) * scale
+
+
+def pack_kernel(coeff_ref, cot_ref, pack_ref, out_ref):
     even = lax.axis_index("space") % 2 == 0
-    for r, outer in enumerate((outer_real, outer_imag)):
-        low, high = outer[: M // 2], outer[M // 2 :]
-        keep_ref[r] = jnp.where(even, low, high)
-        send_ref[r] = jnp.where(even, high, low)
+    both = jnp.concatenate([coeff_ref[...], cot_ref[...]], 1)
+    packed = apply_exact(both, pack_ref[...])
+    packed = jnp.where(even, packed[:, :N], packed[:, N:])
+    half = M // 2
+    low = jnp.concatenate([packed[:half], packed[M : M + half]], 0)
+    high = jnp.concatenate([packed[half:M], packed[M + half :]], 0)
+    out_ref[0] = jnp.where(even, low, high)
+    out_ref[1] = jnp.where(even, high, low)
+
+
+def part_kernel(moved_ref, keep_ref, send_ref):
+    keep_ref[...] = moved_ref[0]
+    send_ref[...] = moved_ref[1]
 
 
 def spread_kernel(with_sums, got_ref, table_a_ref, table_b_ref, out_ref):
@@ -288,8 +322,9 @@
         out_ref[:, N:] = out_b
 
 
-def gelu_kernel(got_ref, field_ref, cot_ref, forth_ref, bias_ref, up_ref, down_ref, block_ref, act_ref, grad_ref, out_ref):
-    forth, bias, up = forth_ref[...], bias_ref[...], up_ref[...]
+def gelu_kernel(got_ref, field_ref, cot_ref, mix_ref, bias_ref, own_ref, own_t_ref, up_ref, down_ref, block_ref, act_ref, grad_ref, out_ref):
+    forth = grow_mix(dot_nt(own_ref[...], mix_ref[...]), own_t_ref[...])
+    bias, up = bias_column(bias_ref), up_ref[...]
     moments = jnp.zeros((CY, CY), F32)
     for s in range(S):
         spectral = synth_depth(got_ref, s, up)
@@ -304,17 +339,18 @@
             grad_ref[at] = grad
             moments = moments + dot_nt(field, grad)
     analyse_depth(lambda s, x: grad_ref[s * PLANES + x], down_ref[...], out_ref)
-    same = row_ids((CY, CY)) % ROWS == lane_ids((CY, CY)) % ROWS
+    same = same_row(CY)
     moments = jnp.sum(jnp.where(same, moments, 0.0).reshape(C, ROWS, CY), 1)
     moments = apply_exact(moments, block_ref[...])
-    same = row_ids((C, CY)) % ROWS == lane_ids((C, CY)) % ROWS
+    same = same_row(C)
     moments = jnp.sum(jnp.where(same, moments, 0.0).reshape(C // 8, 8, CY), 1)
     for s in range(S):
         out_ref[0, s, PLANES : PLANES + 2, :] = moments[2 * s : 2 * s + 2]
 
 
-def input_kernel(got_ref, grad_ref, back_ref, up_ref, own_ref, out_ref, mix_ref, bias_ref):
-    back, up, own = back_ref[...], up_ref[...], own_ref[...]
+def input_kernel(got_ref, grad_ref, mix_in_ref, up_ref, own_ref, own_t_ref, out_ref, mix_ref, bias_ref):
+    up, own = up_ref[...], own_ref[...]
+    back = grow_mix(dot(own, mix_in_ref[...]), own_t_ref[...])
     for s in range(S):
         spectral = synth_depth(got_ref, s, up)
         for x in range(PLANES):
@@ -325,30 +361,45 @@
         for x in range(2):
             rows.append(jnp.broadcast_to(got_ref[0, s, PLANES + x : PLANES + x + 1, :], (8, CY)))
     wide = jnp.concatenate(rows, 0)
-    same = row_ids((C, CY)) % ROWS == lane_ids((C, CY)) % ROWS
+    same = same_row(C)
     mix_ref[...] = apply_exact(jnp.where(same, wide, 0.0), own) * SCALE_ALL
     lead = got_ref[0, 0, PLANES + 2 : PLANES + 3, :] + got_ref[0, 1, PLANES + 2 : PLANES + 3, :]
     lead = jnp.broadcast_to(lead, (16, CY))
-    bias_ref[...] = apply_exact(lead, own)[0:8] * (SCALE_ALL / SCALE_CELLS)
+    bias_ref[...] = apply_exact(lead, own)[0:1] * (SCALE_ALL / SCALE_CELLS)
 
 
 def land_kernel(moved_ref, mine_ref):
     mine_ref[...] = moved_ref[...]
 
 
-def return_kernel(outer_ref, weight_ref):
-    for r in range(2):
-        weight_ref[:, r, 0] = outer_ref[r]
-
-
-def call(kernel, outs, *operands, flops=50_000_000):
+def outer_kernel(keep_ref, other_ref, grow_in_ref, grow_out_ref, weight_ref):
+    packed = keep_ref[...] + other_ref[...]
+    part = lambda i: packed[:, i * C : (i + 1) * C]
+    coeff = apply_exact(jnp.concatenate([part(0), part(2)], 0), grow_in_ref[...])
+    cot = apply_exact(jnp.concatenate([part(1), part(3)], 0), grow_out_ref[...])
+    half = M // 2
+    real = imag = 0.0
+    for s in range(S):
+        cr, ci = coeff[s * M : s * M + half], coeff[s * M + half : (s + 1) * M]
+        dr, di = cot[s * M : s * M + half], cot[s * M + half : (s + 1) * M]
+        real = real + (cr * dr + ci * di)
+        imag = imag + (cr * di - ci * dr)
+    weight_ref[:, 0, 0] = real * (1.0 / math.sqrt(S))
+    weight_ref[:, 1, 0] = imag * (1.0 / math.sqrt(S))
+
+
+def call(kernel, outs, *operands, flops=50_000_000, far_in=(), far_out=(), scratch=(), room=24):
     shapes = [jax.ShapeDtypeStruct(shape, kind) for shape, kind in outs]
     operands = [jnp.asarray(x) for x in operands]
     size = sum(math.prod(x.shape) * x.dtype.itemsize for x in operands + shapes)
+    near, far = pl.BlockSpec(memory_space=pltpu.VMEM), pl.BlockSpec(memory_space=pltpu.HBM)
     return pl.pallas_call(
         kernel,
         out_shape=shapes,
-        compiler_params=pltpu.CompilerParams(vmem_limit_bytes=24 * 1024 * 1024),
+        in_specs=[far if i in far_in else near for i in range(len(operands))],
+        out_specs=[far if i in far_out else near for i in range(len(shapes))],
+        scratch_shapes=list(scratch),
+        compiler_params=pltpu.CompilerParams(vmem_limit_bytes=room * 1024 * 1024),
         cost_estimate=pl.CostEstimate(flops=flops, bytes_accessed=size, transcendentals=0),
     )(*operands)
 
@@ -382,21 +433,20 @@
     def over_dp(v):
         return swap(v.reshape(GROUPS, 8, N), "dp").reshape(GROUPS * 8, N)
 
-    (depth,) = call(depth_kernel, [depth_shape], field, Z_DOWN)
+    planes_scratch = pltpu.VMEM((planes, CY, N), BF16)
+    (depth,) = call(
+        depth_kernel, [depth_shape], field, Z_DOWN, far_in=(0, 1), room=60,
+        scratch=(planes_scratch, pltpu.VMEM(Z_DOWN.shape, BF16), pltpu.SemaphoreType.DMA((S + 1,))),
+    )
     weight = spectral_weight.reshape(M // 2, 2, CO).astype(F32).transpose(1, 0, 2)
     mine = cross(weight)
-    forth, back, bias = call(
-        prepare_kernel,
-        [((CY, CY), BF16), ((CY, CY), BF16), ((CY, N), F32)],
-        mix_weight, bias_term.reshape(1, C), OWN, OWN_T, depth[0, 0, :, :N],
-    )
     got = flat(over_space(depth))
     (plane,) = call(lambda *r: plane_kernel(False, *r), [plane_shape], got, X_DOWN)
     (mine,) = call(land_kernel, [((2, M // 2, CO), F32)], mine, flops=5000000000)
     other = partner(mine)
     got = over_dp(plane)
     mixed, coeff = call(
-        mix_kernel, [plane_shape, ((2 * M, CO), F32)],
+        mix_kernel, [plane_shape, ((2 * M, CY), F32)],
         got, mine, other, Y_DOWN, Y_UP, ROW_COS, ROW_SIN, GROW_IN, SUM_OUT,
     )
     got = over_dp(mixed)
@@ -405,31 +455,33 @@
     wide = ((planes, CY, N), BF16)
     activated, grad, depth = call(
         gelu_kernel, [wide, wide, depth_shape],
-        got, field, cot, forth, bias, Z_UP, Z_DOWN, BLOCK,
+        got, field, cot, mix_weight, bias_term.reshape(1, C), OWN, OWN_T, Z_UP, Z_DOWN, BLOCK,
     )
     got = flat(over_space(depth))
     (plane,) = call(lambda *r: plane_kernel(True, *r), [plane_shape], got, X_DOWN)
     got = over_dp(plane)
-    half = ((2, M // 2, CO), F32)
-    mixed, keep, send = call(
-        back_kernel, [plane_shape, half, half],
-        got, mine, other, coeff, Y_DOWN, Y_UP, ROW_COS, ROW_SIN, GROW_OUT, SUM_IN,
-    )
-    grad_spectral = cross(keep + partner(send))
+    mixed, cot_coeff = call(
+        back_kernel, [plane_shape, ((2 * M, CY), F32)],
+        got, mine, other, Y_DOWN, Y_UP, ROW_COS, ROW_SIN, GROW_OUT, SUM_IN,
+    )
+    half = ((M, N), F32)
+    (packed,) = call(pack_kernel, [((2, M, N), F32)], coeff, cot_coeff, PACK)
+    keep, send = call(part_kernel, [half, half], cross(packed), flops=5_000_000_000)
+    other = partner(send)
     got = over_dp(mixed)
     (spread,) = call(lambda *r: spread_kernel(True, *r), [space_shape], got, X_UP_A, X_UP_B)
     got = over_space(spread).reshape(M, S, 2 * PLANES, CY)
     grad_input, grad_mix, grad_bias = call(
-        input_kernel, [wide, ((C, C), F32), ((8, C), F32)],
-        got, grad, back, Z_UP, OWN,
-    )
-    (grad_weight,) = call(return_kernel, [((M // 2, 2, 1, CO), F32)], grad_spectral, flops=20_000_000_000)
+        input_kernel, [wide, ((C, C), F32), ((1, C), F32)],
+        got, grad, mix_weight, Z_UP, OWN, OWN_T,
+    )
+    (grad_weight,) = call(outer_kernel, [((M // 2, 2, 1, CO), F32)], keep, other, PAIR_IN, PAIR_OUT)
     return (
         activated.reshape(features.shape),
         grad_input.reshape(features.shape),
         grad_weight,
         grad_mix,
-        grad_bias[0],
+        grad_bias.reshape(C),
     )
 
 

time: 153 us -> 147 us (0.961)
  blocking collectives: 42.3 us -> 57.5 us
  starting transfers between devices: 52.3 us -> 41.4 us
  local copies, waits for them, and re-layouts: 7.04 us -> 0.73 us
  waiting for transfers between devices: 38.5 us -> 33.6 us
    all_to_all x3 -> x4, blocking collectives: 42.3 us -> 57.5 us  [swap(): return lax.all_to_all(value, axis, 0, 0, tiled=True)]
    all_to_all x5 -> x4, starting transfers between devices: 44.8 us -> 35.2 us  [swap(): return lax.all_to_all(value, axis, 0, 0, tiled=True)]
    unnamed x64 -> x48, local copies, waits for them, and re-layouts: 5.84 us -> 0.73 us
    all_to_all x5 -> x4, waiting for transfers between devices: 36.7 us -> 31.8 us  [swap(): return lax.all_to_all(value, axis, 0, 0, tiled=True)]
    pallas_call x12 -> x13, Pallas kernels: 11 us -> 11.6 us  [call(): pl.pallas_call(kernel, out_shape=shapes, in_specs=[far if i in far_in els...]
  transfers between devices with their start and end apart: 9 -> 8, of which waited for: 7 -> 6; matrix products, arithmetic and copies ran while one was open for 0% -> 0% of each run, Pallas kernels for 2% -> 2%
where the time goes in v3:
time: 147 us; the launch traced here: 146 us
  blocking collectives  57.5 us (39%)
  starting transfers between devices  41.4 us (28%)
  waiting for transfers between devices  33.6 us (23%)
  Pallas kernels  11.6 us (8%)
    all_to_all x4, blocking collectives, swap(): return lax.all_to_all(value, axis, 0, 0, tiled=True)  57.5 us
    all_to_all x4, starting transfers between devices, swap(): return lax.all_to_all(value, axis, 0, 0, tiled=True)  35.2 us
    all_to_all x4, waiting for transfers between devices, swap(): return lax.all_to_all(value, axis, 0, 0, tiled=True)  31.8 us
    pallas_call x13, Pallas kernels, call(): pl.pallas_call(kernel, out_shape=shapes, in_specs=[far if i in far_in els...  11.6 us
    ppermute x2, starting transfers between devices, on_device(): partner = lambda v: lax.ppermute(v, 'space', pairing)  4.83 us
  transfers between devices with their start and end apart: 8, of which 6 were waited for; matrix products, arithmetic and copies ran while one was open for 0% of the time, Pallas kernels for 2%

profile of v3, /device:TPU:1, one launch (start us, length us, event | category | flops | bytes accessed | tf_op | source)
XLA Modules:
  0.0 145.9 jit_solution(7085079611883600015)
XLA Ops:
  0.6 2.3 %shard_map.263 = f32[16,2,8,256]{3,2,1,0:T(8,128)} custom-call(bf16[8,256,128]{2,1,0:T(8,128)(2,1)} %bitcast.27, bf16[128,512]{1,0:T(8,128)(2,1)} %constant.38.clone.table_hbm.down_ref), custom_call_target="tpu_custom_call" | custom-call | flops 50000000 | bytes 917504 | tf_op jit(solution)/shard_map/pallas_call | solution.py:396
  3.0 0.0 copy-start.2
  3.0 0.0 copy-start.23
  3.0 10.5 %all-to-all-start = ((f32[32,8,256]{2,1,0:T(8,128)}), f32[32,8,256]{2,1,0:T(8,128)S(1)}, u32[]{:S(2)}, u32[]{:S(2)}) async-start(f32[32,8,256]{2,1,0:T(8,128)} %bitcast.43), calls=%async_computation | async-start | bytes 524288 | tf_op jit(solution)/shard_map/all_to_all | solution.py:408
  13.5 0.0 copy-done.23
  13.6 0.7 collective-permute-start
  14.2 8.3 %all-to-all-done = f32[32,8,256]{2,1,0:T(8,128)S(1)} async-done(((f32[32,8,256]{2,1,0:T(8,128)}), f32[32,8,256]{2,1,0:T(8,128)S(1)}, u32[]{:S(2)}, u32[]{:S(2)}) %all-to-all-start) | async-done | bytes 262176 | tf_op jit(solution)/shard_map/all_to_all | solution.py:408
  22.5 0.0 copy-done.2
  22.6 0.9 shard_map.264
  23.4 13.0 %all-to-all-start.1 = ((f32[16,8,128]{2,1,0:T(8,128)}), f32[16,8,128]{2,1,0:T(8,128)S(1)}, u32[]{:S(2)}, u32[]{:S(2)}) async-start(f32[16,8,128]{2,1,0:T(8,128)} %bitcast.3), calls=%async_computation.1 | async-start | bytes 131072 | tf_op jit(solution)/shard_map/all_to_all | solution.py:408
  36.4 0.0 copy-start.9
  36.5 0.0 copy-start.10
  36.5 0.0 copy-start.12
  36.5 0.0 copy-start.14
  36.5 0.0 copy-start.17
  36.5 0.0 copy-start.18
  36.5 0.0 collective-permute-done.moved_ref
  36.5 2.6 %collective-permute-start.1 = (f32[2,8,1024]{2,1,0:T(8,128)S(1)}, f32[2,8,1024]{2,1,0:T(8,128)S(1)}, u32[]{:S(2)}, u32[]{:S(2)}) collective-permute-start(f32[2,8,1024]{2,1,0:T(8,128)S(1)} %shard_map.265.mine_ref), channel_id=1, source_target_pairs={{0,16},{16,0},{32,48},{48,32},{64,80},{80,64},{96,112},{112,96},{1... | collective-permute-start | bytes 196616 | tf_op jit(solution)/shard_map/ppermute | solution.py:423
  39.1 0.9 collective-permute-done.1.other_ref
  40.0 8.1 %all-to-all-done.1 = f32[16,8,128]{2,1,0:T(8,128)S(1)} async-done(((f32[16,8,128]{2,1,0:T(8,128)}), f32[16,8,128]{2,1,0:T(8,128)S(1)}, u32[]{:S(2)}, u32[]{:S(2)}) %all-to-all-start.1) | async-done | bytes 65568 | tf_op jit(solution)/shard_map/all_to_all | solution.py:408
  48.0 0.0 copy-done.9
  48.0 0.0 copy-done.10
  48.0 0.0 copy-done.12
  48.0 0.0 copy-done.14
  48.1 0.0 copy-done.17
  48.1 0.0 copy-done.18
  48.1 0.0 copy-start.3
  48.1 0.0 copy-start.4
  48.1 0.0 copy-start.5
  48.1 0.0 copy-start.16
  48.1 0.0 copy-start.21
  48.1 0.7 shard_map.266
  48.9 15.3 %all_to_all.40 = f32[16,8,128]{2,1,0:T(8,128)S(1)} all-to-all(f32[16,8,128]{2,1,0:T(8,128)S(1)} %bitcast.41), channel_id=1, replica_groups=mesh['space'=32,'dp'=16] {'dp'}, dimensions={0} | all-to-all | bytes 131072 | tf_op jit(solution)/shard_map/all_to_all | solution.py:408
  64.2 0.0 copy-done.3
  64.2 0.0 copy-done.4
  64.2 0.0 copy-start.15
  64.2 0.3 shard_map.267
  64.5 0.0 copy-start.1
  64.5 0.0 copy-start.6
  64.5 15.4 %all_to_all.41 = f32[32,8,256]{2,1,0:T(8,128)S(1)} all-to-all(f32[32,8,256]{2,1,0:T(8,128)S(1)} %bitcast.33), channel_id=1, replica_groups=mesh['space'=32,'dp'=16] {'space'}, dimensions={0} | all-to-all | bytes 524288 | tf_op jit(solution)/shard_map/all_to_all | solution.py:408
  79.9 0.0 copy-done.5
  79.9 0.0 copy-done.16
  80.0 0.6 copy-done.22
  80.6 2.1 %shard_map.268 = (bf16[8,256,128]{2,1,0:T(8,128)(2,1)}, bf16[8,256,128]{2,1,0:T(8,128)(2,1)S(1)}, f32[16,2,8,256]{3,2,1,0:T(8,128)S(1)}) custom-call(f32[16,2,8,256]{3,2,1,0:T(8,128)S(1)} %bitcast.30, bf16[8,256,128]{2,1,0:T(8,128)(2,1)S(1)} %bitcast.28, bf16[8,256,128]{2,1,0:T(8,128)(2,1)S(1)} %bitcast.34, bf16[32,32]{1,0:T(8,128)(2,1)S(1)} %copy-done.21, ...), custom_call_target="tpu_custom_call" | custom-call | flops 50000000 | bytes 3311744 | tf_op jit(solution)/shard_map/pallas_call | solution.py:396
  82.6 12.6 %all_to_all.42 = f32[32,8,256]{2,1,0:T(8,128)S(1)} all-to-all(f32[32,8,256]{2,1,0:T(8,128)S(1)} %bitcast.37), channel_id=1, replica_groups=mesh['space'=32,'dp'=16] {'space'}, dimensions={0} | all-to-all | bytes 524288 | tf_op jit(solution)/shard_map/all_to_all | solution.py:408
  95.2 0.3 shard_map.269
  95.5 14.2 %all_to_all.43 = f32[16,8,128]{2,1,0:T(8,128)S(1)} all-to-all(f32[16,8,128]{2,1,0:T(8,128)S(1)} %bitcast.39), channel_id=1, replica_groups=mesh['space'=32,'dp'=16] {'dp'}, dimensions={0} | all-to-all | bytes 131072 | tf_op jit(solution)/shard_map/all_to_all | solution.py:408
  109.8 0.0 copy-done.8
  109.8 1.4 shard_map.270
  111.1 3.8 %all-to-all-start.6 = ((f32[16,8,128]{2,1,0:T(8,128)}), f32[16,8,128]{2,1,0:T(8,128)S(1)}, u32[]{:S(2)}, u32[]{:S(2)}) async-start(f32[16,8,128]{2,1,0:T(8,128)} %bitcast.18), calls=%async_computation.6 | async-start | bytes 131072 | tf_op jit(solution)/shard_map/all_to_all | solution.py:408
  115.0 0.2 shard_map.273
  115.1 0.7 collective-permute-start.2
  115.8 10.7 %all-to-all-done.6 = f32[16,8,128]{2,1,0:T(8,128)S(1)} async-done(((f32[16,8,128]{2,1,0:T(8,128)}), f32[16,8,128]{2,1,0:T(8,128)S(1)}, u32[]{:S(2)}, u32[]{:S(2)}) %all-to-all-start.6) | async-done | bytes 65568 | tf_op jit(solution)/shard_map/all_to_all | solution.py:408
  126.5 1.0 shard_map.271
  127.5 7.8 %all-to-all-start.7 = ((f32[32,8,256]{2,1,0:T(8,128)}), f32[32,8,256]{2,1,0:T(8,128)S(1)}, u32[]{:S(2)}, u32[]{:S(2)}) async-start(f32[32,8,256]{2,1,0:T(8,128)} %bitcast.20), calls=%async_computation.7 | async-start | bytes 524288 | tf_op jit(solution)/shard_map/all_to_all | solution.py:408
  135.3 0.0 copy-start.19
  135.3 0.0 copy-start.20
  135.3 0.0 collective-permute-done.2.moved_ref
  135.4 2.3 %collective-permute-start.3 = (f32[16,128]{1,0:T(8,128)S(1)}, f32[16,128]{1,0:T(8,128)S(1)}, u32[]{:S(2)}, u32[]{:S(2)}) collective-permute-start(f32[16,128]{1,0:T(8,128)S(1)} %get-tuple-element.26), channel_id=1, source_target_pairs={{0,16},{16,0},{32,48},{48,32},{64,80},{80,64},{96,112},{112,96},{1... | collective-permute-start | bytes 24584 | tf_op jit(solution)/shard_map/ppermute | solution.py:423
  137.6 0.9 collective-permute-done.3.other_ref
  138.6 0.0 copy-done.20
  138.6 0.9 shard_map.275
  139.5 4.7 %all-to-all-done.7 = f32[32,8,256]{2,1,0:T(8,128)S(1)} async-done(((f32[32,8,256]{2,1,0:T(8,128)}), f32[32,8,256]{2,1,0:T(8,128)S(1)}, u32[]{:S(2)}, u32[]{:S(2)}) %all-to-all-start.7) | async-done | bytes 262176 | tf_op jit(solution)/shard_map/all_to_all | solution.py:408
  144.2 1.7 %shard_map.272 = (bf16[8,256,128]{2,1,0:T(8,128)(2,1)}, f32[32,32]{1,0:T(8,128)}, f32[1,32]{1,0:T(1,128)}) custom-call(f32[16,2,8,256]{3,2,1,0:T(8,128)S(1)} %bitcast.29, bf16[8,256,128]{2,1,0:T(8,128)(2,1)S(1)} %get-tuple-element.21.grad_ref, bf16[32,32]{1,0:T(8,128)(2,1)S(1)} %copy-done.21, bf16[384,512]{1,0:T(8,128)(2,1)S(1)} %copy-done.1, ...), custom_call_target="tpu_custom_call" | custom-call | flops 50000000 | bytes 1742976 | tf_op jit(solution)/shard_map/pallas_call | solution.py:396
  (18 shorter events, 0.0 us)
Async XLA Ops:
  3.0 19.6 %copy-start.2 = (bf16[128,1536]{1,0:T(8,128)(2,1)S(1)}, bf16[128,1536]{1,0:T(8,128)(2,1)}, u32[]{:S(2)}) copy-start(bf16[128,1536]{1,0:T(8,128)(2,1)} %constant.39.clone.r_1_) | copy-start | bytes 1179652
  3.0 10.6 %copy-start.23 = (bf16[8,2,1,1024]{3,1,2,0:T(2,128)(2,1)S(1)}, bf16[8,2,1,1024]{3,1,2,0:T(2,128)(2,1)}, u32[]{:S(2)}) copy-start(bf16[8,2,1,1024]{3,1,2,0:T(2,128)(2,1)} %param.26) | copy-start | bytes 98308
  3.0 19.6 %all-to-all-start = ((f32[32,8,256]{2,1,0:T(8,128)}), f32[32,8,256]{2,1,0:T(8,128)S(1)}, u32[]{:S(2)}, u32[]{:S(2)}) async-start(f32[32,8,256]{2,1,0:T(8,128)} %bitcast.43), calls=%async_computation | async-start | bytes 524288 | tf_op jit(solution)/shard_map/all_to_all | solution.py:408
  13.6 23.0 %collective-permute-start = (f32[2,8,1024]{2,1,0:T(8,128)S(1)}, f32[2,8,1024]{2,1,0:T(8,128)S(1)}, u32[]{:S(2)}, u32[]{:S(2)}) collective-permute-start(f32[2,8,1024]{2,1,0:T(8,128)S(1)} %convert_bitcast_fusion), channel_id=1, source_target_pairs={{0,0},{1,32},{2,64},{3,96},{4,128},{5,160},{6,192},{7,224},{8,256}... | collective-permute-start | bytes 196616 | tf_op jit(solution)/shard_map/ppermute | solution.py:422
  23.4 24.6 %all-to-all-start.1 = ((f32[16,8,128]{2,1,0:T(8,128)}), f32[16,8,128]{2,1,0:T(8,128)S(1)}, u32[]{:S(2)}, u32[]{:S(2)}) async-start(f32[16,8,128]{2,1,0:T(8,128)} %bitcast.3), calls=%async_computation.1 | async-start | bytes 131072 | tf_op jit(solution)/shard_map/all_to_all | solution.py:408
  36.4 11.6 %copy-start.9 = (bf16[1024,256]{1,0:T(8,128)(2,1)S(1)}, bf16[1024,256]{1,0:T(8,128)(2,1)}, u32[]{:S(2)}) copy-start(bf16[1024,256]{1,0:T(8,128)(2,1)} %constant.45.clone.sum_ref) | copy-start | bytes 1572868
  36.5 11.6 %copy-start.10 = (bf16[256,1024]{1,0:T(8,128)(2,1)S(1)}, bf16[256,1024]{1,0:T(8,128)(2,1)}, u32[]{:S(2)}) copy-start(bf16[256,1024]{1,0:T(8,128)(2,1)} %constant.44.clone.grow_ref) | copy-start | bytes 1572868
  36.5 11.6 %copy-start.12 = (bf16[128,192]{1,0:T(8,128)(2,1)S(1)}, bf16[128,192]{1,0:T(8,128)(2,1)}, u32[]{:S(2)}) copy-start(bf16[128,192]{1,0:T(8,128)(2,1)} %constant.41.clone.up_ref) | copy-start | bytes 147460
  36.5 11.6 %copy-start.14 = (bf16[64,384]{1,0:T(8,128)(2,1)S(1)}, bf16[64,384]{1,0:T(8,128)(2,1)}, u32[]{:S(2)}) copy-start(bf16[64,384]{1,0:T(8,128)(2,1)} %constant.40.clone.down_ref) | copy-start | bytes 147460
  36.5 11.6 %copy-start.17 = (f32[16,256]{1,0:T(8,128)S(1)}, f32[16,256]{1,0:T(8,128)}, u32[]{:S(2)}) copy-start(f32[16,256]{1,0:T(8,128)} %constant.43.clone.sin_ref) | copy-start | bytes 49156
  36.5 11.6 %copy-start.18 = (f32[16,256]{1,0:T(8,128)S(1)}, f32[16,256]{1,0:T(8,128)}, u32[]{:S(2)}) copy-start(f32[16,256]{1,0:T(8,128)} %constant.42.clone.cos_ref) | copy-start | bytes 49156
  36.5 3.4 %collective-permute-start.1 = (f32[2,8,1024]{2,1,0:T(8,128)S(1)}, f32[2,8,1024]{2,1,0:T(8,128)S(1)}, u32[]{:S(2)}, u32[]{:S(2)}) collective-permute-start(f32[2,8,1024]{2,1,0:T(8,128)S(1)} %shard_map.265.mine_ref), channel_id=1, source_target_pairs={{0,16},{16,0},{32,48},{48,32},{64,80},{80,64},{96,112},{112,96},{1... | collective-permute-start | bytes 196616 | tf_op jit(solution)/shard_map/ppermute | solution.py:423
  48.1 16.1 %copy-start.3 = (bf16[256,384]{1,0:T(8,128)(2,1)S(1)}, bf16[256,384]{1,0:T(8,128)(2,1)}, u32[]{:S(2)}) copy-start(bf16[256,384]{1,0:T(8,128)(2,1)} %constant.47.clone.r_2_) | copy-start | bytes 589828
  48.1 16.1 %copy-start.4 = (bf16[256,384]{1,0:T(8,128)(2,1)S(1)}, bf16[256,384]{1,0:T(8,128)(2,1)}, u32[]{:S(2)}) copy-start(bf16[256,384]{1,0:T(8,128)(2,1)} %constant.46.clone.r_1_) | copy-start | bytes 589828
  48.1 31.8 %copy-start.5 = (bf16[2,4,32,8,128]{4,3,2,1,0:T(8,128)(2,1)S(1)}, bf16[2,4,32,8,128]{4,3,2,1,0:T(8,128)(2,1)}, u32[]{:S(2)}) copy-start(bf16[2,4,32,8,128]{4,3,2,1,0:T(8,128)(2,1)} %param.25) | copy-start | bytes 1572868
  48.1 31.8 %copy-start.16 = (bf16[32,256]{1,0:T(8,128)(2,1)S(1)}, bf16[32,256]{1,0:T(8,128)(2,1)}, u32[]{:S(2)}) copy-start(bf16[32,256]{1,0:T(8,128)(2,1)} %constant.49.clone.own_t_ref) | copy-start | bytes 49156
  48.1 31.8 %copy-start.21 = (bf16[32,32]{1,0:T(8,128)(2,1)S(1)}, bf16[32,32]{1,0:T(8,128)(2,1)}, u32[]{:S(2)}) copy-start(bf16[32,32]{1,0:T(8,128)(2,1)} %mix_in_ref.1) | copy-start | bytes 6148
  64.2 15.7 %copy-start = (bf16[2,4,32,8,128]{4,3,2,1,0:T(8,128)(2,1)S(1)}, bf16[2,4,32,8,128]{4,3,2,1,0:T(8,128)(2,1)}, u32[]{:S(2)}) copy-start(bf16[2,4,32,8,128]{4,3,2,1,0:T(8,128)(2,1)} %param.24) | copy-start | bytes 1572868
  64.2 15.7 %copy-start.11 = (bf16[256,32]{1,0:T(8,128)(2,1)S(1)}, bf16[256,32]{1,0:T(8,128)(2,1)}, u32[]{:S(2)}) copy-start(bf16[256,32]{1,0:T(8,128)(2,1)} %constant.48.clone.own_ref) | copy-start | bytes 49156
  64.2 15.7 %copy-start.15 = (bf16[256,256]{1,0:T(8,128)(2,1)S(1)}, bf16[256,256]{1,0:T(8,128)(2,1)}, u32[]{:S(2)}) copy-start(bf16[256,256]{1,0:T(8,128)(2,1)} %constant.51.clone.block_ref) | copy-start | bytes 393220
  64.5 15.5 %copy-start.1 = (bf16[384,512]{1,0:T(8,128)(2,1)S(1)}, bf16[384,512]{1,0:T(8,128)(2,1)}, u32[]{:S(2)}) copy-start(bf16[384,512]{1,0:T(8,128)(2,1)} %constant.50.clone.up_ref) | copy-start | bytes 1179652
  64.5 15.5 %copy-start.6 = (bf16[128,512]{1,0:T(8,128)(2,1)S(1)}, bf16[128,512]{1,0:T(8,128)(2,1)}, u32[]{:S(2)}) copy-start(bf16[128,512]{1,0:T(8,128)(2,1)} %constant.38.clone.table_hbm.down_ref) | copy-start | bytes 393220
  79.9 0.7 copy-start.22
  82.6 27.1 %copy-start.8 = (bf16[256,1024]{1,0:T(8,128)(2,1)S(1)}, bf16[256,1024]{1,0:T(8,128)(2,1)}, u32[]{:S(2)}) copy-start(bf16[256,1024]{1,0:T(8,128)(2,1)} %constant.52.clone.grow_ref) | copy-start | bytes 1572868
  95.2 14.5 %copy-start.7 = (bf16[1024,256]{1,0:T(8,128)(2,1)S(1)}, bf16[1024,256]{1,0:T(8,128)(2,1)}, u32[]{:S(2)}) copy-start(bf16[1024,256]{1,0:T(8,128)(2,1)} %constant.53.clone.sum_ref) | copy-start | bytes 1572868
  109.8 5.2 %copy-start.13 = (bf16[512,256]{1,0:T(8,128)(2,1)S(1)}, bf16[512,256]{1,0:T(8,128)(2,1)}, u32[]{:S(2)}) copy-start(bf16[512,256]{1,0:T(8,128)(2,1)} %constant.54.clone.pack_ref) | copy-start | bytes 786436
  111.1 15.4 %all-to-all-start.6 = ((f32[16,8,128]{2,1,0:T(8,128)}), f32[16,8,128]{2,1,0:T(8,128)S(1)}, u32[]{:S(2)}, u32[]{:S(2)}) async-start(f32[16,8,128]{2,1,0:T(8,128)} %bitcast.18), calls=%async_computation.6 | async-start | bytes 131072 | tf_op jit(solution)/shard_map/all_to_all | solution.py:408
  115.1 20.2 %collective-permute-start.2 = (f32[2,16,128]{2,1,0:T(8,128)S(1)}, f32[2,16,128]{2,1,0:T(8,128)S(1)}, u32[]{:S(2)}, u32[]{:S(2)}) collective-permute-start(f32[2,16,128]{2,1,0:T(8,128)S(1)} %shard_map.273), channel_id=1, source_target_pairs={{0,0},{1,32},{2,64},{3,96},{4,128},{5,160},{6,192},{7,224},{8,256}... | collective-permute-start | bytes 49160 | tf_op jit(solution)/shard_map/ppermute | solution.py:422
  127.5 16.7 %all-to-all-start.7 = ((f32[32,8,256]{2,1,0:T(8,128)}), f32[32,8,256]{2,1,0:T(8,128)S(1)}, u32[]{:S(2)}, u32[]{:S(2)}) async-start(f32[32,8,256]{2,1,0:T(8,128)} %bitcast.20), calls=%async_computation.7 | async-start | bytes 524288 | tf_op jit(solution)/shard_map/all_to_all | solution.py:408
  135.3 3.2 %copy-start.19 = (bf16[32,1024]{1,0:T(8,128)(2,1)S(1)}, bf16[32,1024]{1,0:T(8,128)(2,1)}, u32[]{:S(2)}) copy-start(bf16[32,1024]{1,0:T(8,128)(2,1)} %constant.56.clone.grow_out_ref) | copy-start | bytes 196612
  135.3 3.2 %copy-start.20 = (bf16[32,1024]{1,0:T(8,128)(2,1)S(1)}, bf16[32,1024]{1,0:T(8,128)(2,1)}, u32[]{:S(2)}) copy-start(bf16[32,1024]{1,0:T(8,128)(2,1)} %constant.55.clone.grow_in_ref) | copy-start | bytes 196612
  135.4 3.2 %collective-permute-start.3 = (f32[16,128]{1,0:T(8,128)S(1)}, f32[16,128]{1,0:T(8,128)S(1)}, u32[]{:S(2)}, u32[]{:S(2)}) collective-permute-start(f32[16,128]{1,0:T(8,128)S(1)} %get-tuple-element.26), channel_id=1, source_target_pairs={{0,16},{16,0},{32,48},{48,32},{64,80},{80,64},{96,112},{112,96},{1... | collective-permute-start | bytes 24584 | tf_op jit(solution)/shard_map/ppermute | solution.py:423

commit v4 on v3

--- a/solution.py
+++ b/solution.py
@@ -132,6 +132,29 @@
 OWN_T = np.ascontiguousarray(OWN.T)
 
 
+SIDE = 4
+
+
+def plane_steps():
+    hops = lambda d, n: min(d, n - d)
+    steps = [(y, x) for y in range(SIDE) for x in range(SIDE)]
+    steps.sort(key=lambda s: -(hops(s[0], SIDE) + hops(s[1], SIDE)))
+    places = sorted(range(GROUPS), key=lambda e: hops(e, GROUPS))
+    out = [None] * GROUPS
+    for place, step in zip(places, steps):
+        out[place] = step
+    return out
+
+
+PLANE_STEPS = plane_steps()
+
+
+def placed(kz, e):
+    dy, dx = PLANE_STEPS[e]
+    kx = (kz // SIDE + dy) % SIDE * SIDE + (kz % SIDE + dx) % SIDE
+    return kx, (kz + e) % GROUPS
+
+
 def dot(a, b):
     return jnp.dot(a, b, preferred_element_type=F32)
 
@@ -187,13 +210,8 @@
     return out
 
 
-def depth_kernel(field_hbm, table_hbm, out_ref, field_ref, table_ref, sems):
-    table_copy = pltpu.make_async_copy(table_hbm, table_ref, sems.at[S])
-    copies = sample_copies(field_hbm, field_ref, sems, 0)
-    for copy in [table_copy] + copies:
-        copy.start()
-    table_copy.wait()
-    analyse_depth(lambda s, x: field_ref[s * PLANES + x], table_ref[...], out_ref, copies)
+def depth_kernel(field_ref, table_ref, out_ref):
+    analyse_depth(lambda s, x: field_ref[s * PLANES + x], table_ref[...], out_ref)
 
 
 def same_row(rows):
@@ -205,12 +223,16 @@
 
 
 def bias_column(bias_ref):
-    bias = jnp.broadcast_to(bias_ref[...], (CY, C))
+    bias = jnp.broadcast_to(bias_ref[0:1], (CY, C))
     picked = jnp.where(lane_ids((CY, C)) == row_ids((CY, C)) // ROWS, bias, 0.0)
     return jnp.sum(picked, 1, keepdims=True)
 
 
-def plane_kernel(with_sums, got_ref, table_ref, out_ref):
+def block_at(i):
+    return pl.ds(pl.multiple_of(i * 8, 8), 8)
+
+
+def plane_kernel(with_sums, got_ref, table_ref, out_ref, held_ref):
     got = got_ref[...]
     data = got
     if with_sums:
@@ -231,7 +253,11 @@
             )
         pair = jnp.concatenate(pair, 0)
         out = (out.reshape(GROUPS // 2, 16, half) + pair[None]).reshape(GROUPS * 8, half)
-    out_ref[...] = out
+    held_ref[...] = out
+    kz = lax.axis_index("space") // 2
+    for e in range(GROUPS):
+        kx, place = placed(kz, e)
+        out_ref[block_at(place), :] = held_ref[block_at(kx), :]
 
 
 def row_spectrum(got_ref, table_ref, cos_ref, sin_ref):
@@ -302,8 +328,12 @@
     send_ref[...] = moved_ref[1]
 
 
-def spread_kernel(with_sums, got_ref, table_a_ref, table_b_ref, out_ref):
-    got = got_ref[...]
+def spread_kernel(with_sums, got_ref, table_a_ref, table_b_ref, out_ref, held_ref):
+    kz = lax.axis_index("space") // 2
+    for e in range(GROUPS):
+        kx, place = placed(kz, e)
+        held_ref[block_at(kx), :] = got_ref[block_at(place), :]
+    got = held_ref[...]
     stacked = stack3(got)
     out_a = dot(table_a_ref[...], stacked)
     out_b = dot(table_b_ref[...], stacked)
@@ -368,8 +398,9 @@
     bias_ref[...] = apply_exact(lead, own)[0:1] * (SCALE_ALL / SCALE_CELLS)
 
 
-def land_kernel(moved_ref, mine_ref):
+def land_kernel(moved_ref, bias_in_ref, mine_ref, bias_ref):
     mine_ref[...] = moved_ref[...]
+    bias_ref[...] = jnp.broadcast_to(bias_in_ref[...], (8, C))
 
 
 def outer_kernel(keep_ref, other_ref, grow_in_ref, grow_out_ref, weight_ref):
@@ -412,14 +443,16 @@
     planes = S * PLANES
     field = features.reshape(planes, CY, N)
     cot = cotangent.reshape(planes, CY, N)
-    crossing = [
-        ((2 * a + h) * GROUPS + b, (2 * b + h) * GROUPS + a)
-        for a in range(M)
-        for h in range(2)
-        for b in range(M)
-    ]
+    held = (pltpu.VMEM((GROUPS * 8, N), F32),)
+    crossing = []
+    for kz in range(M):
+        for e in range(GROUPS):
+            kx, place = placed(kz, e)
+            for h in range(2):
+                crossing.append(((2 * kx + h) * GROUPS + kz, (2 * kz + h) * GROUPS + place))
     pairing = [(i, i ^ 1) for i in range(SPACES)]
     cross = lambda v: lax.ppermute(v, ("space", "dp"), crossing)
+    cross_home = lambda v: lax.ppermute(v, ("space", "dp"), [(b, a) for a, b in crossing])
     partner = lambda v: lax.ppermute(v, "space", pairing)
 
     depth_shape = ((M, S, 2 * PLANES, CY), F32)
@@ -435,14 +468,13 @@
 
     planes_scratch = pltpu.VMEM((planes, CY, N), BF16)
     (depth,) = call(
-        depth_kernel, [depth_shape], field, Z_DOWN, far_in=(0, 1), room=60,
-        scratch=(planes_scratch, pltpu.VMEM(Z_DOWN.shape, BF16), pltpu.SemaphoreType.DMA((S + 1,))),
+        depth_kernel, [depth_shape], field, Z_DOWN, room=60,
     )
     weight = spectral_weight.reshape(M // 2, 2, CO).astype(F32).transpose(1, 0, 2)
     mine = cross(weight)
     got = flat(over_space(depth))
-    (plane,) = call(lambda *r: plane_kernel(False, *r), [plane_shape], got, X_DOWN)
-    (mine,) = call(land_kernel, [((2, M // 2, CO), F32)], mine, flops=5000000000)
+    (plane,) = call(lambda *r: plane_kernel(False, *r), [plane_shape], got, X_DOWN, scratch=held)
+    mine, bias = call(land_kernel, [((2, M // 2, CO), F32), ((8, C), F32)], mine, bias_term.reshape(1, C), flops=5000000000)
     other = partner(mine)
     got = over_dp(plane)
     mixed, coeff = call(
@@ -450,15 +482,15 @@
         got, mine, other, Y_DOWN, Y_UP, ROW_COS, ROW_SIN, GROW_IN, SUM_OUT,
     )
     got = over_dp(mixed)
-    (spread,) = call(lambda *r: spread_kernel(False, *r), [space_shape], got, X_UP_A, X_UP_B)
+    (spread,) = call(lambda *r: spread_kernel(False, *r), [space_shape], got, X_UP_A, X_UP_B, scratch=held)
     got = over_space(spread).reshape(M, S, 2 * PLANES, CY)
     wide = ((planes, CY, N), BF16)
     activated, grad, depth = call(
         gelu_kernel, [wide, wide, depth_shape],
-        got, field, cot, mix_weight, bias_term.reshape(1, C), OWN, OWN_T, Z_UP, Z_DOWN, BLOCK,
+        got, field, cot, mix_weight, bias, OWN, OWN_T, Z_UP, Z_DOWN, BLOCK,
     )
     got = flat(over_space(depth))
-    (plane,) = call(lambda *r: plane_kernel(True, *r), [plane_shape], got, X_DOWN)
+    (plane,) = call(lambda *r: plane_kernel(True, *r), [plane_shape], got, X_DOWN, scratch=held)
     got = over_dp(plane)
     mixed, cot_coeff = call(
         back_kernel, [plane_shape, ((2 * M, CY), F32)],
@@ -466,10 +498,10 @@
     )
     half = ((M, N), F32)
     (packed,) = call(pack_kernel, [((2, M, N), F32)], coeff, cot_coeff, PACK)
-    keep, send = call(part_kernel, [half, half], cross(packed), flops=5_000_000_000)
+    keep, send = call(part_kernel, [half, half], cross_home(packed), flops=5_000_000_000)
     other = partner(send)
     got = over_dp(mixed)
-    (spread,) = call(lambda *r: spread_kernel(True, *r), [space_shape], got, X_UP_A, X_UP_B)
+    (spread,) = call(lambda *r: spread_kernel(True, *r), [space_shape], got, X_UP_A, X_UP_B, scratch=held)
     got = over_space(spread).reshape(M, S, 2 * PLANES, CY)
     grad_input, grad_mix, grad_bias = call(
         input_kernel, [wide, ((C, C), F32), ((1, C), F32)],

time: 147 us -> 144 us (0.980)
  waiting for transfers between devices: 33.6 us -> 22 us
  starting transfers between devices: 41.4 us -> 51.3 us
    ppermute x2 -> x1, starting transfers between devices: 1.34 us -> 13.6 us  [on_device(): cross = lambda v: lax.ppermute(v, ('space', 'dp'), crossing)]
    all_to_all x4, waiting for transfers between devices: 31.8 us -> 20.3 us  [swap(): return lax.all_to_all(value, axis, 0, 0, tiled=True)]
    all_to_all x4, starting transfers between devices: 35.2 us -> 29.4 us  [swap(): return lax.all_to_all(value, axis, 0, 0, tiled=True)]
    ppermute x0 -> x1, starting transfers between devices: none -> 3.32 us  [on_device(): lax.ppermute(v, ('space', 'dp'), [(b, a) for a, b in crossing])]
  transfers between devices with their start and end apart: 8 -> 8, of which waited for: 6 -> 5; matrix products, arithmetic and copies ran while one was open for 0% -> 0% of each run, Pallas kernels for 2% -> 2%
where the time goes in v4:
time: 144 us
  blocking collectives  57 us (40%)
  starting transfers between devices  51.3 us (36%)
  waiting for transfers between devices  22 us (15%)
  Pallas kernels  11.6 us (8%)
    all_to_all x4, blocking collectives, swap(): return lax.all_to_all(value, axis, 0, 0, tiled=True)  57 us
    all_to_all x4, starting transfers between devices, swap(): return lax.all_to_all(value, axis, 0, 0, tiled=True)  29.4 us
    all_to_all x4, waiting for transfers between devices, swap(): return lax.all_to_all(value, axis, 0, 0, tiled=True)  20.3 us
    ppermute x1, starting transfers between devices, on_device(): cross = lambda v: lax.ppermute(v, ('space', 'dp'), crossing)  13.6 us
    pallas_call x13, Pallas kernels, call(): pl.pallas_call(kernel, out_shape=shapes, in_specs=[far if i in far_in els...  11.6 us
    ppermute x2, starting transfers between devices, on_device(): partner = lambda v: lax.ppermute(v, 'space', pairing)  4.94 us
    ppermute x1, starting transfers between devices, on_device(): lax.ppermute(v, ('space', 'dp'), [(b, a) for a, b in crossing])  3.32 us
  transfers between devices with their start and end apart: 8, of which 5 were waited for; matrix products, arithmetic and copies ran while one was open for 0% of the time, Pallas kernels for 2%

profile of v4, /device:TPU:1, one launch (start us, length us, event | category | flops | bytes accessed | tf_op | source)
XLA Modules:
  0.0 143.6 jit_solution(9090422542819304905)
XLA Ops:
  0.6 2.1 %shard_map.263 = f32[16,2,8,256]{3,2,1,0:T(8,128)} custom-call(bf16[8,256,128]{2,1,0:T(8,128)(2,1)} %bitcast.27, bf16[128,512]{1,0:T(8,128)(2,1)} %constant.38.clone.table_ref.down_ref), custom_call_target="tpu_custom_call" | custom-call | flops 50000000 | bytes 917504 | tf_op jit(solution)/shard_map/pallas_call | solution.py:427
  2.7 10.5 %all-to-all-start = ((f32[32,8,256]{2,1,0:T(8,128)}), f32[32,8,256]{2,1,0:T(8,128)S(1)}, u32[]{:S(2)}, u32[]{:S(2)}) async-start(f32[32,8,256]{2,1,0:T(8,128)} %bitcast.43), calls=%async_computation | async-start | bytes 524288 | tf_op jit(solution)/shard_map/all_to_all | solution.py:439
  13.2 0.0 copy-done.23
  13.3 13.6 %collective-permute-start = (f32[2,8,1024]{2,1,0:T(8,128)S(1)}, f32[2,8,1024]{2,1,0:T(8,128)S(1)}, u32[]{:S(2)}, u32[]{:S(2)}) collective-permute-start(f32[2,8,1024]{2,1,0:T(8,128)S(1)} %convert_bitcast_fusion), channel_id=1, source_target_pairs={{320,0},{336,16},{192,1},{208,17},{352,2},{368,18},{64,3},{80,19},... | collective-permute-start | bytes 196616 | tf_op jit(solution)/shard_map/ppermute | solution.py:454
  26.9 0.0 all-to-all-done
  26.9 0.0 copy-done.2
  26.9 0.9 shard_map.264
  27.9 8.3 %all-to-all-start.1 = ((f32[16,8,128]{2,1,0:T(8,128)}), f32[16,8,128]{2,1,0:T(8,128)S(1)}, u32[]{:S(2)}, u32[]{:S(2)}) async-start(f32[16,8,128]{2,1,0:T(8,128)} %bitcast.3), calls=%async_computation.1 | async-start | bytes 131072 | tf_op jit(solution)/shard_map/all_to_all | solution.py:439
  36.2 0.0 copy-start.22
  36.2 0.0 collective-permute-done.moved_ref
  36.2 0.6 copy-done.22
  36.8 0.0 copy-start.17
  36.9 0.0 copy-start.18
  36.9 2.6 %collective-permute-start.1 = (f32[2,8,1024]{2,1,0:T(8,128)S(1)}, f32[2,8,1024]{2,1,0:T(8,128)S(1)}, u32[]{:S(2)}, u32[]{:S(2)}) collective-permute-start(f32[2,8,1024]{2,1,0:T(8,128)S(1)} %get-tuple-element.19.mine_ref), channel_id=1, source_target_pairs={{0,16},{16,0},{32,48},{48,32},{64,80},{80,64},{96,112},{112,96},{1... | collective-permute-start | bytes 196616 | tf_op jit(solution)/shard_map/ppermute | solution.py:456
  39.5 0.9 collective-permute-done.1.other_ref
  40.3 7.4 %all-to-all-done.1 = f32[16,8,128]{2,1,0:T(8,128)S(1)} async-done(((f32[16,8,128]{2,1,0:T(8,128)}), f32[16,8,128]{2,1,0:T(8,128)S(1)}, u32[]{:S(2)}, u32[]{:S(2)}) %all-to-all-start.1) | async-done | bytes 65568 | tf_op jit(solution)/shard_map/all_to_all | solution.py:439
  47.8 0.0 copy-done.8
  47.8 0.0 copy-done.9
  47.8 0.0 copy-done.12
  47.8 0.0 copy-done.14
  47.8 0.0 copy-done.17
  47.8 0.0 copy-done.18
  47.8 0.0 copy-start.3
  47.8 0.0 copy-start.4
  47.8 0.0 copy-start.10
  47.9 0.0 copy-start.16
  47.9 0.0 copy-start.21
  47.9 0.7 shard_map.266
  48.6 15.7 %all_to_all.40 = f32[16,8,128]{2,1,0:T(8,128)S(1)} all-to-all(f32[16,8,128]{2,1,0:T(8,128)S(1)} %bitcast.41), channel_id=1, replica_groups=mesh['space'=32,'dp'=16] {'dp'}, dimensions={0} | all-to-all | bytes 131072 | tf_op jit(solution)/shard_map/all_to_all | solution.py:439
  64.3 0.0 copy-done.3
  64.3 0.0 copy-done.4
  64.3 0.0 copy-start.15
  64.3 0.4 shard_map.267
  64.7 0.0 copy-start.1
  64.7 0.0 copy-start.5
  64.7 14.5 %all_to_all.41 = f32[32,8,256]{2,1,0:T(8,128)S(1)} all-to-all(f32[32,8,256]{2,1,0:T(8,128)S(1)} %bitcast.32), channel_id=1, replica_groups=mesh['space'=32,'dp'=16] {'space'}, dimensions={0} | all-to-all | bytes 524288 | tf_op jit(solution)/shard_map/all_to_all | solution.py:439
  79.2 0.0 copy-done.10
  79.2 0.0 copy-done.16
  79.2 0.0 copy-done.21
  79.2 0.0 copy-done
  79.2 0.0 copy-done.11
  79.2 0.0 copy-done.15
  79.2 2.1 %shard_map.268 = (bf16[8,256,128]{2,1,0:T(8,128)(2,1)}, bf16[8,256,128]{2,1,0:T(8,128)(2,1)S(1)}, f32[16,2,8,256]{3,2,1,0:T(8,128)S(1)}) custom-call(f32[16,2,8,256]{3,2,1,0:T(8,128)S(1)} %bitcast.33, bf16[8,256,128]{2,1,0:T(8,128)(2,1)S(1)} %bitcast.28, bf16[8,256,128]{2,1,0:T(8,128)(2,1)S(1)} %bitcast.34, bf16[32,32]{1,0:T(8,128)(2,1)S(1)} %copy-done.21, ...), custom_call_target="tpu_custom_call" | custom-call | flops 50000000 | bytes 3312640 | tf_op jit(solution)/shard_map/pallas_call | solution.py:427
  81.3 12.6 %all_to_all.42 = f32[32,8,256]{2,1,0:T(8,128)S(1)} all-to-all(f32[32,8,256]{2,1,0:T(8,128)S(1)} %bitcast.37), channel_id=1, replica_groups=mesh['space'=32,'dp'=16] {'space'}, dimensions={0} | all-to-all | bytes 524288 | tf_op jit(solution)/shard_map/all_to_all | solution.py:439
  93.9 0.3 shard_map.269
  94.2 14.3 %all_to_all.43 = f32[16,8,128]{2,1,0:T(8,128)S(1)} all-to-all(f32[16,8,128]{2,1,0:T(8,128)S(1)} %bitcast.39), channel_id=1, replica_groups=mesh['space'=32,'dp'=16] {'dp'}, dimensions={0} | all-to-all | bytes 131072 | tf_op jit(solution)/shard_map/all_to_all | solution.py:439
  108.5 0.0 copy-done.6
  108.5 1.4 shard_map.270
  109.8 3.8 %all-to-all-start.6 = ((f32[16,8,128]{2,1,0:T(8,128)}), f32[16,8,128]{2,1,0:T(8,128)S(1)}, u32[]{:S(2)}, u32[]{:S(2)}) async-start(f32[16,8,128]{2,1,0:T(8,128)} %bitcast.18), calls=%async_computation.6 | async-start | bytes 131072 | tf_op jit(solution)/shard_map/all_to_all | solution.py:439
  113.6 0.0 copy-done.13
  113.6 0.2 shard_map.273
  113.8 3.3 %collective-permute-start.2 = (f32[2,16,128]{2,1,0:T(8,128)S(1)}, f32[2,16,128]{2,1,0:T(8,128)S(1)}, u32[]{:S(2)}, u32[]{:S(2)}) collective-permute-start(f32[2,16,128]{2,1,0:T(8,128)S(1)} %shard_map.273), channel_id=1, source_target_pairs={{0,320},{16,336},{1,192},{17,208},{2,352},{18,368},{3,64},{19,80},... | collective-permute-start | bytes 49160 | tf_op jit(solution)/shard_map/ppermute | solution.py:455
  117.1 8.1 %all-to-all-done.6 = f32[16,8,128]{2,1,0:T(8,128)S(1)} async-done(((f32[16,8,128]{2,1,0:T(8,128)}), f32[16,8,128]{2,1,0:T(8,128)S(1)}, u32[]{:S(2)}, u32[]{:S(2)}) %all-to-all-start.6) | async-done | bytes 65568 | tf_op jit(solution)/shard_map/all_to_all | solution.py:439
  125.2 1.0 shard_map.271
  126.2 6.7 %all-to-all-start.7 = ((f32[32,8,256]{2,1,0:T(8,128)}), f32[32,8,256]{2,1,0:T(8,128)S(1)}, u32[]{:S(2)}, u32[]{:S(2)}) async-start(f32[32,8,256]{2,1,0:T(8,128)} %bitcast.20), calls=%async_computation.7 | async-start | bytes 524288 | tf_op jit(solution)/shard_map/all_to_all | solution.py:439
  133.0 0.0 copy-start.19
  133.0 0.0 copy-start.20
  133.0 0.0 collective-permute-done.2.moved_ref
  133.0 2.4 %collective-permute-start.3 = (f32[16,128]{1,0:T(8,128)S(1)}, f32[16,128]{1,0:T(8,128)S(1)}, u32[]{:S(2)}, u32[]{:S(2)}) collective-permute-start(f32[16,128]{1,0:T(8,128)S(1)} %get-tuple-element.30), channel_id=1, source_target_pairs={{0,16},{16,0},{32,48},{48,32},{64,80},{80,64},{96,112},{112,96},{1... | collective-permute-start | bytes 24584 | tf_op jit(solution)/shard_map/ppermute | solution.py:456
  135.4 0.8 collective-permute-done.3.other_ref
  136.2 0.0 copy-done.19
  136.2 0.9 shard_map.275
  137.1 4.8 %all-to-all-done.7 = f32[32,8,256]{2,1,0:T(8,128)S(1)} async-done(((f32[32,8,256]{2,1,0:T(8,128)}), f32[32,8,256]{2,1,0:T(8,128)S(1)}, u32[]{:S(2)}, u32[]{:S(2)}) %all-to-all-start.7) | async-done | bytes 262176 | tf_op jit(solution)/shard_map/all_to_all | solution.py:439
  142.0 1.7 %shard_map.272 = (bf16[8,256,128]{2,1,0:T(8,128)(2,1)}, f32[32,32]{1,0:T(8,128)}, f32[1,32]{1,0:T(1,128)}) custom-call(f32[16,2,8,256]{3,2,1,0:T(8,128)S(1)} %bitcast.29, bf16[8,256,128]{2,1,0:T(8,128)(2,1)S(1)} %get-tuple-element.25.grad_ref, bf16[32,32]{1,0:T(8,128)(2,1)S(1)} %copy-done.21, bf16[384,512]{1,0:T(8,128)(2,1)S(1)} %copy-done.1, ...), custom_call_target="tpu_custom_call" | custom-call | flops 50000000 | bytes 1742976 | tf_op jit(solution)/shard_map/pallas_call | solution.py:427
  (18 shorter events, 0.0 us)
Async XLA Ops:
  2.7 24.2 %copy-start.2 = (bf16[128,1536]{1,0:T(8,128)(2,1)S(1)}, bf16[128,1536]{1,0:T(8,128)(2,1)}, u32[]{:S(2)}) copy-start(bf16[128,1536]{1,0:T(8,128)(2,1)} %constant.39.clone.r_1_) | copy-start | bytes 1179652
  2.7 10.5 %copy-start.23 = (bf16[8,2,1,1024]{3,1,2,0:T(2,128)(2,1)S(1)}, bf16[8,2,1,1024]{3,1,2,0:T(2,128)(2,1)}, u32[]{:S(2)}) copy-start(bf16[8,2,1,1024]{3,1,2,0:T(2,128)(2,1)} %param.26) | copy-start | bytes 98308
  2.7 24.2 %all-to-all-start = ((f32[32,8,256]{2,1,0:T(8,128)}), f32[32,8,256]{2,1,0:T(8,128)S(1)}, u32[]{:S(2)}, u32[]{:S(2)}) async-start(f32[32,8,256]{2,1,0:T(8,128)} %bitcast.43), calls=%async_computation | async-start | bytes 524288 | tf_op jit(solution)/shard_map/all_to_all | solution.py:439
  13.3 22.9 %collective-permute-start = (f32[2,8,1024]{2,1,0:T(8,128)S(1)}, f32[2,8,1024]{2,1,0:T(8,128)S(1)}, u32[]{:S(2)}, u32[]{:S(2)}) collective-permute-start(f32[2,8,1024]{2,1,0:T(8,128)S(1)} %convert_bitcast_fusion), channel_id=1, source_target_pairs={{320,0},{336,16},{192,1},{208,17},{352,2},{368,18},{64,3},{80,19},... | collective-permute-start | bytes 196616 | tf_op jit(solution)/shard_map/ppermute | solution.py:454
  27.9 19.9 %all-to-all-start.1 = ((f32[16,8,128]{2,1,0:T(8,128)}), f32[16,8,128]{2,1,0:T(8,128)S(1)}, u32[]{:S(2)}, u32[]{:S(2)}) async-start(f32[16,8,128]{2,1,0:T(8,128)} %bitcast.3), calls=%async_computation.1 | async-start | bytes 131072 | tf_op jit(solution)/shard_map/all_to_all | solution.py:439
  36.2 0.7 copy-start.22
  36.8 10.9 %copy-start.8 = (bf16[1024,256]{1,0:T(8,128)(2,1)S(1)}, bf16[1024,256]{1,0:T(8,128)(2,1)}, u32[]{:S(2)}) copy-start(bf16[1024,256]{1,0:T(8,128)(2,1)} %constant.45.clone.sum_ref) | copy-start | bytes 1572868
  36.8 10.9 %copy-start.9 = (bf16[256,1024]{1,0:T(8,128)(2,1)S(1)}, bf16[256,1024]{1,0:T(8,128)(2,1)}, u32[]{:S(2)}) copy-start(bf16[256,1024]{1,0:T(8,128)(2,1)} %constant.44.clone.grow_ref) | copy-start | bytes 1572868
  36.8 10.9 %copy-start.12 = (bf16[128,192]{1,0:T(8,128)(2,1)S(1)}, bf16[128,192]{1,0:T(8,128)(2,1)}, u32[]{:S(2)}) copy-start(bf16[128,192]{1,0:T(8,128)(2,1)} %constant.41.clone.up_ref) | copy-start | bytes 147460
  36.8 10.9 %copy-start.14 = (bf16[64,384]{1,0:T(8,128)(2,1)S(1)}, bf16[64,384]{1,0:T(8,128)(2,1)}, u32[]{:S(2)}) copy-start(bf16[64,384]{1,0:T(8,128)(2,1)} %constant.40.clone.down_ref) | copy-start | bytes 147460
  36.8 10.9 %copy-start.17 = (f32[16,256]{1,0:T(8,128)S(1)}, f32[16,256]{1,0:T(8,128)}, u32[]{:S(2)}) copy-start(f32[16,256]{1,0:T(8,128)} %constant.43.clone.sin_ref) | copy-start | bytes 49156
  36.9 10.9 %copy-start.18 = (f32[16,256]{1,0:T(8,128)S(1)}, f32[16,256]{1,0:T(8,128)}, u32[]{:S(2)}) copy-start(f32[16,256]{1,0:T(8,128)} %constant.42.clone.cos_ref) | copy-start | bytes 49156
  36.9 3.4 %collective-permute-start.1 = (f32[2,8,1024]{2,1,0:T(8,128)S(1)}, f32[2,8,1024]{2,1,0:T(8,128)S(1)}, u32[]{:S(2)}, u32[]{:S(2)}) collective-permute-start(f32[2,8,1024]{2,1,0:T(8,128)S(1)} %get-tuple-element.19.mine_ref), channel_id=1, source_target_pairs={{0,16},{16,0},{32,48},{48,32},{64,80},{80,64},{96,112},{112,96},{1... | collective-permute-start | bytes 196616 | tf_op jit(solution)/shard_map/ppermute | solution.py:456
  47.8 16.5 %copy-start.3 = (bf16[256,384]{1,0:T(8,128)(2,1)S(1)}, bf16[256,384]{1,0:T(8,128)(2,1)}, u32[]{:S(2)}) copy-start(bf16[256,384]{1,0:T(8,128)(2,1)} %constant.47.clone.r_2_) | copy-start | bytes 589828
  47.8 16.5 %copy-start.4 = (bf16[256,384]{1,0:T(8,128)(2,1)S(1)}, bf16[256,384]{1,0:T(8,128)(2,1)}, u32[]{:S(2)}) copy-start(bf16[256,384]{1,0:T(8,128)(2,1)} %constant.46.clone.r_1_) | copy-start | bytes 589828
  47.8 31.3 %copy-start.10 = (bf16[2,4,32,8,128]{4,3,2,1,0:T(8,128)(2,1)S(1)}, bf16[2,4,32,8,128]{4,3,2,1,0:T(8,128)(2,1)}, u32[]{:S(2)}) copy-start(bf16[2,4,32,8,128]{4,3,2,1,0:T(8,128)(2,1)} %param.25) | copy-start | bytes 1572868
  47.9 31.3 %copy-start.16 = (bf16[32,256]{1,0:T(8,128)(2,1)S(1)}, bf16[32,256]{1,0:T(8,128)(2,1)}, u32[]{:S(2)}) copy-start(bf16[32,256]{1,0:T(8,128)(2,1)} %constant.49.clone.own_t_ref) | copy-start | bytes 49156
  47.9 31.3 %copy-start.21 = (bf16[32,32]{1,0:T(8,128)(2,1)S(1)}, bf16[32,32]{1,0:T(8,128)(2,1)}, u32[]{:S(2)}) copy-start(bf16[32,32]{1,0:T(8,128)(2,1)} %mix_in_ref.1) | copy-start | bytes 6148
  64.3 14.9 %copy-start = (bf16[2,4,32,8,128]{4,3,2,1,0:T(8,128)(2,1)S(1)}, bf16[2,4,32,8,128]{4,3,2,1,0:T(8,128)(2,1)}, u32[]{:S(2)}) copy-start(bf16[2,4,32,8,128]{4,3,2,1,0:T(8,128)(2,1)} %param.24) | copy-start | bytes 1572868
  64.3 14.9 %copy-start.11 = (bf16[256,32]{1,0:T(8,128)(2,1)S(1)}, bf16[256,32]{1,0:T(8,128)(2,1)}, u32[]{:S(2)}) copy-start(bf16[256,32]{1,0:T(8,128)(2,1)} %constant.48.clone.own_ref) | copy-start | bytes 49156
  64.3 14.9 %copy-start.15 = (bf16[256,256]{1,0:T(8,128)(2,1)S(1)}, bf16[256,256]{1,0:T(8,128)(2,1)}, u32[]{:S(2)}) copy-start(bf16[256,256]{1,0:T(8,128)(2,1)} %constant.51.clone.block_ref) | copy-start | bytes 393220
  64.7 14.5 %copy-start.1 = (bf16[384,512]{1,0:T(8,128)(2,1)S(1)}, bf16[384,512]{1,0:T(8,128)(2,1)}, u32[]{:S(2)}) copy-start(bf16[384,512]{1,0:T(8,128)(2,1)} %constant.50.clone.up_ref) | copy-start | bytes 1179652
  64.7 14.5 %copy-start.5 = (bf16[128,512]{1,0:T(8,128)(2,1)S(1)}, bf16[128,512]{1,0:T(8,128)(2,1)}, u32[]{:S(2)}) copy-start(bf16[128,512]{1,0:T(8,128)(2,1)} %constant.38.clone.table_ref.down_ref) | copy-start | bytes 393220
  81.3 27.2 %copy-start.7 = (bf16[256,1024]{1,0:T(8,128)(2,1)S(1)}, bf16[256,1024]{1,0:T(8,128)(2,1)}, u32[]{:S(2)}) copy-start(bf16[256,1024]{1,0:T(8,128)(2,1)} %constant.52.clone.grow_ref) | copy-start | bytes 1572868
  93.9 14.6 %copy-start.6 = (bf16[1024,256]{1,0:T(8,128)(2,1)S(1)}, bf16[1024,256]{1,0:T(8,128)(2,1)}, u32[]{:S(2)}) copy-start(bf16[1024,256]{1,0:T(8,128)(2,1)} %constant.53.clone.sum_ref) | copy-start | bytes 1572868
  108.5 5.2 %copy-start.13 = (bf16[512,256]{1,0:T(8,128)(2,1)S(1)}, bf16[512,256]{1,0:T(8,128)(2,1)}, u32[]{:S(2)}) copy-start(bf16[512,256]{1,0:T(8,128)(2,1)} %constant.54.clone.pack_ref) | copy-start | bytes 786436
  109.8 15.4 %all-to-all-start.6 = ((f32[16,8,128]{2,1,0:T(8,128)}), f32[16,8,128]{2,1,0:T(8,128)S(1)}, u32[]{:S(2)}, u32[]{:S(2)}) async-start(f32[16,8,128]{2,1,0:T(8,128)} %bitcast.18), calls=%async_computation.6 | async-start | bytes 131072 | tf_op jit(solution)/shard_map/all_to_all | solution.py:439
  113.8 19.2 %collective-permute-start.2 = (f32[2,16,128]{2,1,0:T(8,128)S(1)}, f32[2,16,128]{2,1,0:T(8,128)S(1)}, u32[]{:S(2)}, u32[]{:S(2)}) collective-permute-start(f32[2,16,128]{2,1,0:T(8,128)S(1)} %shard_map.273), channel_id=1, source_target_pairs={{0,320},{16,336},{1,192},{17,208},{2,352},{18,368},{3,64},{19,80},... | collective-permute-start | bytes 49160 | tf_op jit(solution)/shard_map/ppermute | solution.py:455
  126.2 15.8 %all-to-all-start.7 = ((f32[32,8,256]{2,1,0:T(8,128)}), f32[32,8,256]{2,1,0:T(8,128)S(1)}, u32[]{:S(2)}, u32[]{:S(2)}) async-start(f32[32,8,256]{2,1,0:T(8,128)} %bitcast.20), calls=%async_computation.7 | async-start | bytes 524288 | tf_op jit(solution)/shard_map/all_to_all | solution.py:439
  133.0 3.3 %copy-start.19 = (bf16[32,1024]{1,0:T(8,128)(2,1)S(1)}, bf16[32,1024]{1,0:T(8,128)(2,1)}, u32[]{:S(2)}) copy-start(bf16[32,1024]{1,0:T(8,128)(2,1)} %constant.56.clone.grow_out_ref) | copy-start | bytes 196612
  133.0 3.2 %copy-start.20 = (bf16[32,1024]{1,0:T(8,128)(2,1)S(1)}, bf16[32,1024]{1,0:T(8,128)(2,1)}, u32[]{:S(2)}) copy-start(bf16[32,1024]{1,0:T(8,128)(2,1)} %constant.55.clone.grow_in_ref) | copy-start | bytes 196612
  133.0 3.2 %collective-permute-start.3 = (f32[16,128]{1,0:T(8,128)S(1)}, f32[16,128]{1,0:T(8,128)S(1)}, u32[]{:S(2)}, u32[]{:S(2)}) collective-permute-start(f32[16,128]{1,0:T(8,128)S(1)} %get-tuple-element.30), channel_id=1, source_target_pairs={{0,16},{16,0},{32,48},{48,32},{64,80},{80,64},{96,112},{112,96},{1... | collective-permute-start | bytes 24584 | tf_op jit(solution)/shard_map/ppermute | solution.py:456

commit v5 on v4

--- a/solution.py
+++ b/solution.py
@@ -130,6 +130,11 @@
 PAIR_IN = np.ascontiguousarray(GROW_IN[::ROWS])
 PAIR_OUT = np.ascontiguousarray(GROW_OUT[::ROWS])
 OWN_T = np.ascontiguousarray(OWN.T)
+X_DOWN_4 = X_DOWN.reshape(M, 8, -1)[:, :4].reshape(M * 4, -1)
+Y_DOWN_4 = Y_DOWN.reshape(-1, 3, GROUPS, 8)[..., :4].reshape(4 * M, -1)
+Y_UP_4 = Y_UP.reshape(GROUPS, 8, -1)[:, :4].reshape(GROUPS * 4, -1)
+X_UP_A_4 = X_UP_A.reshape(-1, 3, M, 8)[..., :4].reshape(SPACES * 8, -1)
+X_UP_B_4 = X_UP_B.reshape(-1, 3, M, 8)[..., :4].reshape(SPACES * 8, -1)
 
 
 SIDE = 4
@@ -228,8 +233,17 @@
     return jnp.sum(picked, 1, keepdims=True)
 
 
-def block_at(i):
-    return pl.ds(pl.multiple_of(i * 8, 8), 8)
+def put_blocks(value, blocks_ref):
+    rows = blocks_ref.shape[1]
+    for i in range(GROUPS):
+        blocks_ref[i] = value[i * rows : (i + 1) * rows]
+
+
+def take_blocks(blocks_ref, flat_ref):
+    rows = blocks_ref.shape[1]
+    for i in range(GROUPS):
+        flat_ref[i * rows : (i + 1) * rows, :] = blocks_ref[i]
+    return flat_ref[...]
 
 
 def plane_kernel(with_sums, got_ref, table_ref, out_ref, held_ref):
@@ -253,15 +267,15 @@
             )
         pair = jnp.concatenate(pair, 0)
         out = (out.reshape(GROUPS // 2, 16, half) + pair[None]).reshape(GROUPS * 8, half)
-    held_ref[...] = out
     kz = lax.axis_index("space") // 2
+    put_blocks(out, held_ref)
     for e in range(GROUPS):
         kx, place = placed(kz, e)
-        out_ref[block_at(place), :] = held_ref[block_at(kx), :]
-
-
-def row_spectrum(got_ref, table_ref, cos_ref, sin_ref):
-    flat = dot(table_ref[...], stack3(got_ref[...]))
+        out_ref[place] = held_ref[kx]
+
+
+def row_spectrum(got, table_ref, cos_ref, sin_ref):
+    flat = dot(table_ref[...], stack3(got))
     real = jnp.concatenate([flat[0:M], flat[2 * M : 3 * M]], 1)
     imag = jnp.concatenate([flat[M : 2 * M], flat[3 * M :]], 1)
     cosine, sine = cos_ref[...], sin_ref[...]
@@ -284,37 +298,36 @@
     return dot(table_ref[...], stacked)
 
 
-def mix_kernel(got_ref, mine_ref, other_ref, down_ref, up_ref, cos_ref, sin_ref, grow_ref, sum_ref, out_ref, spectrum_ref):
-    real, imag = row_spectrum(got_ref, down_ref, cos_ref, sin_ref)
+def mix_kernel(got_ref, mine_ref, other_ref, down_ref, up_ref, cos_ref, sin_ref, grow_ref, sum_ref, out_ref, spectrum_ref, flat_ref):
+    real, imag = row_spectrum(take_blocks(got_ref, flat_ref), down_ref, cos_ref, sin_ref)
     spectrum = jnp.concatenate([real, imag], 0)
     spectrum_ref[...] = spectrum
     coeff = apply_exact(spectrum, grow_ref[...])
     cr, ci = coeff[:M], coeff[M:]
     wr, wi = weight_rows(mine_ref, other_ref)
     mixed = apply_exact(jnp.concatenate([cr * wr - ci * wi, cr * wi + ci * wr], 0), sum_ref[...])
-    out_ref[...] = row_synth(mixed[:M], mixed[M:], up_ref, cos_ref, sin_ref)
-
-
-def back_kernel(got_ref, mine_ref, other_ref, down_ref, up_ref, cos_ref, sin_ref, grow_ref, sum_ref, out_ref, spectrum_ref):
-    real, imag = row_spectrum(got_ref, down_ref, cos_ref, sin_ref)
+    put_blocks(row_synth(mixed[:M], mixed[M:], up_ref, cos_ref, sin_ref), out_ref)
+
+
+def back_kernel(got_ref, mine_ref, other_ref, down_ref, up_ref, cos_ref, sin_ref, grow_ref, sum_ref, pack_ref, coeff_ref, out_ref, packed_ref):
+    real, imag = row_spectrum(got_ref[...].reshape(GROUPS * 8, N), down_ref, cos_ref, sin_ref)
     spectrum = jnp.concatenate([real, imag], 0)
-    spectrum_ref[...] = spectrum
+    pack(coeff_ref[...], spectrum, pack_ref[...], packed_ref)
     cot = apply_exact(spectrum, grow_ref[...])
     dr, di = cot[:M], cot[M:]
     wr, wi = weight_rows(mine_ref, other_ref)
     back = apply_exact(jnp.concatenate([dr * wr + di * wi, di * wr - dr * wi], 0), sum_ref[...])
     out = row_synth(back[:M], back[M:], up_ref, cos_ref, sin_ref)
-    total = jnp.sum(got_ref[...].reshape(GROUPS, 8, N), 0)
+    total = jnp.sum(got_ref[...], 0)
     rows = row_ids((8, N))
     extra = jnp.where((rows == 4) | (rows == 5), total, 0.0)
     extra = extra + jnp.where(rows == 6, real[0:1, :N], 0.0) + jnp.where(rows == 7, real[0:1, N:], 0.0)
-    out_ref[...] = (out.reshape(GROUPS, 8, N) + extra[None]).reshape(GROUPS * 8, N)
-
-
-def pack_kernel(coeff_ref, cot_ref, pack_ref, out_ref):
+    out_ref[...] = out.reshape(GROUPS, 8, N) + extra[None]
+
+
+def pack(coeff, cot, table, out_ref):
     even = lax.axis_index("space") % 2 == 0
-    both = jnp.concatenate([coeff_ref[...], cot_ref[...]], 1)
-    packed = apply_exact(both, pack_ref[...])
+    packed = apply_exact(jnp.concatenate([coeff, cot], 1), table)
     packed = jnp.where(even, packed[:, :N], packed[:, N:])
     half = M // 2
     low = jnp.concatenate([packed[:half], packed[M : M + half]], 0)
@@ -328,12 +341,12 @@
     send_ref[...] = moved_ref[1]
 
 
-def spread_kernel(with_sums, got_ref, table_a_ref, table_b_ref, out_ref, held_ref):
+def spread_kernel(with_sums, got_ref, table_a_ref, table_b_ref, out_ref, held_ref, flat_ref):
     kz = lax.axis_index("space") // 2
     for e in range(GROUPS):
         kx, place = placed(kz, e)
-        held_ref[block_at(kx), :] = got_ref[block_at(place), :]
-    got = held_ref[...]
+        held_ref[kx] = got_ref[place]
+    got = take_blocks(held_ref, flat_ref)
     stacked = stack3(got)
     out_a = dot(table_a_ref[...], stacked)
     out_b = dot(table_b_ref[...], stacked)
@@ -358,16 +371,20 @@
     moments = jnp.zeros((CY, CY), F32)
     for s in range(S):
         spectral = synth_depth(got_ref, s, up)
+        field = jnp.concatenate([field_ref[s * PLANES + x] for x in range(PLANES)], 1)
+        linear = dot(forth, field)
+        grads = []
         for x in range(PLANES):
             at = s * PLANES + x
-            field = field_ref[at]
-            preact = spectral[:, x * N : (x + 1) * N] + dot(forth, field) + bias
+            lanes = slice(x * N, (x + 1) * N)
+            preact = spectral[:, lanes] + linear[:, lanes] + bias
             normal_cdf = 0.5 * (1.0 + lax.erf(preact * ROOT_HALF))
             act_ref[at] = (preact * normal_cdf).astype(BF16)
             slope = normal_cdf + preact * jnp.exp(-0.5 * preact * preact) * INV_ROOT_TAU
             grad = (cot_ref[at].astype(F32) * slope).astype(BF16)
             grad_ref[at] = grad
-            moments = moments + dot_nt(field, grad)
+            grads.append(grad)
+        moments = moments + dot_nt(field, jnp.concatenate(grads, 1))
     analyse_depth(lambda s, x: grad_ref[s * PLANES + x], down_ref[...], out_ref)
     same = same_row(CY)
     moments = jnp.sum(jnp.where(same, moments, 0.0).reshape(C, ROWS, CY), 1)
@@ -383,9 +400,10 @@
     back = grow_mix(dot(own, mix_in_ref[...]), own_t_ref[...])
     for s in range(S):
         spectral = synth_depth(got_ref, s, up)
+        linear = dot(back, jnp.concatenate([grad_ref[s * PLANES + x] for x in range(PLANES)], 1))
+        total = (spectral + linear).astype(BF16)
         for x in range(PLANES):
-            at = s * PLANES + x
-            out_ref[at] = (spectral[:, x * N : (x + 1) * N] + dot(back, grad_ref[at])).astype(BF16)
+            out_ref[s * PLANES + x] = total[:, x * N : (x + 1) * N]
     rows = []
     for s in range(S):
         for x in range(2):
@@ -443,7 +461,8 @@
     planes = S * PLANES
     field = features.reshape(planes, CY, N)
     cot = cotangent.reshape(planes, CY, N)
-    held = (pltpu.VMEM((GROUPS * 8, N), F32),)
+    held = lambda rows: (pltpu.VMEM((GROUPS, rows, N), F32),)
+    line = lambda rows: (pltpu.VMEM((GROUPS * rows, N), F32),)
     crossing = []
     for kz in range(M):
         for e in range(GROUPS):
@@ -456,7 +475,7 @@
     partner = lambda v: lax.ppermute(v, "space", pairing)
 
     depth_shape = ((M, S, 2 * PLANES, CY), F32)
-    plane_shape = ((GROUPS * 8, N), F32)
+    short_shape, plane_shape = ((GROUPS, 4, N), F32), ((GROUPS, 8, N), F32)
     space_shape = ((SPACES * 2 * PLANES, CY), F32)
     flat = lambda v: v.reshape(SPACES * 2 * PLANES, CY)
 
@@ -464,7 +483,7 @@
         return swap(v.reshape(SPACES, 2 * PLANES, CY), "space")
 
     def over_dp(v):
-        return swap(v.reshape(GROUPS, 8, N), "dp").reshape(GROUPS * 8, N)
+        return swap(v, "dp")
 
     planes_scratch = pltpu.VMEM((planes, CY, N), BF16)
     (depth,) = call(
@@ -473,16 +492,16 @@
     weight = spectral_weight.reshape(M // 2, 2, CO).astype(F32).transpose(1, 0, 2)
     mine = cross(weight)
     got = flat(over_space(depth))
-    (plane,) = call(lambda *r: plane_kernel(False, *r), [plane_shape], got, X_DOWN, scratch=held)
+    (plane,) = call(lambda *r: plane_kernel(False, *r), [short_shape], got, X_DOWN_4, scratch=held(4))
     mine, bias = call(land_kernel, [((2, M // 2, CO), F32), ((8, C), F32)], mine, bias_term.reshape(1, C), flops=5000000000)
     other = partner(mine)
     got = over_dp(plane)
     mixed, coeff = call(
-        mix_kernel, [plane_shape, ((2 * M, CY), F32)],
-        got, mine, other, Y_DOWN, Y_UP, ROW_COS, ROW_SIN, GROW_IN, SUM_OUT,
+        mix_kernel, [short_shape, ((2 * M, CY), F32)],
+        got, mine, other, Y_DOWN_4, Y_UP_4, ROW_COS, ROW_SIN, GROW_IN, SUM_OUT, scratch=line(4),
     )
     got = over_dp(mixed)
-    (spread,) = call(lambda *r: spread_kernel(False, *r), [space_shape], got, X_UP_A, X_UP_B, scratch=held)
+    (spread,) = call(lambda *r: spread_kernel(False, *r), [space_shape], got, X_UP_A_4, X_UP_B_4, scratch=held(4) + line(4))
     got = over_space(spread).reshape(M, S, 2 * PLANES, CY)
     wide = ((planes, CY, N), BF16)
     activated, grad, depth = call(
@@ -490,18 +509,17 @@
         got, field, cot, mix_weight, bias, OWN, OWN_T, Z_UP, Z_DOWN, BLOCK,
     )
     got = flat(over_space(depth))
-    (plane,) = call(lambda *r: plane_kernel(True, *r), [plane_shape], got, X_DOWN, scratch=held)
+    (plane,) = call(lambda *r: plane_kernel(True, *r), [plane_shape], got, X_DOWN, scratch=held(8))
     got = over_dp(plane)
-    mixed, cot_coeff = call(
-        back_kernel, [plane_shape, ((2 * M, CY), F32)],
-        got, mine, other, Y_DOWN, Y_UP, ROW_COS, ROW_SIN, GROW_OUT, SUM_IN,
+    mixed, packed = call(
+        back_kernel, [plane_shape, ((2, M, N), F32)],
+        got, mine, other, Y_DOWN, Y_UP, ROW_COS, ROW_SIN, GROW_OUT, SUM_IN, PACK, coeff,
     )
     half = ((M, N), F32)
-    (packed,) = call(pack_kernel, [((2, M, N), F32)], coeff, cot_coeff, PACK)
     keep, send = call(part_kernel, [half, half], cross_home(packed), flops=5_000_000_000)
     other = partner(send)
     got = over_dp(mixed)
-    (spread,) = call(lambda *r: spread_kernel(True, *r), [space_shape], got, X_UP_A, X_UP_B, scratch=held)
+    (spread,) = call(lambda *r: spread_kernel(True, *r), [space_shape], got, X_UP_A, X_UP_B, scratch=held(8) + line(8))
     got = over_space(spread).reshape(M, S, 2 * PLANES, CY)
     grad_input, grad_mix, grad_bias = call(
         input_kernel, [wide, ((C, C), F32), ((1, C), F32)],

time: 144 us -> 143 us (level)
    pallas_call x13 -> x12, Pallas kernels: 11.6 us -> 10.9 us  [call(): pl.pallas_call(kernel, out_shape=shapes, in_specs=[far if i in far_in els...]
where the time goes in v5:
time: 143 us
  blocking collectives  56.6 us (40%)
  starting transfers between devices  51.1 us (36%)
  waiting for transfers between devices  22.1 us (15%)
  Pallas kernels  10.9 us (8%)
    all_to_all x4, blocking collectives, swap(): return lax.all_to_all(value, axis, 0, 0, tiled=True)  56.6 us
    all_to_all x4, starting transfers between devices, swap(): return lax.all_to_all(value, axis, 0, 0, tiled=True)  29.2 us
    all_to_all x4, waiting for transfers between devices, swap(): return lax.all_to_all(value, axis, 0, 0, tiled=True)  20.4 us
    ppermute x1, starting transfers between devices, on_device(): cross = lambda v: lax.ppermute(v, ('space', 'dp'), crossing)  13.6 us
    pallas_call x12, Pallas kernels, call(): pl.pallas_call(kernel, out_shape=shapes, in_specs=[far if i in far_in els...  10.9 us
    ppermute x2, starting transfers between devices, on_device(): partner = lambda v: lax.ppermute(v, 'space', pairing)  4.94 us
    ppermute x1, starting transfers between devices, on_device(): lax.ppermute(v, ('space', 'dp'), [(b, a) for a, b in crossing])  3.34 us
  transfers between devices with their start and end apart: 8, of which 5 were waited for; matrix products, arithmetic and copies ran while one was open for 0% of the time, Pallas kernels for 2%

profile of v5, /device:TPU:1, one launch (start us, length us, event | category | flops | bytes accessed | tf_op | source)
XLA Modules:
  0.0 142.6 jit_solution(10182863416706223505)
XLA Ops:
  0.6 2.1 %shard_map.308 = f32[16,2,8,256]{3,2,1,0:T(8,128)} custom-call(bf16[8,256,128]{2,1,0:T(8,128)(2,1)} %bitcast.19, bf16[128,512]{1,0:T(8,128)(2,1)} %constant.48.clone.table_ref.down_ref), custom_call_target="tpu_custom_call" | custom-call | flops 50000000 | bytes 917504 | tf_op jit(solution)/shard_map/pallas_call | solution.py:445
  2.7 10.5 %all-to-all-start = ((f32[32,8,256]{2,1,0:T(8,128)}), f32[32,8,256]{2,1,0:T(8,128)S(1)}, u32[]{:S(2)}, u32[]{:S(2)}) async-start(f32[32,8,256]{2,1,0:T(8,128)} %bitcast.29), calls=%async_computation | async-start | bytes 524288 | tf_op jit(solution)/shard_map/all_to_all | solution.py:457
  13.2 0.0 copy-done.28
  13.3 13.6 %collective-permute-start = (f32[2,8,1024]{2,1,0:T(8,128)S(1)}, f32[2,8,1024]{2,1,0:T(8,128)S(1)}, u32[]{:S(2)}, u32[]{:S(2)}) collective-permute-start(f32[2,8,1024]{2,1,0:T(8,128)S(1)} %convert_bitcast_fusion), channel_id=1, source_target_pairs={{320,0},{336,16},{192,1},{208,17},{352,2},{368,18},{64,3},{80,19},... | collective-permute-start | bytes 196616 | tf_op jit(solution)/shard_map/ppermute | solution.py:473
  26.9 0.0 all-to-all-done
  26.9 0.0 copy-done.13
  26.9 0.8 shard_map.309
  27.8 8.3 %all-to-all-start.1 = ((f32[16,4,128]{2,1,0:T(4,128)}), f32[16,4,128]{2,1,0:T(4,128)S(1)}, u32[]{:S(2)}, u32[]{:S(2)}) async-start(f32[16,4,128]{2,1,0:T(4,128)} %shard_map.309), calls=%async_computation.1 | async-start | bytes 65536 | tf_op jit(solution)/shard_map/all_to_all | solution.py:457
  36.1 0.0 copy-start.27
  36.1 0.0 collective-permute-done.moved_ref
  36.1 0.6 copy-done.27
  36.8 0.0 copy-start.25
  36.8 0.0 copy-start.26
  36.8 2.6 %collective-permute-start.1 = (f32[2,8,1024]{2,1,0:T(8,128)S(1)}, f32[2,8,1024]{2,1,0:T(8,128)S(1)}, u32[]{:S(2)}, u32[]{:S(2)}) collective-permute-start(f32[2,8,1024]{2,1,0:T(8,128)S(1)} %get-tuple-element.19.mine_ref), channel_id=1, source_target_pairs={{0,16},{16,0},{32,48},{48,32},{64,80},{80,64},{96,112},{112,96},{1... | collective-permute-start | bytes 196616 | tf_op jit(solution)/shard_map/ppermute | solution.py:475
  39.4 0.9 collective-permute-done.1.other_ref
  40.3 7.3 %all-to-all-done.1.got_ref = f32[16,4,128]{2,1,0:T(4,128)S(1)} async-done(((f32[16,4,128]{2,1,0:T(4,128)}), f32[16,4,128]{2,1,0:T(4,128)S(1)}, u32[]{:S(2)}, u32[]{:S(2)}) %all-to-all-start.1) | async-done | bytes 32800 | tf_op jit(solution)/shard_map/all_to_all | solution.py:457
  47.6 0.0 copy-done.5
  47.6 0.0 copy-done.6
  47.6 0.0 copy-done.18
  47.6 0.0 copy-done.19
  47.6 0.0 copy-done.25
  47.6 0.0 copy-done.26
  47.6 0.0 copy-start.15
  47.7 0.0 copy-start.16
  47.7 0.0 copy-start.7
  47.7 0.0 copy-start.10
  47.7 0.0 copy-start.14
  47.7 0.7 shard_map.311
  48.4 15.7 %all_to_all.40.r_0_ = f32[16,4,128]{2,1,0:T(4,128)S(1)} all-to-all(f32[16,4,128]{2,1,0:T(4,128)S(1)} %get-tuple-element.20), channel_id=1, replica_groups=mesh['space'=32,'dp'=16] {'dp'}, dimensions={0} | all-to-all | bytes 65536 | tf_op jit(solution)/shard_map/all_to_all | solution.py:457
  64.1 0.0 copy-done.15
  64.1 0.0 copy-done.16
  64.1 0.0 copy-start.24
  64.1 0.3 shard_map.312
  64.4 0.0 copy-start.1
  64.5 0.0 copy-start.4
  64.5 14.1 %all_to_all.41 = f32[32,8,256]{2,1,0:T(8,128)S(1)} all-to-all(f32[32,8,256]{2,1,0:T(8,128)S(1)} %bitcast.22), channel_id=1, replica_groups=mesh['space'=32,'dp'=16] {'space'}, dimensions={0} | all-to-all | bytes 524288 | tf_op jit(solution)/shard_map/all_to_all | solution.py:457
  78.5 0.0 copy-done.7
  78.5 0.0 copy-done.10
  78.5 0.0 copy-done.14
  78.6 0.0 copy-start.8
  78.6 0.0 copy-start.23
  78.6 1.7 %shard_map.313 = (bf16[8,256,128]{2,1,0:T(8,128)(2,1)}, bf16[8,256,128]{2,1,0:T(8,128)(2,1)S(1)}, f32[16,2,8,256]{3,2,1,0:T(8,128)S(1)}) custom-call(f32[16,2,8,256]{3,2,1,0:T(8,128)S(1)} %bitcast.25, bf16[8,256,128]{2,1,0:T(8,128)(2,1)S(1)} %bitcast.20, bf16[8,256,128]{2,1,0:T(8,128)(2,1)S(1)} %bitcast.26, bf16[32,32]{1,0:T(8,128)(2,1)S(1)} %copy-done.24, ...), custom_call_target="tpu_custom_call" | custom-call | flops 50000000 | bytes 3312640 | tf_op jit(solution)/shard_map/pallas_call | solution.py:445
  80.4 12.6 %all_to_all.42 = f32[32,8,256]{2,1,0:T(8,128)S(1)} all-to-all(f32[32,8,256]{2,1,0:T(8,128)S(1)} %bitcast.27), channel_id=1, replica_groups=mesh['space'=32,'dp'=16] {'space'}, dimensions={0} | all-to-all | bytes 524288 | tf_op jit(solution)/shard_map/all_to_all | solution.py:457
  93.0 0.3 shard_map.314
  93.3 0.0 copy-start.20
  93.3 14.3 %all_to_all.43.got_ref = f32[16,8,128]{2,1,0:T(8,128)S(1)} all-to-all(f32[16,8,128]{2,1,0:T(8,128)S(1)} %shard_map.314), channel_id=1, replica_groups=mesh['space'=32,'dp'=16] {'dp'}, dimensions={0} | all-to-all | bytes 131072 | tf_op jit(solution)/shard_map/all_to_all | solution.py:457
  107.6 0.0 copy-start.11
  107.6 0.0 copy-start.12
  107.7 1.4 shard_map.315
  109.0 3.9 %all-to-all-start.6 = ((f32[16,8,128]{2,1,0:T(8,128)}), f32[16,8,128]{2,1,0:T(8,128)S(1)}, u32[]{:S(2)}, u32[]{:S(2)}) async-start(f32[16,8,128]{2,1,0:T(8,128)} %get-tuple-element.25), calls=%async_computation.6 | async-start | bytes 131072 | tf_op jit(solution)/shard_map/all_to_all | solution.py:457
  112.9 3.3 %collective-permute-start.2 = (f32[2,16,128]{2,1,0:T(8,128)S(1)}, f32[2,16,128]{2,1,0:T(8,128)S(1)}, u32[]{:S(2)}, u32[]{:S(2)}) collective-permute-start(f32[2,16,128]{2,1,0:T(8,128)S(1)} %get-tuple-element.28), channel_id=1, source_target_pairs={{0,320},{16,336},{1,192},{17,208},{2,352},{18,368},{3,64},{19,80},... | collective-permute-start | bytes 49160 | tf_op jit(solution)/shard_map/ppermute | solution.py:474
  116.2 8.3 %all-to-all-done.6.r_0_ = f32[16,8,128]{2,1,0:T(8,128)S(1)} async-done(((f32[16,8,128]{2,1,0:T(8,128)}), f32[16,8,128]{2,1,0:T(8,128)S(1)}, u32[]{:S(2)}, u32[]{:S(2)}) %all-to-all-start.6) | async-done | bytes 65568 | tf_op jit(solution)/shard_map/all_to_all | solution.py:457
  124.5 0.0 copy-done.11
  124.5 1.0 shard_map.316
  125.6 6.5 %all-to-all-start.7 = ((f32[32,8,256]{2,1,0:T(8,128)}), f32[32,8,256]{2,1,0:T(8,128)S(1)}, u32[]{:S(2)}, u32[]{:S(2)}) async-start(f32[32,8,256]{2,1,0:T(8,128)} %bitcast.12), calls=%async_computation.7 | async-start | bytes 524288 | tf_op jit(solution)/shard_map/all_to_all | solution.py:457
  132.0 0.0 copy-start.21
  132.1 0.0 copy-start.22
  132.1 0.0 collective-permute-done.2.moved_ref
  132.1 2.4 %collective-permute-start.3 = (f32[16,128]{1,0:T(8,128)S(1)}, f32[16,128]{1,0:T(8,128)S(1)}, u32[]{:S(2)}, u32[]{:S(2)}) collective-permute-start(f32[16,128]{1,0:T(8,128)S(1)} %get-tuple-element.30), channel_id=1, source_target_pairs={{0,16},{16,0},{32,48},{48,32},{64,80},{80,64},{96,112},{112,96},{1... | collective-permute-start | bytes 24584 | tf_op jit(solution)/shard_map/ppermute | solution.py:475
  134.5 0.8 collective-permute-done.3.other_ref
  135.3 0.0 copy-done.22
  135.3 0.9 shard_map.319
  136.2 4.8 %all-to-all-done.7 = f32[32,8,256]{2,1,0:T(8,128)S(1)} async-done(((f32[32,8,256]{2,1,0:T(8,128)}), f32[32,8,256]{2,1,0:T(8,128)S(1)}, u32[]{:S(2)}, u32[]{:S(2)}) %all-to-all-start.7) | async-done | bytes 262176 | tf_op jit(solution)/shard_map/all_to_all | solution.py:457
  141.1 1.6 %shard_map.317 = (bf16[8,256,128]{2,1,0:T(8,128)(2,1)}, f32[32,32]{1,0:T(8,128)}, f32[1,32]{1,0:T(1,128)}) custom-call(f32[16,2,8,256]{3,2,1,0:T(8,128)S(1)} %bitcast.21, bf16[8,256,128]{2,1,0:T(8,128)(2,1)S(1)} %get-tuple-element.26.grad_ref, bf16[32,32]{1,0:T(8,128)(2,1)S(1)} %copy-done.24, bf16[384,512]{1,0:T(8,128)(2,1)S(1)} %copy-done.1, ...), custom_call_target="tpu_custom_call" | custom-call | flops 50000000 | bytes 1742976 | tf_op jit(solution)/shard_map/pallas_call | solution.py:445
  (27 shorter events, 0.1 us)
Async XLA Ops:
  2.7 10.5 %copy-start.28 = (bf16[8,2,1,1024]{3,1,2,0:T(2,128)(2,1)S(1)}, bf16[8,2,1,1024]{3,1,2,0:T(2,128)(2,1)}, u32[]{:S(2)}) copy-start(bf16[8,2,1,1024]{3,1,2,0:T(2,128)(2,1)} %param.31) | copy-start | bytes 98308
  2.7 24.2 %copy-start.13 = (bf16[64,1536]{1,0:T(8,128)(2,1)S(1)}, bf16[64,1536]{1,0:T(8,128)(2,1)}, u32[]{:S(2)}) copy-start(bf16[64,1536]{1,0:T(8,128)(2,1)} %constant.49.clone.r_1_) | copy-start | bytes 589828
  2.7 24.2 %all-to-all-start = ((f32[32,8,256]{2,1,0:T(8,128)}), f32[32,8,256]{2,1,0:T(8,128)S(1)}, u32[]{:S(2)}, u32[]{:S(2)}) async-start(f32[32,8,256]{2,1,0:T(8,128)} %bitcast.29), calls=%async_computation | async-start | bytes 524288 | tf_op jit(solution)/shard_map/all_to_all | solution.py:457
  13.3 22.8 %collective-permute-start = (f32[2,8,1024]{2,1,0:T(8,128)S(1)}, f32[2,8,1024]{2,1,0:T(8,128)S(1)}, u32[]{:S(2)}, u32[]{:S(2)}) collective-permute-start(f32[2,8,1024]{2,1,0:T(8,128)S(1)} %convert_bitcast_fusion), channel_id=1, source_target_pairs={{320,0},{336,16},{192,1},{208,17},{352,2},{368,18},{64,3},{80,19},... | collective-permute-start | bytes 196616 | tf_op jit(solution)/shard_map/ppermute | solution.py:473
  27.8 19.8 %all-to-all-start.1 = ((f32[16,4,128]{2,1,0:T(4,128)}), f32[16,4,128]{2,1,0:T(4,128)S(1)}, u32[]{:S(2)}, u32[]{:S(2)}) async-start(f32[16,4,128]{2,1,0:T(4,128)} %shard_map.309), calls=%async_computation.1 | async-start | bytes 65536 | tf_op jit(solution)/shard_map/all_to_all | solution.py:457
  36.1 0.7 copy-start.27
  36.8 10.8 %copy-start.5 = (bf16[256,1024]{1,0:T(8,128)(2,1)S(1)}, bf16[256,1024]{1,0:T(8,128)(2,1)}, u32[]{:S(2)}) copy-start(bf16[256,1024]{1,0:T(8,128)(2,1)} %constant.54.clone.grow_ref) | copy-start | bytes 1572868
  36.8 10.8 %copy-start.6 = (bf16[1024,256]{1,0:T(8,128)(2,1)S(1)}, bf16[1024,256]{1,0:T(8,128)(2,1)}, u32[]{:S(2)}) copy-start(bf16[1024,256]{1,0:T(8,128)(2,1)} %constant.55.clone.sum_ref) | copy-start | bytes 1572868
  36.8 10.8 %copy-start.18 = (f32[16,256]{1,0:T(8,128)S(1)}, f32[16,256]{1,0:T(8,128)}, u32[]{:S(2)}) copy-start(f32[16,256]{1,0:T(8,128)} %constant.52.clone.cos_ref) | copy-start | bytes 49156
  36.8 10.8 %copy-start.19 = (f32[16,256]{1,0:T(8,128)S(1)}, f32[16,256]{1,0:T(8,128)}, u32[]{:S(2)}) copy-start(f32[16,256]{1,0:T(8,128)} %constant.53.clone.sin_ref) | copy-start | bytes 49156
  36.8 10.8 %copy-start.25 = (bf16[64,192]{1,0:T(8,128)(2,1)S(1)}, bf16[64,192]{1,0:T(8,128)(2,1)}, u32[]{:S(2)}) copy-start(bf16[64,192]{1,0:T(8,128)(2,1)} %constant.50.clone.down_ref) | copy-start | bytes 73732
  36.8 10.8 %copy-start.26 = (bf16[64,192]{1,0:T(8,128)(2,1)S(1)}, bf16[64,192]{1,0:T(8,128)(2,1)}, u32[]{:S(2)}) copy-start(bf16[64,192]{1,0:T(8,128)(2,1)} %constant.51.clone.up_ref) | copy-start | bytes 73732
  36.8 3.4 %collective-permute-start.1 = (f32[2,8,1024]{2,1,0:T(8,128)S(1)}, f32[2,8,1024]{2,1,0:T(8,128)S(1)}, u32[]{:S(2)}, u32[]{:S(2)}) collective-permute-start(f32[2,8,1024]{2,1,0:T(8,128)S(1)} %get-tuple-element.19.mine_ref), channel_id=1, source_target_pairs={{0,16},{16,0},{32,48},{48,32},{64,80},{80,64},{96,112},{112,96},{1... | collective-permute-start | bytes 196616 | tf_op jit(solution)/shard_map/ppermute | solution.py:475
  47.6 16.4 %copy-start.15 = (bf16[256,192]{1,0:T(8,128)(2,1)S(1)}, bf16[256,192]{1,0:T(8,128)(2,1)}, u32[]{:S(2)}) copy-start(bf16[256,192]{1,0:T(8,128)(2,1)} %constant.56.clone.r_1_) | copy-start | bytes 294916
  47.7 16.4 %copy-start.16 = (bf16[256,192]{1,0:T(8,128)(2,1)S(1)}, bf16[256,192]{1,0:T(8,128)(2,1)}, u32[]{:S(2)}) copy-start(bf16[256,192]{1,0:T(8,128)(2,1)} %constant.57.clone.r_2_) | copy-start | bytes 294916
  47.7 30.9 %copy-start.7 = (bf16[2,4,32,8,128]{4,3,2,1,0:T(8,128)(2,1)S(1)}, bf16[2,4,32,8,128]{4,3,2,1,0:T(8,128)(2,1)}, u32[]{:S(2)}) copy-start(bf16[2,4,32,8,128]{4,3,2,1,0:T(8,128)(2,1)} %param.30) | copy-start | bytes 1572868
  47.7 30.9 %copy-start.10 = (bf16[256,32]{1,0:T(8,128)(2,1)S(1)}, bf16[256,32]{1,0:T(8,128)(2,1)}, u32[]{:S(2)}) copy-start(bf16[256,32]{1,0:T(8,128)(2,1)} %constant.58.clone.own_ref) | copy-start | bytes 49156
  47.7 30.9 %copy-start.14 = (bf16[256,256]{1,0:T(8,128)(2,1)S(1)}, bf16[256,256]{1,0:T(8,128)(2,1)}, u32[]{:S(2)}) copy-start(bf16[256,256]{1,0:T(8,128)(2,1)} %constant.61.clone.block_ref) | copy-start | bytes 393220
  64.1 14.5 %copy-start = (bf16[2,4,32,8,128]{4,3,2,1,0:T(8,128)(2,1)S(1)}, bf16[2,4,32,8,128]{4,3,2,1,0:T(8,128)(2,1)}, u32[]{:S(2)}) copy-start(bf16[2,4,32,8,128]{4,3,2,1,0:T(8,128)(2,1)} %param.29) | copy-start | bytes 1572868
  64.1 14.5 %copy-start.17 = (bf16[32,256]{1,0:T(8,128)(2,1)S(1)}, bf16[32,256]{1,0:T(8,128)(2,1)}, u32[]{:S(2)}) copy-start(bf16[32,256]{1,0:T(8,128)(2,1)} %constant.59.clone.own_t_ref) | copy-start | bytes 49156
  64.1 14.5 %copy-start.24 = (bf16[32,32]{1,0:T(8,128)(2,1)S(1)}, bf16[32,32]{1,0:T(8,128)(2,1)}, u32[]{:S(2)}) copy-start(bf16[32,32]{1,0:T(8,128)(2,1)} %mix_in_ref.1) | copy-start | bytes 6148
  64.4 14.1 %copy-start.1 = (bf16[384,512]{1,0:T(8,128)(2,1)S(1)}, bf16[384,512]{1,0:T(8,128)(2,1)}, u32[]{:S(2)}) copy-start(bf16[384,512]{1,0:T(8,128)(2,1)} %constant.60.clone.up_ref) | copy-start | bytes 1179652
  64.5 14.1 %copy-start.4 = (bf16[128,512]{1,0:T(8,128)(2,1)S(1)}, bf16[128,512]{1,0:T(8,128)(2,1)}, u32[]{:S(2)}) copy-start(bf16[128,512]{1,0:T(8,128)(2,1)} %constant.48.clone.table_ref.down_ref) | copy-start | bytes 393220
  78.6 14.4 %copy-start.8 = (bf16[128,1536]{1,0:T(8,128)(2,1)S(1)}, bf16[128,1536]{1,0:T(8,128)(2,1)}, u32[]{:S(2)}) copy-start(bf16[128,1536]{1,0:T(8,128)(2,1)} %constant.62.clone.r_1_) | copy-start | bytes 1179652
  78.6 29.0 %copy-start.23 = (bf16[64,384]{1,0:T(8,128)(2,1)S(1)}, bf16[64,384]{1,0:T(8,128)(2,1)}, u32[]{:S(2)}) copy-start(bf16[64,384]{1,0:T(8,128)(2,1)} %constant.63.clone.down_ref) | copy-start | bytes 147460
  80.4 27.2 %copy-start.3 = (bf16[1024,256]{1,0:T(8,128)(2,1)S(1)}, bf16[1024,256]{1,0:T(8,128)(2,1)}, u32[]{:S(2)}) copy-start(bf16[1024,256]{1,0:T(8,128)(2,1)} %constant.66.clone.sum_ref) | copy-start | bytes 1572868
  93.0 14.7 %copy-start.2 = (bf16[256,1024]{1,0:T(8,128)(2,1)S(1)}, bf16[256,1024]{1,0:T(8,128)(2,1)}, u32[]{:S(2)}) copy-start(bf16[256,1024]{1,0:T(8,128)(2,1)} %constant.65.clone.grow_ref) | copy-start | bytes 1572868
  93.0 14.7 %copy-start.9 = (bf16[512,256]{1,0:T(8,128)(2,1)S(1)}, bf16[512,256]{1,0:T(8,128)(2,1)}, u32[]{:S(2)}) copy-start(bf16[512,256]{1,0:T(8,128)(2,1)} %constant.67.clone.pack_ref) | copy-start | bytes 786436
  93.3 14.3 %copy-start.20 = (bf16[128,192]{1,0:T(8,128)(2,1)S(1)}, bf16[128,192]{1,0:T(8,128)(2,1)}, u32[]{:S(2)}) copy-start(bf16[128,192]{1,0:T(8,128)(2,1)} %constant.64.clone.up_ref) | copy-start | bytes 147460
  107.6 16.9 %copy-start.11 = (bf16[256,384]{1,0:T(8,128)(2,1)S(1)}, bf16[256,384]{1,0:T(8,128)(2,1)}, u32[]{:S(2)}) copy-start(bf16[256,384]{1,0:T(8,128)(2,1)} %constant.68.clone.r_1_) | copy-start | bytes 589828
  107.6 16.9 %copy-start.12 = (bf16[256,384]{1,0:T(8,128)(2,1)S(1)}, bf16[256,384]{1,0:T(8,128)(2,1)}, u32[]{:S(2)}) copy-start(bf16[256,384]{1,0:T(8,128)(2,1)} %constant.69.clone.r_2_) | copy-start | bytes 589828
  109.0 15.5 %all-to-all-start.6 = ((f32[16,8,128]{2,1,0:T(8,128)}), f32[16,8,128]{2,1,0:T(8,128)S(1)}, u32[]{:S(2)}, u32[]{:S(2)}) async-start(f32[16,8,128]{2,1,0:T(8,128)} %get-tuple-element.25), calls=%async_computation.6 | async-start | bytes 131072 | tf_op jit(solution)/shard_map/all_to_all | solution.py:457
  112.9 19.2 %collective-permute-start.2 = (f32[2,16,128]{2,1,0:T(8,128)S(1)}, f32[2,16,128]{2,1,0:T(8,128)S(1)}, u32[]{:S(2)}, u32[]{:S(2)}) collective-permute-start(f32[2,16,128]{2,1,0:T(8,128)S(1)} %get-tuple-element.28), channel_id=1, source_target_pairs={{0,320},{16,336},{1,192},{17,208},{2,352},{18,368},{3,64},{19,80},... | collective-permute-start | bytes 49160 | tf_op jit(solution)/shard_map/ppermute | solution.py:474
  125.6 15.5 %all-to-all-start.7 = ((f32[32,8,256]{2,1,0:T(8,128)}), f32[32,8,256]{2,1,0:T(8,128)S(1)}, u32[]{:S(2)}, u32[]{:S(2)}) async-start(f32[32,8,256]{2,1,0:T(8,128)} %bitcast.12), calls=%async_computation.7 | async-start | bytes 524288 | tf_op jit(solution)/shard_map/all_to_all | solution.py:457
  132.0 3.3 %copy-start.21 = (bf16[32,1024]{1,0:T(8,128)(2,1)S(1)}, bf16[32,1024]{1,0:T(8,128)(2,1)}, u32[]{:S(2)}) copy-start(bf16[32,1024]{1,0:T(8,128)(2,1)} %constant.70.clone.grow_in_ref) | copy-start | bytes 196612
  132.1 3.2 %copy-start.22 = (bf16[32,1024]{1,0:T(8,128)(2,1)S(1)}, bf16[32,1024]{1,0:T(8,128)(2,1)}, u32[]{:S(2)}) copy-start(bf16[32,1024]{1,0:T(8,128)(2,1)} %constant.71.clone.grow_out_ref) | copy-start | bytes 196612
  132.1 3.2 %collective-permute-start.3 = (f32[16,128]{1,0:T(8,128)S(1)}, f32[16,128]{1,0:T(8,128)S(1)}, u32[]{:S(2)}, u32[]{:S(2)}) collective-permute-start(f32[16,128]{1,0:T(8,128)S(1)} %get-tuple-element.30), channel_id=1, source_target_pairs={{0,16},{16,0},{32,48},{48,32},{64,80},{80,64},{96,112},{112,96},{1... | collective-permute-start | bytes 24584 | tf_op jit(solution)/shard_map/ppermute | solution.py:475

commit v6 on v5

--- a/solution.py
+++ b/solution.py
@@ -395,13 +395,23 @@
         out_ref[0, s, PLANES : PLANES + 2, :] = moments[2 * s : 2 * s + 2]
 
 
-def input_kernel(got_ref, grad_ref, mix_in_ref, up_ref, own_ref, own_t_ref, out_ref, mix_ref, bias_ref):
+def store_kernel(held_ref, after_ref, out_ref):
+    del after_ref
+    out_ref[...] = held_ref[...]
+
+
+def linear_kernel(grad_ref, back_ref, after_ref, out_ref):
+    del after_ref
+    for s in range(S):
+        grad = jnp.concatenate([grad_ref[s * PLANES + x] for x in range(PLANES)], 1)
+        out_ref[s] = dot(back_ref[...], grad)
+
+
+def input_kernel(got_ref, linear_ref, up_ref, own_ref, out_ref, mix_ref, bias_ref):
     up, own = up_ref[...], own_ref[...]
-    back = grow_mix(dot(own, mix_in_ref[...]), own_t_ref[...])
     for s in range(S):
         spectral = synth_depth(got_ref, s, up)
-        linear = dot(back, jnp.concatenate([grad_ref[s * PLANES + x] for x in range(PLANES)], 1))
-        total = (spectral + linear).astype(BF16)
+        total = (spectral + linear_ref[s]).astype(BF16)
         for x in range(PLANES):
             out_ref[s * PLANES + x] = total[:, x * N : (x + 1) * N]
     rows = []
@@ -416,7 +426,8 @@
     bias_ref[...] = apply_exact(lead, own)[0:1] * (SCALE_ALL / SCALE_CELLS)
 
 
-def land_kernel(moved_ref, bias_in_ref, mine_ref, bias_ref):
+def land_kernel(moved_ref, bias_in_ref, mix_ref, own_ref, own_t_ref, mine_ref, bias_ref, back_ref):
+    back_ref[...] = grow_mix(dot(own_ref[...], mix_ref[...]), own_t_ref[...])
     mine_ref[...] = moved_ref[...]
     bias_ref[...] = jnp.broadcast_to(bias_in_ref[...], (8, C))
 
@@ -493,7 +504,9 @@
     mine = cross(weight)
     got = flat(over_space(depth))
     (plane,) = call(lambda *r: plane_kernel(False, *r), [short_shape], got, X_DOWN_4, scratch=held(4))
-    mine, bias = call(land_kernel, [((2, M // 2, CO), F32), ((8, C), F32)], mine, bias_term.reshape(1, C), flops=5000000000)
+    mine, bias, back = call(
+        land_kernel, [((2, M // 2, CO), F32), ((8, C), F32), ((CY, CY), BF16)],
+        mine, bias_term.reshape(1, C), mix_weight, OWN, OWN_T, flops=5000000000)
     other = partner(mine)
     got = over_dp(plane)
     mixed, coeff = call(
@@ -517,13 +530,15 @@
     )
     half = ((M, N), F32)
     keep, send = call(part_kernel, [half, half], cross_home(packed), flops=5_000_000_000)
+    (activated,) = call(store_kernel, [wide], activated, keep)
+    (linear,) = call(linear_kernel, [((S, CY, PLANES * N), F32)], grad, back, keep)
     other = partner(send)
     got = over_dp(mixed)
     (spread,) = call(lambda *r: spread_kernel(True, *r), [space_shape], got, X_UP_A, X_UP_B, scratch=held(8) + line(8))
     got = over_space(spread).reshape(M, S, 2 * PLANES, CY)
     grad_input, grad_mix, grad_bias = call(
         input_kernel, [wide, ((C, C), F32), ((1, C), F32)],
-        got, grad, mix_weight, Z_UP, OWN, OWN_T,
+        got, linear, Z_UP, OWN,
     )
     (grad_weight,) = call(outer_kernel, [((M // 2, 2, 1, CO), F32)], keep, other, PAIR_IN, PAIR_OUT)
     return (

time: 143 us -> 143 us (level)
  waiting for transfers between devices: 22.1 us -> 20.3 us
    pallas_call x12 -> x14, Pallas kernels: 10.9 us -> 11.8 us  [call(): pl.pallas_call(kernel, out_shape=shapes, in_specs=[far if i in far_in els...]
  transfers between devices with their start and end apart: 8 -> 8, of which waited for: 5 -> 4; matrix products, arithmetic and copies ran while one was open for 0% -> 0% of each run, Pallas kernels for 2% -> 3%
where the time goes in v6:
time: 143 us; the launch traced here: 142 us
  blocking collectives  57 us (40%)
  starting transfers between devices  51.1 us (36%)
  waiting for transfers between devices  20.3 us (14%)
  Pallas kernels  11.8 us (8%)
    all_to_all x4, blocking collectives, swap(): return lax.all_to_all(value, axis, 0, 0, tiled=True)  57 us
    all_to_all x4, starting transfers between devices, swap(): return lax.all_to_all(value, axis, 0, 0, tiled=True)  29.3 us
    all_to_all x4, waiting for transfers between devices, swap(): return lax.all_to_all(value, axis, 0, 0, tiled=True)  19.4 us
    ppermute x1, starting transfers between devices, on_device(): cross = lambda v: lax.ppermute(v, ('space', 'dp'), crossing)  13.6 us
    pallas_call x14, Pallas kernels, call(): pl.pallas_call(kernel, out_shape=shapes, in_specs=[far if i in far_in els...  11.8 us
    ppermute x2, starting transfers between devices, on_device(): partner = lambda v: lax.ppermute(v, 'space', pairing)  4.81 us
    ppermute x1, starting transfers between devices, on_device(): lax.ppermute(v, ('space', 'dp'), [(b, a) for a, b in crossing])  3.34 us
  transfers between devices with their start and end apart: 8, of which 4 were waited for; matrix products, arithmetic and copies ran while one was open for 0% of the time, Pallas kernels for 3%

profile of v6, /device:TPU:1, one launch (start us, length us, event | category | flops | bytes accessed | tf_op | source)
XLA Modules:
  0.0 142.5 jit_solution(16692969282297877204)
XLA Ops:
  0.6 2.1 %shard_map.308 = f32[16,2,8,256]{3,2,1,0:T(8,128)} custom-call(bf16[8,256,128]{2,1,0:T(8,128)(2,1)} %bitcast.19, bf16[128,512]{1,0:T(8,128)(2,1)} %constant.48.clone.table_ref.down_ref), custom_call_target="tpu_custom_call" | custom-call | flops 50000000 | bytes 917504 | tf_op jit(solution)/shard_map/pallas_call | solution.py:456
  2.7 10.5 %all-to-all-start = ((f32[32,8,256]{2,1,0:T(8,128)}), f32[32,8,256]{2,1,0:T(8,128)S(1)}, u32[]{:S(2)}, u32[]{:S(2)}) async-start(f32[32,8,256]{2,1,0:T(8,128)} %bitcast.29), calls=%async_computation | async-start | bytes 524288 | tf_op jit(solution)/shard_map/all_to_all | solution.py:468
  13.2 0.0 copy-done.28
  13.3 13.6 %collective-permute-start = (f32[2,8,1024]{2,1,0:T(8,128)S(1)}, f32[2,8,1024]{2,1,0:T(8,128)S(1)}, u32[]{:S(2)}, u32[]{:S(2)}) collective-permute-start(f32[2,8,1024]{2,1,0:T(8,128)S(1)} %convert_bitcast_fusion), channel_id=1, source_target_pairs={{320,0},{336,16},{192,1},{208,17},{352,2},{368,18},{64,3},{80,19},... | collective-permute-start | bytes 196616 | tf_op jit(solution)/shard_map/ppermute | solution.py:484
  26.9 0.0 all-to-all-done
  26.9 0.0 copy-done.13
  26.9 0.0 copy-start.25
  26.9 0.0 copy-start.26
  27.0 0.8 shard_map.309
  27.8 8.4 %all-to-all-start.1 = ((f32[16,4,128]{2,1,0:T(4,128)}), f32[16,4,128]{2,1,0:T(4,128)S(1)}, u32[]{:S(2)}, u32[]{:S(2)}) async-start(f32[16,4,128]{2,1,0:T(4,128)} %shard_map.309), calls=%async_computation.1 | async-start | bytes 65536 | tf_op jit(solution)/shard_map/all_to_all | solution.py:468
  36.2 0.0 copy-start.27
  36.3 0.0 collective-permute-done.moved_ref
  36.3 0.0 copy-done.25
  36.3 0.0 copy-done.26
  36.3 0.6 copy-done.27
  36.9 0.0 copy-start.23
  36.9 0.0 copy-start.24
  36.9 0.3 shard_map.310
  37.2 2.6 %collective-permute-start.1 = (f32[2,8,1024]{2,1,0:T(8,128)S(1)}, f32[2,8,1024]{2,1,0:T(8,128)S(1)}, u32[]{:S(2)}, u32[]{:S(2)}) collective-permute-start(f32[2,8,1024]{2,1,0:T(8,128)S(1)} %get-tuple-element.20.mine_ref), channel_id=1, source_target_pairs={{0,16},{16,0},{32,48},{48,32},{64,80},{80,64},{96,112},{112,96},{1... | collective-permute-start | bytes 196616 | tf_op jit(solution)/shard_map/ppermute | solution.py:486
  39.8 0.9 collective-permute-done.1.other_ref
  40.7 7.0 %all-to-all-done.1.got_ref = f32[16,4,128]{2,1,0:T(4,128)S(1)} async-done(((f32[16,4,128]{2,1,0:T(4,128)}), f32[16,4,128]{2,1,0:T(4,128)S(1)}, u32[]{:S(2)}, u32[]{:S(2)}) %all-to-all-start.1) | async-done | bytes 32800 | tf_op jit(solution)/shard_map/all_to_all | solution.py:468
  47.7 0.0 copy-done.5
  47.8 0.0 copy-start.15
  47.8 0.0 copy-start.16
  47.8 0.0 copy-start.7
  47.8 0.0 copy-start.14
  47.8 0.7 shard_map.311
  48.5 16.0 %all_to_all.40.r_0_ = f32[16,4,128]{2,1,0:T(4,128)S(1)} all-to-all(f32[16,4,128]{2,1,0:T(4,128)S(1)} %get-tuple-element.21), channel_id=1, replica_groups=mesh['space'=32,'dp'=16] {'dp'}, dimensions={0} | all-to-all | bytes 65536 | tf_op jit(solution)/shard_map/all_to_all | solution.py:468
  64.5 0.0 copy-done.15
  64.5 0.3 shard_map.312
  64.8 0.0 copy-start.1
  64.8 0.0 copy-start.4
  64.9 14.1 %all_to_all.41 = f32[32,8,256]{2,1,0:T(8,128)S(1)} all-to-all(f32[32,8,256]{2,1,0:T(8,128)S(1)} %bitcast.22), channel_id=1, replica_groups=mesh['space'=32,'dp'=16] {'space'}, dimensions={0} | all-to-all | bytes 524288 | tf_op jit(solution)/shard_map/all_to_all | solution.py:468
  78.9 0.0 copy-done
  78.9 0.0 copy-done.1
  79.0 0.0 copy-done.4
  79.0 0.0 copy-start.8
  79.0 0.0 copy-start.22
  79.0 1.5 %shard_map.313 = (bf16[8,256,128]{2,1,0:T(8,128)(2,1)S(1)}, bf16[8,256,128]{2,1,0:T(8,128)(2,1)S(1)}, f32[16,2,8,256]{3,2,1,0:T(8,128)S(1)}) custom-call(f32[16,2,8,256]{3,2,1,0:T(8,128)S(1)} %bitcast.25, bf16[8,256,128]{2,1,0:T(8,128)(2,1)S(1)} %bitcast.20, bf16[8,256,128]{2,1,0:T(8,128)(2,1)S(1)} %bitcast.26, bf16[32,32]{1,0:T(8,128)(2,1)S(1)} %copy-done.26, ...), custom_call_target="tpu_custom_call" | custom-call | flops 50000000 | bytes 3312640 | tf_op jit(solution)/shard_map/pallas_call | solution.py:456
  80.5 0.0 copy-start.3
  80.5 12.6 %all_to_all.42 = f32[32,8,256]{2,1,0:T(8,128)S(1)} all-to-all(f32[32,8,256]{2,1,0:T(8,128)S(1)} %bitcast.27), channel_id=1, replica_groups=mesh['space'=32,'dp'=16] {'space'}, dimensions={0} | all-to-all | bytes 524288 | tf_op jit(solution)/shard_map/all_to_all | solution.py:468
  93.1 0.3 shard_map.314
  93.4 0.0 copy-start.19
  93.5 14.3 %all_to_all.43.got_ref = f32[16,8,128]{2,1,0:T(8,128)S(1)} all-to-all(f32[16,8,128]{2,1,0:T(8,128)S(1)} %shard_map.314), channel_id=1, replica_groups=mesh['space'=32,'dp'=16] {'dp'}, dimensions={0} | all-to-all | bytes 131072 | tf_op jit(solution)/shard_map/all_to_all | solution.py:468
  107.8 0.0 copy-done.10
  107.8 0.0 copy-done.19
  107.8 0.0 copy-start.11
  107.8 0.0 copy-start.12
  107.8 1.4 shard_map.315
  109.2 3.9 %all-to-all-start.6 = ((f32[16,8,128]{2,1,0:T(8,128)}), f32[16,8,128]{2,1,0:T(8,128)S(1)}, u32[]{:S(2)}, u32[]{:S(2)}) async-start(f32[16,8,128]{2,1,0:T(8,128)} %get-tuple-element.28), calls=%async_computation.6 | async-start | bytes 131072 | tf_op jit(solution)/shard_map/all_to_all | solution.py:468
  113.1 3.3 %collective-permute-start.2 = (f32[2,16,128]{2,1,0:T(8,128)S(1)}, f32[2,16,128]{2,1,0:T(8,128)S(1)}, u32[]{:S(2)}, u32[]{:S(2)}) collective-permute-start(f32[2,16,128]{2,1,0:T(8,128)S(1)} %get-tuple-element.26), channel_id=1, source_target_pairs={{0,320},{16,336},{1,192},{17,208},{2,352},{18,368},{3,64},{19,80},... | collective-permute-start | bytes 49160 | tf_op jit(solution)/shard_map/ppermute | solution.py:485
  116.4 8.2 %all-to-all-done.6.r_0_ = f32[16,8,128]{2,1,0:T(8,128)S(1)} async-done(((f32[16,8,128]{2,1,0:T(8,128)}), f32[16,8,128]{2,1,0:T(8,128)S(1)}, u32[]{:S(2)}, u32[]{:S(2)}) %all-to-all-start.6) | async-done | bytes 65568 | tf_op jit(solution)/shard_map/all_to_all | solution.py:468
  124.7 1.0 shard_map.318
  125.7 6.5 %all-to-all-start.7 = ((f32[32,8,256]{2,1,0:T(8,128)}), f32[32,8,256]{2,1,0:T(8,128)S(1)}, u32[]{:S(2)}, u32[]{:S(2)}) async-start(f32[32,8,256]{2,1,0:T(8,128)} %bitcast.12), calls=%async_computation.7 | async-start | bytes 524288 | tf_op jit(solution)/shard_map/all_to_all | solution.py:468
  132.2 0.0 collective-permute-done.2.moved_ref
  132.2 2.3 %collective-permute-start.3 = (f32[16,128]{1,0:T(8,128)S(1)}, f32[16,128]{1,0:T(8,128)S(1)}, u32[]{:S(2)}, u32[]{:S(2)}) collective-permute-start(f32[16,128]{1,0:T(8,128)S(1)} %get-tuple-element.32), channel_id=1, source_target_pairs={{0,16},{16,0},{32,48},{48,32},{64,80},{80,64},{96,112},{112,96},{1... | collective-permute-start | bytes 24584 | tf_op jit(solution)/shard_map/ppermute | solution.py:486
  134.5 0.8 shard_map.317
  135.3 0.3 shard_map.319.linear_ref
  135.6 0.0 collective-permute-done.3.other_ref
  135.6 0.5 copy-done.20
  136.2 0.0 copy-done.21
  136.2 0.9 shard_map.321
  137.1 4.1 %all-to-all-done.7 = f32[32,8,256]{2,1,0:T(8,128)S(1)} async-done(((f32[32,8,256]{2,1,0:T(8,128)}), f32[32,8,256]{2,1,0:T(8,128)S(1)}, u32[]{:S(2)}, u32[]{:S(2)}) %all-to-all-start.7) | async-done | bytes 262176 | tf_op jit(solution)/shard_map/all_to_all | solution.py:468
  141.2 1.3 shard_map.320
  (29 shorter events, 0.1 us)
Async XLA Ops:
  2.7 10.5 %copy-start.28 = (bf16[8,2,1,1024]{3,1,2,0:T(2,128)(2,1)S(1)}, bf16[8,2,1,1024]{3,1,2,0:T(2,128)(2,1)}, u32[]{:S(2)}) copy-start(bf16[8,2,1,1024]{3,1,2,0:T(2,128)(2,1)} %param.31) | copy-start | bytes 98308
  2.7 24.2 %copy-start.13 = (bf16[64,1536]{1,0:T(8,128)(2,1)S(1)}, bf16[64,1536]{1,0:T(8,128)(2,1)}, u32[]{:S(2)}) copy-start(bf16[64,1536]{1,0:T(8,128)(2,1)} %constant.49.clone.r_1_) | copy-start | bytes 589828
  2.7 24.2 %all-to-all-start = ((f32[32,8,256]{2,1,0:T(8,128)}), f32[32,8,256]{2,1,0:T(8,128)S(1)}, u32[]{:S(2)}, u32[]{:S(2)}) async-start(f32[32,8,256]{2,1,0:T(8,128)} %bitcast.29), calls=%async_computation | async-start | bytes 524288 | tf_op jit(solution)/shard_map/all_to_all | solution.py:468
  13.3 23.0 %collective-permute-start = (f32[2,8,1024]{2,1,0:T(8,128)S(1)}, f32[2,8,1024]{2,1,0:T(8,128)S(1)}, u32[]{:S(2)}, u32[]{:S(2)}) collective-permute-start(f32[2,8,1024]{2,1,0:T(8,128)S(1)} %convert_bitcast_fusion), channel_id=1, source_target_pairs={{320,0},{336,16},{192,1},{208,17},{352,2},{368,18},{64,3},{80,19},... | collective-permute-start | bytes 196616 | tf_op jit(solution)/shard_map/ppermute | solution.py:484
  26.9 9.3 %copy-start.25 = (bf16[32,256]{1,0:T(8,128)(2,1)S(1)}, bf16[32,256]{1,0:T(8,128)(2,1)}, u32[]{:S(2)}) copy-start(bf16[32,256]{1,0:T(8,128)(2,1)} %constant.51.clone.own_t_ref) | copy-start | bytes 49156
  26.9 9.3 %copy-start.26 = (bf16[32,32]{1,0:T(8,128)(2,1)S(1)}, bf16[32,32]{1,0:T(8,128)(2,1)}, u32[]{:S(2)}) copy-start(bf16[32,32]{1,0:T(8,128)(2,1)} %mix_ref.3) | copy-start | bytes 6148
  27.8 8.5 %copy-start.9 = (bf16[256,32]{1,0:T(8,128)(2,1)S(1)}, bf16[256,32]{1,0:T(8,128)(2,1)}, u32[]{:S(2)}) copy-start(bf16[256,32]{1,0:T(8,128)(2,1)} %constant.50.clone.own_ref) | copy-start | bytes 49156
  27.8 19.9 %all-to-all-start.1 = ((f32[16,4,128]{2,1,0:T(4,128)}), f32[16,4,128]{2,1,0:T(4,128)S(1)}, u32[]{:S(2)}, u32[]{:S(2)}) async-start(f32[16,4,128]{2,1,0:T(4,128)} %shard_map.309), calls=%async_computation.1 | async-start | bytes 65536 | tf_op jit(solution)/shard_map/all_to_all | solution.py:468
  36.2 0.7 copy-start.27
  36.9 10.8 %copy-start.5 = (bf16[256,1024]{1,0:T(8,128)(2,1)S(1)}, bf16[256,1024]{1,0:T(8,128)(2,1)}, u32[]{:S(2)}) copy-start(bf16[256,1024]{1,0:T(8,128)(2,1)} %constant.56.clone.grow_ref) | copy-start | bytes 1572868
  36.9 10.8 %copy-start.6 = (bf16[1024,256]{1,0:T(8,128)(2,1)S(1)}, bf16[1024,256]{1,0:T(8,128)(2,1)}, u32[]{:S(2)}) copy-start(bf16[1024,256]{1,0:T(8,128)(2,1)} %constant.57.clone.sum_ref) | copy-start | bytes 1572868
  36.9 10.8 %copy-start.17 = (f32[16,256]{1,0:T(8,128)S(1)}, f32[16,256]{1,0:T(8,128)}, u32[]{:S(2)}) copy-start(f32[16,256]{1,0:T(8,128)} %constant.54.clone.cos_ref) | copy-start | bytes 49156
  36.9 10.8 %copy-start.18 = (f32[16,256]{1,0:T(8,128)S(1)}, f32[16,256]{1,0:T(8,128)}, u32[]{:S(2)}) copy-start(f32[16,256]{1,0:T(8,128)} %constant.55.clone.sin_ref) | copy-start | bytes 49156
  36.9 10.8 %copy-start.23 = (bf16[64,192]{1,0:T(8,128)(2,1)S(1)}, bf16[64,192]{1,0:T(8,128)(2,1)}, u32[]{:S(2)}) copy-start(bf16[64,192]{1,0:T(8,128)(2,1)} %constant.52.clone.down_ref) | copy-start | bytes 73732
  36.9 10.8 %copy-start.24 = (bf16[64,192]{1,0:T(8,128)(2,1)S(1)}, bf16[64,192]{1,0:T(8,128)(2,1)}, u32[]{:S(2)}) copy-start(bf16[64,192]{1,0:T(8,128)(2,1)} %constant.53.clone.up_ref) | copy-start | bytes 73732
  37.2 3.4 %collective-permute-start.1 = (f32[2,8,1024]{2,1,0:T(8,128)S(1)}, f32[2,8,1024]{2,1,0:T(8,128)S(1)}, u32[]{:S(2)}, u32[]{:S(2)}) collective-permute-start(f32[2,8,1024]{2,1,0:T(8,128)S(1)} %get-tuple-element.20.mine_ref), channel_id=1, source_target_pairs={{0,16},{16,0},{32,48},{48,32},{64,80},{80,64},{96,112},{112,96},{1... | collective-permute-start | bytes 196616 | tf_op jit(solution)/shard_map/ppermute | solution.py:486
  47.8 16.7 %copy-start.15 = (bf16[256,192]{1,0:T(8,128)(2,1)S(1)}, bf16[256,192]{1,0:T(8,128)(2,1)}, u32[]{:S(2)}) copy-start(bf16[256,192]{1,0:T(8,128)(2,1)} %constant.58.clone.r_1_) | copy-start | bytes 294916
  47.8 16.7 %copy-start.16 = (bf16[256,192]{1,0:T(8,128)(2,1)S(1)}, bf16[256,192]{1,0:T(8,128)(2,1)}, u32[]{:S(2)}) copy-start(bf16[256,192]{1,0:T(8,128)(2,1)} %constant.59.clone.r_2_) | copy-start | bytes 294916
  47.8 31.1 %copy-start.7 = (bf16[2,4,32,8,128]{4,3,2,1,0:T(8,128)(2,1)S(1)}, bf16[2,4,32,8,128]{4,3,2,1,0:T(8,128)(2,1)}, u32[]{:S(2)}) copy-start(bf16[2,4,32,8,128]{4,3,2,1,0:T(8,128)(2,1)} %param.30) | copy-start | bytes 1572868
  47.8 31.1 %copy-start.14 = (bf16[256,256]{1,0:T(8,128)(2,1)S(1)}, bf16[256,256]{1,0:T(8,128)(2,1)}, u32[]{:S(2)}) copy-start(bf16[256,256]{1,0:T(8,128)(2,1)} %constant.61.clone.block_ref) | copy-start | bytes 393220
  64.5 14.4 %copy-start = (bf16[2,4,32,8,128]{4,3,2,1,0:T(8,128)(2,1)S(1)}, bf16[2,4,32,8,128]{4,3,2,1,0:T(8,128)(2,1)}, u32[]{:S(2)}) copy-start(bf16[2,4,32,8,128]{4,3,2,1,0:T(8,128)(2,1)} %param.29) | copy-start | bytes 1572868
  64.8 14.1 %copy-start.1 = (bf16[384,512]{1,0:T(8,128)(2,1)S(1)}, bf16[384,512]{1,0:T(8,128)(2,1)}, u32[]{:S(2)}) copy-start(bf16[384,512]{1,0:T(8,128)(2,1)} %constant.60.clone.up_ref) | copy-start | bytes 1179652
  64.8 14.1 %copy-start.4 = (bf16[128,512]{1,0:T(8,128)(2,1)S(1)}, bf16[128,512]{1,0:T(8,128)(2,1)}, u32[]{:S(2)}) copy-start(bf16[128,512]{1,0:T(8,128)(2,1)} %constant.48.clone.table_ref.down_ref) | copy-start | bytes 393220
  79.0 14.1 %copy-start.8 = (bf16[128,1536]{1,0:T(8,128)(2,1)S(1)}, bf16[128,1536]{1,0:T(8,128)(2,1)}, u32[]{:S(2)}) copy-start(bf16[128,1536]{1,0:T(8,128)(2,1)} %constant.62.clone.r_1_) | copy-start | bytes 1179652
  79.0 28.8 %copy-start.22 = (bf16[64,384]{1,0:T(8,128)(2,1)S(1)}, bf16[64,384]{1,0:T(8,128)(2,1)}, u32[]{:S(2)}) copy-start(bf16[64,384]{1,0:T(8,128)(2,1)} %constant.63.clone.down_ref) | copy-start | bytes 147460
  80.5 27.3 %copy-start.3 = (bf16[1024,256]{1,0:T(8,128)(2,1)S(1)}, bf16[1024,256]{1,0:T(8,128)(2,1)}, u32[]{:S(2)}) copy-start(bf16[1024,256]{1,0:T(8,128)(2,1)} %constant.66.clone.sum_ref) | copy-start | bytes 1572868
  93.1 14.7 %copy-start.2 = (bf16[256,1024]{1,0:T(8,128)(2,1)S(1)}, bf16[256,1024]{1,0:T(8,128)(2,1)}, u32[]{:S(2)}) copy-start(bf16[256,1024]{1,0:T(8,128)(2,1)} %constant.65.clone.grow_ref) | copy-start | bytes 1572868
  93.1 14.7 %copy-start.10 = (bf16[512,256]{1,0:T(8,128)(2,1)S(1)}, bf16[512,256]{1,0:T(8,128)(2,1)}, u32[]{:S(2)}) copy-start(bf16[512,256]{1,0:T(8,128)(2,1)} %constant.67.clone.pack_ref) | copy-start | bytes 786436
  93.4 14.3 %copy-start.19 = (bf16[128,192]{1,0:T(8,128)(2,1)S(1)}, bf16[128,192]{1,0:T(8,128)(2,1)}, u32[]{:S(2)}) copy-start(bf16[128,192]{1,0:T(8,128)(2,1)} %constant.64.clone.up_ref) | copy-start | bytes 147460
  107.8 16.9 %copy-start.11 = (bf16[256,384]{1,0:T(8,128)(2,1)S(1)}, bf16[256,384]{1,0:T(8,128)(2,1)}, u32[]{:S(2)}) copy-start(bf16[256,384]{1,0:T(8,128)(2,1)} %constant.68.clone.r_1_) | copy-start | bytes 589828
  107.8 16.9 %copy-start.12 = (bf16[256,384]{1,0:T(8,128)(2,1)S(1)}, bf16[256,384]{1,0:T(8,128)(2,1)}, u32[]{:S(2)}) copy-start(bf16[256,384]{1,0:T(8,128)(2,1)} %constant.69.clone.r_2_) | copy-start | bytes 589828
  109.2 15.5 %all-to-all-start.6 = ((f32[16,8,128]{2,1,0:T(8,128)}), f32[16,8,128]{2,1,0:T(8,128)S(1)}, u32[]{:S(2)}, u32[]{:S(2)}) async-start(f32[16,8,128]{2,1,0:T(8,128)} %get-tuple-element.28), calls=%async_computation.6 | async-start | bytes 131072 | tf_op jit(solution)/shard_map/all_to_all | solution.py:468
  113.1 19.2 %collective-permute-start.2 = (f32[2,16,128]{2,1,0:T(8,128)S(1)}, f32[2,16,128]{2,1,0:T(8,128)S(1)}, u32[]{:S(2)}, u32[]{:S(2)}) collective-permute-start(f32[2,16,128]{2,1,0:T(8,128)S(1)} %get-tuple-element.26), channel_id=1, source_target_pairs={{0,320},{16,336},{1,192},{17,208},{2,352},{18,368},{3,64},{19,80},... | collective-permute-start | bytes 49160 | tf_op jit(solution)/shard_map/ppermute | solution.py:485
  125.7 15.5 %all-to-all-start.7 = ((f32[32,8,256]{2,1,0:T(8,128)}), f32[32,8,256]{2,1,0:T(8,128)S(1)}, u32[]{:S(2)}, u32[]{:S(2)}) async-start(f32[32,8,256]{2,1,0:T(8,128)} %bitcast.12), calls=%async_computation.7 | async-start | bytes 524288 | tf_op jit(solution)/shard_map/all_to_all | solution.py:468
  132.2 3.4 %collective-permute-start.3 = (f32[16,128]{1,0:T(8,128)S(1)}, f32[16,128]{1,0:T(8,128)S(1)}, u32[]{:S(2)}, u32[]{:S(2)}) collective-permute-start(f32[16,128]{1,0:T(8,128)S(1)} %get-tuple-element.32), channel_id=1, source_target_pairs={{0,16},{16,0},{32,48},{48,32},{64,80},{80,64},{96,112},{112,96},{1... | collective-permute-start | bytes 24584 | tf_op jit(solution)/shard_map/ppermute | solution.py:486
  135.3 0.8 copy-start.20
  135.3 0.9 copy-start.21

commit v7 on v6

--- a/solution.py
+++ b/solution.py
@@ -282,13 +282,11 @@
     return real * cosine + imag * sine, imag * cosine - real * sine
 
 
-def weight_rows(mine_ref, other_ref):
+def weight_kernel(mine_ref, other_ref, out_ref):
     even = lax.axis_index("space") % 2 == 0
     mine, other = mine_ref[...], other_ref[...]
-    first = jnp.where(even, mine, other)
-    second = jnp.where(even, other, mine)
-    whole = jnp.concatenate([first, second], 1)
-    return whole[0], whole[1]
+    out_ref[:, : M // 2] = jnp.where(even, mine, other)
+    out_ref[:, M // 2 :] = jnp.where(even, other, mine)
 
 
 def row_synth(real, imag, table_ref, cos_ref, sin_ref):
@@ -298,24 +296,24 @@
     return dot(table_ref[...], stacked)
 
 
-def mix_kernel(got_ref, mine_ref, other_ref, down_ref, up_ref, cos_ref, sin_ref, grow_ref, sum_ref, out_ref, spectrum_ref, flat_ref):
+def mix_kernel(got_ref, weight_ref, down_ref, up_ref, cos_ref, sin_ref, grow_ref, sum_ref, out_ref, spectrum_ref, flat_ref):
     real, imag = row_spectrum(take_blocks(got_ref, flat_ref), down_ref, cos_ref, sin_ref)
     spectrum = jnp.concatenate([real, imag], 0)
     spectrum_ref[...] = spectrum
     coeff = apply_exact(spectrum, grow_ref[...])
     cr, ci = coeff[:M], coeff[M:]
-    wr, wi = weight_rows(mine_ref, other_ref)
+    wr, wi = weight_ref[0], weight_ref[1]
     mixed = apply_exact(jnp.concatenate([cr * wr - ci * wi, cr * wi + ci * wr], 0), sum_ref[...])
     put_blocks(row_synth(mixed[:M], mixed[M:], up_ref, cos_ref, sin_ref), out_ref)
 
 
-def back_kernel(got_ref, mine_ref, other_ref, down_ref, up_ref, cos_ref, sin_ref, grow_ref, sum_ref, pack_ref, coeff_ref, out_ref, packed_ref):
+def back_kernel(got_ref, weight_ref, down_ref, up_ref, cos_ref, sin_ref, grow_ref, sum_ref, pack_ref, coeff_ref, out_ref, packed_ref):
     real, imag = row_spectrum(got_ref[...].reshape(GROUPS * 8, N), down_ref, cos_ref, sin_ref)
     spectrum = jnp.concatenate([real, imag], 0)
     pack(coeff_ref[...], spectrum, pack_ref[...], packed_ref)
     cot = apply_exact(spectrum, grow_ref[...])
     dr, di = cot[:M], cot[M:]
-    wr, wi = weight_rows(mine_ref, other_ref)
+    wr, wi = weight_ref[0], weight_ref[1]
     back = apply_exact(jnp.concatenate([dr * wr + di * wi, di * wr - dr * wi], 0), sum_ref[...])
     out = row_synth(back[:M], back[M:], up_ref, cos_ref, sin_ref)
     total = jnp.sum(got_ref[...], 0)
@@ -507,11 +505,11 @@
     mine, bias, back = call(
         land_kernel, [((2, M // 2, CO), F32), ((8, C), F32), ((CY, CY), BF16)],
         mine, bias_term.reshape(1, C), mix_weight, OWN, OWN_T, flops=5000000000)
-    other = partner(mine)
+    (weight,) = call(weight_kernel, [((2, M, CO), F32)], mine, partner(mine))
     got = over_dp(plane)
     mixed, coeff = call(
         mix_kernel, [short_shape, ((2 * M, CY), F32)],
-        got, mine, other, Y_DOWN_4, Y_UP_4, ROW_COS, ROW_SIN, GROW_IN, SUM_OUT, scratch=line(4),
+        got, weight, Y_DOWN_4, Y_UP_4, ROW_COS, ROW_SIN, GROW_IN, SUM_OUT, scratch=line(4),
     )
     got = over_dp(mixed)
     (spread,) = call(lambda *r: spread_kernel(False, *r), [space_shape], got, X_UP_A_4, X_UP_B_4, scratch=held(4) + line(4))
@@ -526,7 +524,7 @@
     got = over_dp(plane)
     mixed, packed = call(
         back_kernel, [plane_shape, ((2, M, N), F32)],
-        got, mine, other, Y_DOWN, Y_UP, ROW_COS, ROW_SIN, GROW_OUT, SUM_IN, PACK, coeff,
+        got, weight, Y_DOWN, Y_UP, ROW_COS, ROW_SIN, GROW_OUT, SUM_IN, PACK, coeff,
     )
     half = ((M, N), F32)
     keep, send = call(part_kernel, [half, half], cross_home(packed), flops=5_000_000_000)

time: 143 us -> 143 us (level)
    pallas_call x14 -> x15, Pallas kernels: 11.8 us -> 11.8 us  [call(): pl.pallas_call(kernel, out_shape=shapes, in_specs=[far if i in far_in els...]
where the time goes in v7:
time: 143 us
  blocking collectives  57 us (40%)
  starting transfers between devices  51.1 us (36%)
  waiting for transfers between devices  20.2 us (14%)
  Pallas kernels  11.8 us (8%)
    all_to_all x4, blocking collectives, swap(): return lax.all_to_all(value, axis, 0, 0, tiled=True)  57 us
    all_to_all x4, starting transfers between devices, swap(): return lax.all_to_all(value, axis, 0, 0, tiled=True)  29.3 us
    all_to_all x4, waiting for transfers between devices, swap(): return lax.all_to_all(value, axis, 0, 0, tiled=True)  19.4 us
    ppermute x1, starting transfers between devices, on_device(): cross = lambda v: lax.ppermute(v, ('space', 'dp'), crossing)  13.6 us
    pallas_call x15, Pallas kernels, call(): pl.pallas_call(kernel, out_shape=shapes, in_specs=[far if i in far_in els...  11.8 us
    ppermute x2, starting transfers between devices, on_device(): partner = lambda v: lax.ppermute(v, 'space', pairing)  4.81 us
    ppermute x1, starting transfers between devices, on_device(): lax.ppermute(v, ('space', 'dp'), [(b, a) for a, b in crossing])  3.34 us
  transfers between devices with their start and end apart: 8, of which 4 were waited for; matrix products, arithmetic and copies ran while one was open for 0% of the time, Pallas kernels for 3%

profile of v7, /device:TPU:1, one launch (start us, length us, event | category | flops | bytes accessed | tf_op | source)
XLA Modules:
  0.0 142.5 jit_solution(280627200798200533)
XLA Ops:
  0.6 2.1 %shard_map.308 = f32[16,2,8,256]{3,2,1,0:T(8,128)} custom-call(bf16[8,256,128]{2,1,0:T(8,128)(2,1)} %bitcast.19, bf16[128,512]{1,0:T(8,128)(2,1)} %constant.48.clone.table_ref.down_ref), custom_call_target="tpu_custom_call" | custom-call | flops 50000000 | bytes 917504 | tf_op jit(solution)/shard_map/pallas_call | solution.py:454
  2.7 10.5 %all-to-all-start = ((f32[32,8,256]{2,1,0:T(8,128)}), f32[32,8,256]{2,1,0:T(8,128)S(1)}, u32[]{:S(2)}, u32[]{:S(2)}) async-start(f32[32,8,256]{2,1,0:T(8,128)} %bitcast.29), calls=%async_computation | async-start | bytes 524288 | tf_op jit(solution)/shard_map/all_to_all | solution.py:466
  13.2 0.0 copy-done.28
  13.3 13.6 %collective-permute-start = (f32[2,8,1024]{2,1,0:T(8,128)S(1)}, f32[2,8,1024]{2,1,0:T(8,128)S(1)}, u32[]{:S(2)}, u32[]{:S(2)}) collective-permute-start(f32[2,8,1024]{2,1,0:T(8,128)S(1)} %convert_bitcast_fusion), channel_id=1, source_target_pairs={{320,0},{336,16},{192,1},{208,17},{352,2},{368,18},{64,3},{80,19},... | collective-permute-start | bytes 196616 | tf_op jit(solution)/shard_map/ppermute | solution.py:482
  26.9 0.0 all-to-all-done
  26.9 0.0 copy-done.13
  26.9 0.0 copy-start.25
  26.9 0.0 copy-start.26
  27.0 0.8 shard_map.309
  27.8 8.4 %all-to-all-start.1 = ((f32[16,4,128]{2,1,0:T(4,128)}), f32[16,4,128]{2,1,0:T(4,128)S(1)}, u32[]{:S(2)}, u32[]{:S(2)}) async-start(f32[16,4,128]{2,1,0:T(4,128)} %shard_map.309), calls=%async_computation.1 | async-start | bytes 65536 | tf_op jit(solution)/shard_map/all_to_all | solution.py:466
  36.2 0.0 copy-start.27
  36.3 0.0 collective-permute-done.moved_ref
  36.3 0.0 copy-done.25
  36.3 0.0 copy-done.26
  36.3 0.0 copy-done.9
  36.3 0.6 copy-done.27
  36.9 0.3 shard_map.310
  37.2 0.0 copy-start.17
  37.2 0.0 copy-start.18
  37.2 0.0 copy-start.23
  37.3 0.0 copy-start.24
  37.3 2.6 %collective-permute-start.1 = (f32[2,8,1024]{2,1,0:T(8,128)S(1)}, f32[2,8,1024]{2,1,0:T(8,128)S(1)}, u32[]{:S(2)}, u32[]{:S(2)}) collective-permute-start(f32[2,8,1024]{2,1,0:T(8,128)S(1)} %get-tuple-element.20.mine_ref), channel_id=1, source_target_pairs={{0,16},{16,0},{32,48},{48,32},{64,80},{80,64},{96,112},{112,96},{1... | collective-permute-start | bytes 196616 | tf_op jit(solution)/shard_map/ppermute | solution.py:484
  39.8 0.9 collective-permute-done.1.other_ref
  40.7 7.0 %all-to-all-done.1.got_ref = f32[16,4,128]{2,1,0:T(4,128)S(1)} async-done(((f32[16,4,128]{2,1,0:T(4,128)}), f32[16,4,128]{2,1,0:T(4,128)S(1)}, u32[]{:S(2)}, u32[]{:S(2)}) %all-to-all-start.1) | async-done | bytes 32800 | tf_op jit(solution)/shard_map/all_to_all | solution.py:466
  47.7 0.0 copy-done.5
  47.8 0.0 copy-start.15
  47.8 0.0 copy-start.16
  47.8 0.0 copy-start.7
  47.8 0.0 copy-start.14
  47.8 0.7 shard_map.312
  48.5 16.0 %all_to_all.40.r_0_ = f32[16,4,128]{2,1,0:T(4,128)S(1)} all-to-all(f32[16,4,128]{2,1,0:T(4,128)S(1)} %get-tuple-element.21), channel_id=1, replica_groups=mesh['space'=32,'dp'=16] {'dp'}, dimensions={0} | all-to-all | bytes 65536 | tf_op jit(solution)/shard_map/all_to_all | solution.py:466
  64.6 0.3 shard_map.313
  64.9 0.0 copy-start.1
  64.9 0.0 copy-start.4
  64.9 14.1 %all_to_all.41 = f32[32,8,256]{2,1,0:T(8,128)S(1)} all-to-all(f32[32,8,256]{2,1,0:T(8,128)S(1)} %bitcast.22), channel_id=1, replica_groups=mesh['space'=32,'dp'=16] {'space'}, dimensions={0} | all-to-all | bytes 524288 | tf_op jit(solution)/shard_map/all_to_all | solution.py:466
  79.0 0.0 copy-done.7
  79.0 0.0 copy-start.8
  79.0 0.0 copy-start.22
  79.0 1.5 %shard_map.314 = (bf16[8,256,128]{2,1,0:T(8,128)(2,1)S(1)}, bf16[8,256,128]{2,1,0:T(8,128)(2,1)S(1)}, f32[16,2,8,256]{3,2,1,0:T(8,128)S(1)}) custom-call(f32[16,2,8,256]{3,2,1,0:T(8,128)S(1)} %bitcast.25, bf16[8,256,128]{2,1,0:T(8,128)(2,1)S(1)} %bitcast.20, bf16[8,256,128]{2,1,0:T(8,128)(2,1)S(1)} %bitcast.26, bf16[32,32]{1,0:T(8,128)(2,1)S(1)} %copy-done.26, ...), custom_call_target="tpu_custom_call" | custom-call | flops 50000000 | bytes 3312640 | tf_op jit(solution)/shard_map/pallas_call | solution.py:454
  80.5 0.0 copy-start.3
  80.5 12.6 %all_to_all.42 = f32[32,8,256]{2,1,0:T(8,128)S(1)} all-to-all(f32[32,8,256]{2,1,0:T(8,128)S(1)} %bitcast.27), channel_id=1, replica_groups=mesh['space'=32,'dp'=16] {'space'}, dimensions={0} | all-to-all | bytes 524288 | tf_op jit(solution)/shard_map/all_to_all | solution.py:466
  93.1 0.3 shard_map.315
  93.5 0.0 copy-start.19
  93.5 14.3 %all_to_all.43.got_ref = f32[16,8,128]{2,1,0:T(8,128)S(1)} all-to-all(f32[16,8,128]{2,1,0:T(8,128)S(1)} %shard_map.315), channel_id=1, replica_groups=mesh['space'=32,'dp'=16] {'dp'}, dimensions={0} | all-to-all | bytes 131072 | tf_op jit(solution)/shard_map/all_to_all | solution.py:466
  107.8 0.0 copy-done.3
  107.8 0.0 copy-start.11
  107.8 0.0 copy-start.12
  107.8 1.4 shard_map.316
  109.2 3.9 %all-to-all-start.6 = ((f32[16,8,128]{2,1,0:T(8,128)}), f32[16,8,128]{2,1,0:T(8,128)S(1)}, u32[]{:S(2)}, u32[]{:S(2)}) async-start(f32[16,8,128]{2,1,0:T(8,128)} %get-tuple-element.28), calls=%async_computation.6 | async-start | bytes 131072 | tf_op jit(solution)/shard_map/all_to_all | solution.py:466
  113.1 3.3 %collective-permute-start.2 = (f32[2,16,128]{2,1,0:T(8,128)S(1)}, f32[2,16,128]{2,1,0:T(8,128)S(1)}, u32[]{:S(2)}, u32[]{:S(2)}) collective-permute-start(f32[2,16,128]{2,1,0:T(8,128)S(1)} %get-tuple-element.26), channel_id=1, source_target_pairs={{0,320},{16,336},{1,192},{17,208},{2,352},{18,368},{3,64},{19,80},... | collective-permute-start | bytes 49160 | tf_op jit(solution)/shard_map/ppermute | solution.py:483
  116.4 8.2 %all-to-all-done.6.r_0_ = f32[16,8,128]{2,1,0:T(8,128)S(1)} async-done(((f32[16,8,128]{2,1,0:T(8,128)}), f32[16,8,128]{2,1,0:T(8,128)S(1)}, u32[]{:S(2)}, u32[]{:S(2)}) %all-to-all-start.6) | async-done | bytes 65568 | tf_op jit(solution)/shard_map/all_to_all | solution.py:466
  124.7 0.0 copy-done.12
  124.7 1.0 shard_map.319
  125.7 6.5 %all-to-all-start.7 = ((f32[32,8,256]{2,1,0:T(8,128)}), f32[32,8,256]{2,1,0:T(8,128)S(1)}, u32[]{:S(2)}, u32[]{:S(2)}) async-start(f32[32,8,256]{2,1,0:T(8,128)} %bitcast.12), calls=%async_computation.7 | async-start | bytes 524288 | tf_op jit(solution)/shard_map/all_to_all | solution.py:466
  132.2 0.0 collective-permute-done.2.moved_ref
  132.3 2.3 %collective-permute-start.3 = (f32[16,128]{1,0:T(8,128)S(1)}, f32[16,128]{1,0:T(8,128)S(1)}, u32[]{:S(2)}, u32[]{:S(2)}) collective-permute-start(f32[16,128]{1,0:T(8,128)S(1)} %get-tuple-element.32), channel_id=1, source_target_pairs={{0,16},{16,0},{32,48},{48,32},{64,80},{80,64},{96,112},{112,96},{1... | collective-permute-start | bytes 24584 | tf_op jit(solution)/shard_map/ppermute | solution.py:484
  134.5 0.8 shard_map.318
  135.4 0.3 shard_map.320.linear_ref
  135.7 0.0 collective-permute-done.3.other_ref
  135.7 0.5 copy-done.20
  136.2 0.0 copy-done.21
  136.2 0.9 shard_map.322
  137.2 4.1 %all-to-all-done.7 = f32[32,8,256]{2,1,0:T(8,128)S(1)} async-done(((f32[32,8,256]{2,1,0:T(8,128)}), f32[32,8,256]{2,1,0:T(8,128)S(1)}, u32[]{:S(2)}, u32[]{:S(2)}) %all-to-all-start.7) | async-done | bytes 262176 | tf_op jit(solution)/shard_map/all_to_all | solution.py:466
  141.2 1.3 shard_map.321
  (30 shorter events, 0.1 us)
Async XLA Ops:
  2.7 10.5 %copy-start.28 = (bf16[8,2,1,1024]{3,1,2,0:T(2,128)(2,1)S(1)}, bf16[8,2,1,1024]{3,1,2,0:T(2,128)(2,1)}, u32[]{:S(2)}) copy-start(bf16[8,2,1,1024]{3,1,2,0:T(2,128)(2,1)} %param.31) | copy-start | bytes 98308
  2.7 24.2 %copy-start.13 = (bf16[64,1536]{1,0:T(8,128)(2,1)S(1)}, bf16[64,1536]{1,0:T(8,128)(2,1)}, u32[]{:S(2)}) copy-start(bf16[64,1536]{1,0:T(8,128)(2,1)} %constant.49.clone.r_1_) | copy-start | bytes 589828
  2.7 24.2 %all-to-all-start = ((f32[32,8,256]{2,1,0:T(8,128)}), f32[32,8,256]{2,1,0:T(8,128)S(1)}, u32[]{:S(2)}, u32[]{:S(2)}) async-start(f32[32,8,256]{2,1,0:T(8,128)} %bitcast.29), calls=%async_computation | async-start | bytes 524288 | tf_op jit(solution)/shard_map/all_to_all | solution.py:466
  13.3 23.0 %collective-permute-start = (f32[2,8,1024]{2,1,0:T(8,128)S(1)}, f32[2,8,1024]{2,1,0:T(8,128)S(1)}, u32[]{:S(2)}, u32[]{:S(2)}) collective-permute-start(f32[2,8,1024]{2,1,0:T(8,128)S(1)} %convert_bitcast_fusion), channel_id=1, source_target_pairs={{320,0},{336,16},{192,1},{208,17},{352,2},{368,18},{64,3},{80,19},... | collective-permute-start | bytes 196616 | tf_op jit(solution)/shard_map/ppermute | solution.py:482
  26.9 9.3 %copy-start.25 = (bf16[32,256]{1,0:T(8,128)(2,1)S(1)}, bf16[32,256]{1,0:T(8,128)(2,1)}, u32[]{:S(2)}) copy-start(bf16[32,256]{1,0:T(8,128)(2,1)} %constant.51.clone.own_t_ref) | copy-start | bytes 49156
  26.9 9.3 %copy-start.26 = (bf16[32,32]{1,0:T(8,128)(2,1)S(1)}, bf16[32,32]{1,0:T(8,128)(2,1)}, u32[]{:S(2)}) copy-start(bf16[32,32]{1,0:T(8,128)(2,1)} %mix_ref.3) | copy-start | bytes 6148
  27.8 8.5 %copy-start.9 = (bf16[256,32]{1,0:T(8,128)(2,1)S(1)}, bf16[256,32]{1,0:T(8,128)(2,1)}, u32[]{:S(2)}) copy-start(bf16[256,32]{1,0:T(8,128)(2,1)} %constant.50.clone.own_ref) | copy-start | bytes 49156
  27.8 19.9 %all-to-all-start.1 = ((f32[16,4,128]{2,1,0:T(4,128)}), f32[16,4,128]{2,1,0:T(4,128)S(1)}, u32[]{:S(2)}, u32[]{:S(2)}) async-start(f32[16,4,128]{2,1,0:T(4,128)} %shard_map.309), calls=%async_computation.1 | async-start | bytes 65536 | tf_op jit(solution)/shard_map/all_to_all | solution.py:466
  36.2 0.7 copy-start.27
  36.9 10.8 %copy-start.5 = (bf16[256,1024]{1,0:T(8,128)(2,1)S(1)}, bf16[256,1024]{1,0:T(8,128)(2,1)}, u32[]{:S(2)}) copy-start(bf16[256,1024]{1,0:T(8,128)(2,1)} %constant.56.clone.grow_ref) | copy-start | bytes 1572868
  36.9 10.8 %copy-start.6 = (bf16[1024,256]{1,0:T(8,128)(2,1)S(1)}, bf16[1024,256]{1,0:T(8,128)(2,1)}, u32[]{:S(2)}) copy-start(bf16[1024,256]{1,0:T(8,128)(2,1)} %constant.57.clone.sum_ref) | copy-start | bytes 1572868
  37.2 10.5 %copy-start.17 = (f32[16,256]{1,0:T(8,128)S(1)}, f32[16,256]{1,0:T(8,128)}, u32[]{:S(2)}) copy-start(f32[16,256]{1,0:T(8,128)} %constant.54.clone.cos_ref) | copy-start | bytes 49156
  37.2 10.5 %copy-start.18 = (f32[16,256]{1,0:T(8,128)S(1)}, f32[16,256]{1,0:T(8,128)}, u32[]{:S(2)}) copy-start(f32[16,256]{1,0:T(8,128)} %constant.55.clone.sin_ref) | copy-start | bytes 49156
  37.2 10.5 %copy-start.23 = (bf16[64,192]{1,0:T(8,128)(2,1)S(1)}, bf16[64,192]{1,0:T(8,128)(2,1)}, u32[]{:S(2)}) copy-start(bf16[64,192]{1,0:T(8,128)(2,1)} %constant.52.clone.down_ref) | copy-start | bytes 73732
  37.3 10.5 %copy-start.24 = (bf16[64,192]{1,0:T(8,128)(2,1)S(1)}, bf16[64,192]{1,0:T(8,128)(2,1)}, u32[]{:S(2)}) copy-start(bf16[64,192]{1,0:T(8,128)(2,1)} %constant.53.clone.up_ref) | copy-start | bytes 73732
  37.3 3.4 %collective-permute-start.1 = (f32[2,8,1024]{2,1,0:T(8,128)S(1)}, f32[2,8,1024]{2,1,0:T(8,128)S(1)}, u32[]{:S(2)}, u32[]{:S(2)}) collective-permute-start(f32[2,8,1024]{2,1,0:T(8,128)S(1)} %get-tuple-element.20.mine_ref), channel_id=1, source_target_pairs={{0,16},{16,0},{32,48},{48,32},{64,80},{80,64},{96,112},{112,96},{1... | collective-permute-start | bytes 196616 | tf_op jit(solution)/shard_map/ppermute | solution.py:484
  47.8 16.8 %copy-start.15 = (bf16[256,192]{1,0:T(8,128)(2,1)S(1)}, bf16[256,192]{1,0:T(8,128)(2,1)}, u32[]{:S(2)}) copy-start(bf16[256,192]{1,0:T(8,128)(2,1)} %constant.58.clone.r_1_) | copy-start | bytes 294916
  47.8 16.8 %copy-start.16 = (bf16[256,192]{1,0:T(8,128)(2,1)S(1)}, bf16[256,192]{1,0:T(8,128)(2,1)}, u32[]{:S(2)}) copy-start(bf16[256,192]{1,0:T(8,128)(2,1)} %constant.59.clone.r_2_) | copy-start | bytes 294916
  47.8 31.2 %copy-start.7 = (bf16[2,4,32,8,128]{4,3,2,1,0:T(8,128)(2,1)S(1)}, bf16[2,4,32,8,128]{4,3,2,1,0:T(8,128)(2,1)}, u32[]{:S(2)}) copy-start(bf16[2,4,32,8,128]{4,3,2,1,0:T(8,128)(2,1)} %param.30) | copy-start | bytes 1572868
  47.8 31.2 %copy-start.14 = (bf16[256,256]{1,0:T(8,128)(2,1)S(1)}, bf16[256,256]{1,0:T(8,128)(2,1)}, u32[]{:S(2)}) copy-start(bf16[256,256]{1,0:T(8,128)(2,1)} %constant.61.clone.block_ref) | copy-start | bytes 393220
  64.6 14.4 %copy-start = (bf16[2,4,32,8,128]{4,3,2,1,0:T(8,128)(2,1)S(1)}, bf16[2,4,32,8,128]{4,3,2,1,0:T(8,128)(2,1)}, u32[]{:S(2)}) copy-start(bf16[2,4,32,8,128]{4,3,2,1,0:T(8,128)(2,1)} %param.29) | copy-start | bytes 1572868
  64.9 14.1 %copy-start.1 = (bf16[384,512]{1,0:T(8,128)(2,1)S(1)}, bf16[384,512]{1,0:T(8,128)(2,1)}, u32[]{:S(2)}) copy-start(bf16[384,512]{1,0:T(8,128)(2,1)} %constant.60.clone.up_ref) | copy-start | bytes 1179652
  64.9 14.1 %copy-start.4 = (bf16[128,512]{1,0:T(8,128)(2,1)S(1)}, bf16[128,512]{1,0:T(8,128)(2,1)}, u32[]{:S(2)}) copy-start(bf16[128,512]{1,0:T(8,128)(2,1)} %constant.48.clone.table_ref.down_ref) | copy-start | bytes 393220
  79.0 14.1 %copy-start.8 = (bf16[128,1536]{1,0:T(8,128)(2,1)S(1)}, bf16[128,1536]{1,0:T(8,128)(2,1)}, u32[]{:S(2)}) copy-start(bf16[128,1536]{1,0:T(8,128)(2,1)} %constant.62.clone.r_1_) | copy-start | bytes 1179652
  79.0 28.8 %copy-start.22 = (bf16[64,384]{1,0:T(8,128)(2,1)S(1)}, bf16[64,384]{1,0:T(8,128)(2,1)}, u32[]{:S(2)}) copy-start(bf16[64,384]{1,0:T(8,128)(2,1)} %constant.63.clone.down_ref) | copy-start | bytes 147460
  80.5 27.3 %copy-start.3 = (bf16[1024,256]{1,0:T(8,128)(2,1)S(1)}, bf16[1024,256]{1,0:T(8,128)(2,1)}, u32[]{:S(2)}) copy-start(bf16[1024,256]{1,0:T(8,128)(2,1)} %constant.66.clone.sum_ref) | copy-start | bytes 1572868
  93.1 14.7 %copy-start.2 = (bf16[256,1024]{1,0:T(8,128)(2,1)S(1)}, bf16[256,1024]{1,0:T(8,128)(2,1)}, u32[]{:S(2)}) copy-start(bf16[256,1024]{1,0:T(8,128)(2,1)} %constant.65.clone.grow_ref) | copy-start | bytes 1572868
  93.1 14.7 %copy-start.10 = (bf16[512,256]{1,0:T(8,128)(2,1)S(1)}, bf16[512,256]{1,0:T(8,128)(2,1)}, u32[]{:S(2)}) copy-start(bf16[512,256]{1,0:T(8,128)(2,1)} %constant.67.clone.pack_ref) | copy-start | bytes 786436
  93.5 14.3 %copy-start.19 = (bf16[128,192]{1,0:T(8,128)(2,1)S(1)}, bf16[128,192]{1,0:T(8,128)(2,1)}, u32[]{:S(2)}) copy-start(bf16[128,192]{1,0:T(8,128)(2,1)} %constant.64.clone.up_ref) | copy-start | bytes 147460
  107.8 16.9 %copy-start.11 = (bf16[256,384]{1,0:T(8,128)(2,1)S(1)}, bf16[256,384]{1,0:T(8,128)(2,1)}, u32[]{:S(2)}) copy-start(bf16[256,384]{1,0:T(8,128)(2,1)} %constant.68.clone.r_1_) | copy-start | bytes 589828
  107.8 16.9 %copy-start.12 = (bf16[256,384]{1,0:T(8,128)(2,1)S(1)}, bf16[256,384]{1,0:T(8,128)(2,1)}, u32[]{:S(2)}) copy-start(bf16[256,384]{1,0:T(8,128)(2,1)} %constant.69.clone.r_2_) | copy-start | bytes 589828
  109.2 15.5 %all-to-all-start.6 = ((f32[16,8,128]{2,1,0:T(8,128)}), f32[16,8,128]{2,1,0:T(8,128)S(1)}, u32[]{:S(2)}, u32[]{:S(2)}) async-start(f32[16,8,128]{2,1,0:T(8,128)} %get-tuple-element.28), calls=%async_computation.6 | async-start | bytes 131072 | tf_op jit(solution)/shard_map/all_to_all | solution.py:466
  113.1 19.2 %collective-permute-start.2 = (f32[2,16,128]{2,1,0:T(8,128)S(1)}, f32[2,16,128]{2,1,0:T(8,128)S(1)}, u32[]{:S(2)}, u32[]{:S(2)}) collective-permute-start(f32[2,16,128]{2,1,0:T(8,128)S(1)} %get-tuple-element.26), channel_id=1, source_target_pairs={{0,320},{16,336},{1,192},{17,208},{2,352},{18,368},{3,64},{19,80},... | collective-permute-start | bytes 49160 | tf_op jit(solution)/shard_map/ppermute | solution.py:483
  125.7 15.5 %all-to-all-start.7 = ((f32[32,8,256]{2,1,0:T(8,128)}), f32[32,8,256]{2,1,0:T(8,128)S(1)}, u32[]{:S(2)}, u32[]{:S(2)}) async-start(f32[32,8,256]{2,1,0:T(8,128)} %bitcast.12), calls=%async_computation.7 | async-start | bytes 524288 | tf_op jit(solution)/shard_map/all_to_all | solution.py:466
  132.3 3.4 %collective-permute-start.3 = (f32[16,128]{1,0:T(8,128)S(1)}, f32[16,128]{1,0:T(8,128)S(1)}, u32[]{:S(2)}, u32[]{:S(2)}) collective-permute-start(f32[16,128]{1,0:T(8,128)S(1)} %get-tuple-element.32), channel_id=1, source_target_pairs={{0,16},{16,0},{32,48},{48,32},{64,80},{80,64},{96,112},{112,96},{1... | collective-permute-start | bytes 24584 | tf_op jit(solution)/shard_map/ppermute | solution.py:484
  135.4 0.8 copy-start.20
  135.4 0.9 copy-start.21

commit v8 on v7

--- a/solution.py
+++ b/solution.py
@@ -228,7 +228,7 @@
 
 
 def bias_column(bias_ref):
-    bias = jnp.broadcast_to(bias_ref[0:1], (CY, C))
+    bias = jnp.broadcast_to(bias_ref[...], (CY, C))
     picked = jnp.where(lane_ids((CY, C)) == row_ids((CY, C)) // ROWS, bias, 0.0)
     return jnp.sum(picked, 1, keepdims=True)
 
@@ -365,7 +365,7 @@
 
 def gelu_kernel(got_ref, field_ref, cot_ref, mix_ref, bias_ref, own_ref, own_t_ref, up_ref, down_ref, block_ref, act_ref, grad_ref, out_ref):
     forth = grow_mix(dot_nt(own_ref[...], mix_ref[...]), own_t_ref[...])
-    bias, up = bias_column(bias_ref), up_ref[...]
+    bias, up = bias_ref[...], up_ref[...]
     moments = jnp.zeros((CY, CY), F32)
     for s in range(S):
         spectral = synth_depth(got_ref, s, up)
@@ -427,7 +427,7 @@
 def land_kernel(moved_ref, bias_in_ref, mix_ref, own_ref, own_t_ref, mine_ref, bias_ref, back_ref):
     back_ref[...] = grow_mix(dot(own_ref[...], mix_ref[...]), own_t_ref[...])
     mine_ref[...] = moved_ref[...]
-    bias_ref[...] = jnp.broadcast_to(bias_in_ref[...], (8, C))
+    bias_ref[...] = jnp.broadcast_to(bias_column(bias_in_ref), (CY, N))
 
 
 def outer_kernel(keep_ref, other_ref, grow_in_ref, grow_out_ref, weight_ref):
@@ -503,7 +503,7 @@
     got = flat(over_space(depth))
     (plane,) = call(lambda *r: plane_kernel(False, *r), [short_shape], got, X_DOWN_4, scratch=held(4))
     mine, bias, back = call(
-        land_kernel, [((2, M // 2, CO), F32), ((8, C), F32), ((CY, CY), BF16)],
+        land_kernel, [((2, M // 2, CO), F32), ((CY, N), F32), ((CY, CY), BF16)],
         mine, bias_term.reshape(1, C), mix_weight, OWN, OWN_T, flops=5000000000)
     (weight,) = call(weight_kernel, [((2, M, CO), F32)], mine, partner(mine))
     got = over_dp(plane)

time: 143 us -> 143 us (level)
  no operation moved by 1% of the time
where the time goes in v8:
time: 143 us
  blocking collectives  57 us (40%)
  starting transfers between devices  51.1 us (36%)
  waiting for transfers between devices  20.3 us (14%)
  Pallas kernels  11.8 us (8%)
    all_to_all x4, blocking collectives, swap(): return lax.all_to_all(value, axis, 0, 0, tiled=True)  57 us
    all_to_all x4, starting transfers between devices, swap(): return lax.all_to_all(value, axis, 0, 0, tiled=True)  29.3 us
    all_to_all x4, waiting for transfers between devices, swap(): return lax.all_to_all(value, axis, 0, 0, tiled=True)  19.4 us
    ppermute x1, starting transfers between devices, on_device(): cross = lambda v: lax.ppermute(v, ('space', 'dp'), crossing)  13.6 us
    pallas_call x15, Pallas kernels, call(): pl.pallas_call(kernel, out_shape=shapes, in_specs=[far if i in far_in els...  11.8 us
    ppermute x2, starting transfers between devices, on_device(): partner = lambda v: lax.ppermute(v, 'space', pairing)  4.81 us
    ppermute x1, starting transfers between devices, on_device(): lax.ppermute(v, ('space', 'dp'), [(b, a) for a, b in crossing])  3.34 us
  transfers between devices with their start and end apart: 8, of which 4 were waited for; matrix products, arithmetic and copies ran while one was open for 0% of the time, Pallas kernels for 3%

profile of v8, /device:TPU:1, one launch (start us, length us, event | category | flops | bytes accessed | tf_op | source)
XLA Modules:
  0.0 142.5 jit_solution(15254663946655335232)
XLA Ops:
  0.6 2.1 %shard_map.308 = f32[16,2,8,256]{3,2,1,0:T(8,128)} custom-call(bf16[8,256,128]{2,1,0:T(8,128)(2,1)} %bitcast.19, bf16[128,512]{1,0:T(8,128)(2,1)} %constant.48.clone.table_ref.down_ref), custom_call_target="tpu_custom_call" | custom-call | flops 50000000 | bytes 917504 | tf_op jit(solution)/shard_map/pallas_call | solution.py:454
  2.7 10.5 %all-to-all-start = ((f32[32,8,256]{2,1,0:T(8,128)}), f32[32,8,256]{2,1,0:T(8,128)S(1)}, u32[]{:S(2)}, u32[]{:S(2)}) async-start(f32[32,8,256]{2,1,0:T(8,128)} %bitcast.29), calls=%async_computation | async-start | bytes 524288 | tf_op jit(solution)/shard_map/all_to_all | solution.py:466
  13.2 0.0 copy-done.28
  13.3 13.6 %collective-permute-start = (f32[2,8,1024]{2,1,0:T(8,128)S(1)}, f32[2,8,1024]{2,1,0:T(8,128)S(1)}, u32[]{:S(2)}, u32[]{:S(2)}) collective-permute-start(f32[2,8,1024]{2,1,0:T(8,128)S(1)} %convert_bitcast_fusion), channel_id=1, source_target_pairs={{320,0},{336,16},{192,1},{208,17},{352,2},{368,18},{64,3},{80,19},... | collective-permute-start | bytes 196616 | tf_op jit(solution)/shard_map/ppermute | solution.py:482
  26.9 0.0 all-to-all-done
  26.9 0.0 copy-done.13
  26.9 0.0 copy-start.25
  26.9 0.0 copy-start.26
  27.0 0.8 shard_map.309
  27.8 8.4 %all-to-all-start.1 = ((f32[16,4,128]{2,1,0:T(4,128)}), f32[16,4,128]{2,1,0:T(4,128)S(1)}, u32[]{:S(2)}, u32[]{:S(2)}) async-start(f32[16,4,128]{2,1,0:T(4,128)} %shard_map.309), calls=%async_computation.1 | async-start | bytes 65536 | tf_op jit(solution)/shard_map/all_to_all | solution.py:466
  36.2 0.0 copy-start.27
  36.3 0.0 collective-permute-done.moved_ref
  36.3 0.0 copy-done.25
  36.3 0.0 copy-done.26
  36.3 0.6 copy-done.27
  36.9 0.3 shard_map.310
  37.2 0.0 copy-start.17
  37.2 0.0 copy-start.18
  37.2 0.0 copy-start.23
  37.3 0.0 copy-start.24
  37.3 2.6 %collective-permute-start.1 = (f32[2,8,1024]{2,1,0:T(8,128)S(1)}, f32[2,8,1024]{2,1,0:T(8,128)S(1)}, u32[]{:S(2)}, u32[]{:S(2)}) collective-permute-start(f32[2,8,1024]{2,1,0:T(8,128)S(1)} %get-tuple-element.20.mine_ref), channel_id=1, source_target_pairs={{0,16},{16,0},{32,48},{48,32},{64,80},{80,64},{96,112},{112,96},{1... | collective-permute-start | bytes 196616 | tf_op jit(solution)/shard_map/ppermute | solution.py:484
  39.8 0.9 collective-permute-done.1.other_ref
  40.7 7.0 %all-to-all-done.1.got_ref = f32[16,4,128]{2,1,0:T(4,128)S(1)} async-done(((f32[16,4,128]{2,1,0:T(4,128)}), f32[16,4,128]{2,1,0:T(4,128)S(1)}, u32[]{:S(2)}, u32[]{:S(2)}) %all-to-all-start.1) | async-done | bytes 32800 | tf_op jit(solution)/shard_map/all_to_all | solution.py:466
  47.7 0.0 copy-done.5
  47.8 0.0 copy-start.15
  47.8 0.0 copy-start.16
  47.8 0.0 copy-start.7
  47.8 0.0 copy-start.14
  47.8 0.7 shard_map.312
  48.5 16.0 %all_to_all.40.r_0_ = f32[16,4,128]{2,1,0:T(4,128)S(1)} all-to-all(f32[16,4,128]{2,1,0:T(4,128)S(1)} %get-tuple-element.21), channel_id=1, replica_groups=mesh['space'=32,'dp'=16] {'dp'}, dimensions={0} | all-to-all | bytes 65536 | tf_op jit(solution)/shard_map/all_to_all | solution.py:466
  64.6 0.0 copy-done.15
  64.6 0.3 shard_map.313
  64.9 0.0 copy-start.1
  64.9 0.0 copy-start.4
  64.9 14.1 %all_to_all.41 = f32[32,8,256]{2,1,0:T(8,128)S(1)} all-to-all(f32[32,8,256]{2,1,0:T(8,128)S(1)} %bitcast.23), channel_id=1, replica_groups=mesh['space'=32,'dp'=16] {'space'}, dimensions={0} | all-to-all | bytes 524288 | tf_op jit(solution)/shard_map/all_to_all | solution.py:466
  79.0 0.0 copy-done.14
  79.0 0.0 copy-start.8
  79.0 0.0 copy-start.22
  79.0 1.5 %shard_map.314 = (bf16[8,256,128]{2,1,0:T(8,128)(2,1)S(1)}, bf16[8,256,128]{2,1,0:T(8,128)(2,1)S(1)}, f32[16,2,8,256]{3,2,1,0:T(8,128)S(1)}) custom-call(f32[16,2,8,256]{3,2,1,0:T(8,128)S(1)} %bitcast.22, bf16[8,256,128]{2,1,0:T(8,128)(2,1)S(1)} %bitcast.20, bf16[8,256,128]{2,1,0:T(8,128)(2,1)S(1)} %bitcast.26, bf16[32,32]{1,0:T(8,128)(2,1)S(1)} %copy-done.26, ...), custom_call_target="tpu_custom_call" | custom-call | flops 50000000 | bytes 3442688 | tf_op jit(solution)/shard_map/pallas_call | solution.py:454
  80.5 0.0 copy-start.3
  80.6 12.6 %all_to_all.42 = f32[32,8,256]{2,1,0:T(8,128)S(1)} all-to-all(f32[32,8,256]{2,1,0:T(8,128)S(1)} %bitcast.27), channel_id=1, replica_groups=mesh['space'=32,'dp'=16] {'space'}, dimensions={0} | all-to-all | bytes 524288 | tf_op jit(solution)/shard_map/all_to_all | solution.py:466
  93.2 0.0 copy-done.8
  93.2 0.3 shard_map.315
  93.5 0.0 copy-start.19
  93.5 14.3 %all_to_all.43.got_ref = f32[16,8,128]{2,1,0:T(8,128)S(1)} all-to-all(f32[16,8,128]{2,1,0:T(8,128)S(1)} %shard_map.315), channel_id=1, replica_groups=mesh['space'=32,'dp'=16] {'dp'}, dimensions={0} | all-to-all | bytes 131072 | tf_op jit(solution)/shard_map/all_to_all | solution.py:466
  107.8 0.0 copy-done.3
  107.8 0.0 copy-start.11
  107.8 0.0 copy-start.12
  107.9 1.4 shard_map.316
  109.2 3.9 %all-to-all-start.6 = ((f32[16,8,128]{2,1,0:T(8,128)}), f32[16,8,128]{2,1,0:T(8,128)S(1)}, u32[]{:S(2)}, u32[]{:S(2)}) async-start(f32[16,8,128]{2,1,0:T(8,128)} %get-tuple-element.28), calls=%async_computation.6 | async-start | bytes 131072 | tf_op jit(solution)/shard_map/all_to_all | solution.py:466
  113.1 3.3 %collective-permute-start.2 = (f32[2,16,128]{2,1,0:T(8,128)S(1)}, f32[2,16,128]{2,1,0:T(8,128)S(1)}, u32[]{:S(2)}, u32[]{:S(2)}) collective-permute-start(f32[2,16,128]{2,1,0:T(8,128)S(1)} %get-tuple-element.26), channel_id=1, source_target_pairs={{0,320},{16,336},{1,192},{17,208},{2,352},{18,368},{3,64},{19,80},... | collective-permute-start | bytes 49160 | tf_op jit(solution)/shard_map/ppermute | solution.py:483
  116.4 8.3 %all-to-all-done.6.r_0_ = f32[16,8,128]{2,1,0:T(8,128)S(1)} async-done(((f32[16,8,128]{2,1,0:T(8,128)}), f32[16,8,128]{2,1,0:T(8,128)S(1)}, u32[]{:S(2)}, u32[]{:S(2)}) %all-to-all-start.6) | async-done | bytes 65568 | tf_op jit(solution)/shard_map/all_to_all | solution.py:466
  124.7 1.0 shard_map.319
  125.8 6.5 %all-to-all-start.7 = ((f32[32,8,256]{2,1,0:T(8,128)}), f32[32,8,256]{2,1,0:T(8,128)S(1)}, u32[]{:S(2)}, u32[]{:S(2)}) async-start(f32[32,8,256]{2,1,0:T(8,128)} %bitcast.12), calls=%async_computation.7 | async-start | bytes 524288 | tf_op jit(solution)/shard_map/all_to_all | solution.py:466
  132.2 0.0 collective-permute-done.2.moved_ref
  132.3 2.3 %collective-permute-start.3 = (f32[16,128]{1,0:T(8,128)S(1)}, f32[16,128]{1,0:T(8,128)S(1)}, u32[]{:S(2)}, u32[]{:S(2)}) collective-permute-start(f32[16,128]{1,0:T(8,128)S(1)} %get-tuple-element.32), channel_id=1, source_target_pairs={{0,16},{16,0},{32,48},{48,32},{64,80},{80,64},{96,112},{112,96},{1... | collective-permute-start | bytes 24584 | tf_op jit(solution)/shard_map/ppermute | solution.py:484
  134.5 0.8 shard_map.318
  135.4 0.3 shard_map.320.linear_ref
  135.7 0.0 collective-permute-done.3.other_ref
  135.7 0.5 copy-done.20
  136.2 0.0 copy-done.21
  136.2 0.9 shard_map.322
  137.2 4.1 %all-to-all-done.7 = f32[32,8,256]{2,1,0:T(8,128)S(1)} async-done(((f32[32,8,256]{2,1,0:T(8,128)}), f32[32,8,256]{2,1,0:T(8,128)S(1)}, u32[]{:S(2)}, u32[]{:S(2)}) %all-to-all-start.7) | async-done | bytes 262176 | tf_op jit(solution)/shard_map/all_to_all | solution.py:466
  141.3 1.3 shard_map.321
  (30 shorter events, 0.1 us)
Async XLA Ops:
  2.7 10.5 %copy-start.28 = (bf16[8,2,1,1024]{3,1,2,0:T(2,128)(2,1)S(1)}, bf16[8,2,1,1024]{3,1,2,0:T(2,128)(2,1)}, u32[]{:S(2)}) copy-start(bf16[8,2,1,1024]{3,1,2,0:T(2,128)(2,1)} %param.31) | copy-start | bytes 98308
  2.7 24.2 %copy-start.13 = (bf16[64,1536]{1,0:T(8,128)(2,1)S(1)}, bf16[64,1536]{1,0:T(8,128)(2,1)}, u32[]{:S(2)}) copy-start(bf16[64,1536]{1,0:T(8,128)(2,1)} %constant.49.clone.r_1_) | copy-start | bytes 589828
  2.7 24.2 %all-to-all-start = ((f32[32,8,256]{2,1,0:T(8,128)}), f32[32,8,256]{2,1,0:T(8,128)S(1)}, u32[]{:S(2)}, u32[]{:S(2)}) async-start(f32[32,8,256]{2,1,0:T(8,128)} %bitcast.29), calls=%async_computation | async-start | bytes 524288 | tf_op jit(solution)/shard_map/all_to_all | solution.py:466
  13.3 23.0 %collective-permute-start = (f32[2,8,1024]{2,1,0:T(8,128)S(1)}, f32[2,8,1024]{2,1,0:T(8,128)S(1)}, u32[]{:S(2)}, u32[]{:S(2)}) collective-permute-start(f32[2,8,1024]{2,1,0:T(8,128)S(1)} %convert_bitcast_fusion), channel_id=1, source_target_pairs={{320,0},{336,16},{192,1},{208,17},{352,2},{368,18},{64,3},{80,19},... | collective-permute-start | bytes 196616 | tf_op jit(solution)/shard_map/ppermute | solution.py:482
  26.9 9.3 %copy-start.25 = (bf16[32,256]{1,0:T(8,128)(2,1)S(1)}, bf16[32,256]{1,0:T(8,128)(2,1)}, u32[]{:S(2)}) copy-start(bf16[32,256]{1,0:T(8,128)(2,1)} %constant.51.clone.own_t_ref) | copy-start | bytes 49156
  26.9 9.3 %copy-start.26 = (bf16[32,32]{1,0:T(8,128)(2,1)S(1)}, bf16[32,32]{1,0:T(8,128)(2,1)}, u32[]{:S(2)}) copy-start(bf16[32,32]{1,0:T(8,128)(2,1)} %mix_ref.3) | copy-start | bytes 6148
  27.8 8.5 %copy-start.9 = (bf16[256,32]{1,0:T(8,128)(2,1)S(1)}, bf16[256,32]{1,0:T(8,128)(2,1)}, u32[]{:S(2)}) copy-start(bf16[256,32]{1,0:T(8,128)(2,1)} %constant.50.clone.own_ref) | copy-start | bytes 49156
  27.8 19.9 %all-to-all-start.1 = ((f32[16,4,128]{2,1,0:T(4,128)}), f32[16,4,128]{2,1,0:T(4,128)S(1)}, u32[]{:S(2)}, u32[]{:S(2)}) async-start(f32[16,4,128]{2,1,0:T(4,128)} %shard_map.309), calls=%async_computation.1 | async-start | bytes 65536 | tf_op jit(solution)/shard_map/all_to_all | solution.py:466
  36.2 0.7 copy-start.27
  36.9 10.8 %copy-start.5 = (bf16[256,1024]{1,0:T(8,128)(2,1)S(1)}, bf16[256,1024]{1,0:T(8,128)(2,1)}, u32[]{:S(2)}) copy-start(bf16[256,1024]{1,0:T(8,128)(2,1)} %constant.56.clone.grow_ref) | copy-start | bytes 1572868
  36.9 10.8 %copy-start.6 = (bf16[1024,256]{1,0:T(8,128)(2,1)S(1)}, bf16[1024,256]{1,0:T(8,128)(2,1)}, u32[]{:S(2)}) copy-start(bf16[1024,256]{1,0:T(8,128)(2,1)} %constant.57.clone.sum_ref) | copy-start | bytes 1572868
  37.2 10.5 %copy-start.17 = (f32[16,256]{1,0:T(8,128)S(1)}, f32[16,256]{1,0:T(8,128)}, u32[]{:S(2)}) copy-start(f32[16,256]{1,0:T(8,128)} %constant.54.clone.cos_ref) | copy-start | bytes 49156
  37.2 10.5 %copy-start.18 = (f32[16,256]{1,0:T(8,128)S(1)}, f32[16,256]{1,0:T(8,128)}, u32[]{:S(2)}) copy-start(f32[16,256]{1,0:T(8,128)} %constant.55.clone.sin_ref) | copy-start | bytes 49156
  37.2 10.5 %copy-start.23 = (bf16[64,192]{1,0:T(8,128)(2,1)S(1)}, bf16[64,192]{1,0:T(8,128)(2,1)}, u32[]{:S(2)}) copy-start(bf16[64,192]{1,0:T(8,128)(2,1)} %constant.52.clone.down_ref) | copy-start | bytes 73732
  37.3 10.5 %copy-start.24 = (bf16[64,192]{1,0:T(8,128)(2,1)S(1)}, bf16[64,192]{1,0:T(8,128)(2,1)}, u32[]{:S(2)}) copy-start(bf16[64,192]{1,0:T(8,128)(2,1)} %constant.53.clone.up_ref) | copy-start | bytes 73732
  37.3 3.4 %collective-permute-start.1 = (f32[2,8,1024]{2,1,0:T(8,128)S(1)}, f32[2,8,1024]{2,1,0:T(8,128)S(1)}, u32[]{:S(2)}, u32[]{:S(2)}) collective-permute-start(f32[2,8,1024]{2,1,0:T(8,128)S(1)} %get-tuple-element.20.mine_ref), channel_id=1, source_target_pairs={{0,16},{16,0},{32,48},{48,32},{64,80},{80,64},{96,112},{112,96},{1... | collective-permute-start | bytes 196616 | tf_op jit(solution)/shard_map/ppermute | solution.py:484
  47.8 16.8 %copy-start.15 = (bf16[256,192]{1,0:T(8,128)(2,1)S(1)}, bf16[256,192]{1,0:T(8,128)(2,1)}, u32[]{:S(2)}) copy-start(bf16[256,192]{1,0:T(8,128)(2,1)} %constant.58.clone.r_1_) | copy-start | bytes 294916
  47.8 16.8 %copy-start.16 = (bf16[256,192]{1,0:T(8,128)(2,1)S(1)}, bf16[256,192]{1,0:T(8,128)(2,1)}, u32[]{:S(2)}) copy-start(bf16[256,192]{1,0:T(8,128)(2,1)} %constant.59.clone.r_2_) | copy-start | bytes 294916
  47.8 31.2 %copy-start.7 = (bf16[2,4,32,8,128]{4,3,2,1,0:T(8,128)(2,1)S(1)}, bf16[2,4,32,8,128]{4,3,2,1,0:T(8,128)(2,1)}, u32[]{:S(2)}) copy-start(bf16[2,4,32,8,128]{4,3,2,1,0:T(8,128)(2,1)} %param.30) | copy-start | bytes 1572868
  47.8 31.2 %copy-start.14 = (bf16[256,256]{1,0:T(8,128)(2,1)S(1)}, bf16[256,256]{1,0:T(8,128)(2,1)}, u32[]{:S(2)}) copy-start(bf16[256,256]{1,0:T(8,128)(2,1)} %constant.61.clone.block_ref) | copy-start | bytes 393220
  64.6 14.4 %copy-start = (bf16[2,4,32,8,128]{4,3,2,1,0:T(8,128)(2,1)S(1)}, bf16[2,4,32,8,128]{4,3,2,1,0:T(8,128)(2,1)}, u32[]{:S(2)}) copy-start(bf16[2,4,32,8,128]{4,3,2,1,0:T(8,128)(2,1)} %param.29) | copy-start | bytes 1572868
  64.9 14.1 %copy-start.1 = (bf16[384,512]{1,0:T(8,128)(2,1)S(1)}, bf16[384,512]{1,0:T(8,128)(2,1)}, u32[]{:S(2)}) copy-start(bf16[384,512]{1,0:T(8,128)(2,1)} %constant.60.clone.up_ref) | copy-start | bytes 1179652
  64.9 14.1 %copy-start.4 = (bf16[128,512]{1,0:T(8,128)(2,1)S(1)}, bf16[128,512]{1,0:T(8,128)(2,1)}, u32[]{:S(2)}) copy-start(bf16[128,512]{1,0:T(8,128)(2,1)} %constant.48.clone.table_ref.down_ref) | copy-start | bytes 393220
  79.0 14.1 %copy-start.8 = (bf16[128,1536]{1,0:T(8,128)(2,1)S(1)}, bf16[128,1536]{1,0:T(8,128)(2,1)}, u32[]{:S(2)}) copy-start(bf16[128,1536]{1,0:T(8,128)(2,1)} %constant.62.clone.r_1_) | copy-start | bytes 1179652
  79.0 28.8 %copy-start.22 = (bf16[64,384]{1,0:T(8,128)(2,1)S(1)}, bf16[64,384]{1,0:T(8,128)(2,1)}, u32[]{:S(2)}) copy-start(bf16[64,384]{1,0:T(8,128)(2,1)} %constant.63.clone.down_ref) | copy-start | bytes 147460
  80.5 27.3 %copy-start.3 = (bf16[1024,256]{1,0:T(8,128)(2,1)S(1)}, bf16[1024,256]{1,0:T(8,128)(2,1)}, u32[]{:S(2)}) copy-start(bf16[1024,256]{1,0:T(8,128)(2,1)} %constant.66.clone.sum_ref) | copy-start | bytes 1572868
  93.2 14.7 %copy-start.2 = (bf16[256,1024]{1,0:T(8,128)(2,1)S(1)}, bf16[256,1024]{1,0:T(8,128)(2,1)}, u32[]{:S(2)}) copy-start(bf16[256,1024]{1,0:T(8,128)(2,1)} %constant.65.clone.grow_ref) | copy-start | bytes 1572868
  93.2 14.7 %copy-start.10 = (bf16[512,256]{1,0:T(8,128)(2,1)S(1)}, bf16[512,256]{1,0:T(8,128)(2,1)}, u32[]{:S(2)}) copy-start(bf16[512,256]{1,0:T(8,128)(2,1)} %constant.67.clone.pack_ref) | copy-start | bytes 786436
  93.5 14.3 %copy-start.19 = (bf16[128,192]{1,0:T(8,128)(2,1)S(1)}, bf16[128,192]{1,0:T(8,128)(2,1)}, u32[]{:S(2)}) copy-start(bf16[128,192]{1,0:T(8,128)(2,1)} %constant.64.clone.up_ref) | copy-start | bytes 147460
  107.8 16.9 %copy-start.11 = (bf16[256,384]{1,0:T(8,128)(2,1)S(1)}, bf16[256,384]{1,0:T(8,128)(2,1)}, u32[]{:S(2)}) copy-start(bf16[256,384]{1,0:T(8,128)(2,1)} %constant.68.clone.r_1_) | copy-start | bytes 589828
  107.8 16.9 %copy-start.12 = (bf16[256,384]{1,0:T(8,128)(2,1)S(1)}, bf16[256,384]{1,0:T(8,128)(2,1)}, u32[]{:S(2)}) copy-start(bf16[256,384]{1,0:T(8,128)(2,1)} %constant.69.clone.r_2_) | copy-start | bytes 589828
  109.2 15.5 %all-to-all-start.6 = ((f32[16,8,128]{2,1,0:T(8,128)}), f32[16,8,128]{2,1,0:T(8,128)S(1)}, u32[]{:S(2)}, u32[]{:S(2)}) async-start(f32[16,8,128]{2,1,0:T(8,128)} %get-tuple-element.28), calls=%async_computation.6 | async-start | bytes 131072 | tf_op jit(solution)/shard_map/all_to_all | solution.py:466
  113.1 19.2 %collective-permute-start.2 = (f32[2,16,128]{2,1,0:T(8,128)S(1)}, f32[2,16,128]{2,1,0:T(8,128)S(1)}, u32[]{:S(2)}, u32[]{:S(2)}) collective-permute-start(f32[2,16,128]{2,1,0:T(8,128)S(1)} %get-tuple-element.26), channel_id=1, source_target_pairs={{0,320},{16,336},{1,192},{17,208},{2,352},{18,368},{3,64},{19,80},... | collective-permute-start | bytes 49160 | tf_op jit(solution)/shard_map/ppermute | solution.py:483
  125.8 15.5 %all-to-all-start.7 = ((f32[32,8,256]{2,1,0:T(8,128)}), f32[32,8,256]{2,1,0:T(8,128)S(1)}, u32[]{:S(2)}, u32[]{:S(2)}) async-start(f32[32,8,256]{2,1,0:T(8,128)} %bitcast.12), calls=%async_computation.7 | async-start | bytes 524288 | tf_op jit(solution)/shard_map/all_to_all | solution.py:466
  132.3 3.4 %collective-permute-start.3 = (f32[16,128]{1,0:T(8,128)S(1)}, f32[16,128]{1,0:T(8,128)S(1)}, u32[]{:S(2)}, u32[]{:S(2)}) collective-permute-start(f32[16,128]{1,0:T(8,128)S(1)} %get-tuple-element.32), channel_id=1, source_target_pairs={{0,16},{16,0},{32,48},{48,32},{64,80},{80,64},{96,112},{112,96},{1... | collective-permute-start | bytes 24584 | tf_op jit(solution)/shard_map/ppermute | solution.py:484
  135.4 0.8 copy-start.20
  135.4 0.9 copy-start.21
